TPU v7x, 128 devices: a whole 4x4x4 slice. The times are simulated.
128 devices in a mesh: row: 8 (over y_hi, z), col: 16 (over x, y_lo, core).
Axes of the slice: x: 4, y: 4 (y_hi: 2, y_lo: 2; y = y_hi * 2 + y_lo), z: 4, core: 2. Of those that a mesh axis runs over, the one named last changes fastest.
Arguments:
- tiles: bfloat16 [8, 16, 512, 128, 128], P('row', 'col'), may hold values from -0.125 to 0.125
- tile_coords: int32 [8, 16, 512, 2], P('row', 'col'), may hold values from 0 to 255, as said below
- tile_counts: int32 [8, 16], P('row', 'col'), may hold values from 128 to 512, as said below
- omega: bfloat16 [64, 262144], P(None, 'col'), may hold values from -6 to 6
Outputs:
- sketch: float32 [64, 262144], P(None, 'col')
Inputs may be any that keep to these rules, and one draw needn't show every extreme that they name: `tile_coords`: within one device the 512 slots name distinct blocks; block rows lie in 0 to 255 and block columns in 0 to 127. `tile_counts`: each count is 512, 256 or 128.
All inputs are finite; a program needn't handle non-finite values.
Results may differ from a plain program's by a relative error of at most 0.0021.
Values may be sent and summed in bfloat16 or wider, within the bound.
No kernel may reach another device: no remote copies, remote signals or barrier semaphores. Data moves between devices by JAX's collectives and lax.ppermute only.
A program may use at most 128 MiB of HBM per device.

v0:
```python
import jax
import jax.numpy as jnp
from jax import lax
from jax.sharding import PartitionSpec as P

TILE = 128


def shards(tiles, tile_coords, tile_counts, omega):
    blocks = tiles[0, 0]
    coords = tile_coords[0, 0]
    rows_local = coords[:, 0]
    cols_local = coords[:, 1]
    slots = blocks.shape[0]
    live = (jnp.arange(slots, dtype=jnp.int32) < tile_counts[0, 0]).astype(jnp.float32)
    width = omega.shape[0]
    blk_col = omega.shape[1] // TILE
    blk_row = blk_col * lax.axis_size("col") // lax.axis_size("row")
    omega_blocks = omega.reshape(width, blk_col, TILE).transpose(1, 0, 2)
    picked = jnp.take(omega_blocks, cols_local, axis=0)
    forward = jnp.einsum("kcb,krb->kcr", picked, blocks, preferred_element_type=jnp.float32)
    forward = forward * live[:, None, None]
    partial_value = jax.ops.segment_sum(forward, rows_local, num_segments=blk_row)
    partial_value = partial_value.transpose(1, 0, 2).reshape(width, blk_row * TILE)
    share = lax.psum_scatter(partial_value, "col", scatter_dimension=1, tiled=True).astype(
        jnp.bfloat16
    )
    inner = lax.all_gather(share, "col", axis=1, tiled=True)
    inner_blocks = inner.reshape(width, blk_row, TILE).transpose(1, 0, 2)
    gathered = jnp.take(inner_blocks, rows_local, axis=0)
    backward = jnp.einsum("kcr,krb->kcb", gathered, blocks, preferred_element_type=jnp.float32)
    backward = backward * live[:, None, None]
    column_part = jax.ops.segment_sum(backward, cols_local, num_segments=blk_col)
    column_part = column_part.transpose(1, 0, 2).reshape(width, blk_col * TILE)
    sketch = lax.psum(column_part, "row")
    return sketch


def solution(mesh):
    return jax.shard_map(
        shards,
        mesh=mesh,
        in_specs=(
            P("row", "col", None, None, None),
            P("row", "col", None, None),
            P("row", "col"),
            P(None, "col"),
        ),
        out_specs=P(None, "col"),
        check_vma=False,
    )
```

profile of v0, /device:TPU:0, one launch (start us, length us, event | category | flops | bytes accessed | tf_op | source)
XLA Modules:
  0.0 529.0 jit_solution(13615469914831827839)
XLA Ops:
  6.5 0.0 copy-start
  6.5 0.0 reduce-scatter.2.cloned.1.call-start
  6.5 0.9 and_reduce_fusion.1
  7.4 0.8 fusion.19
  8.2 0.0 copy-done
  8.2 1.9 bitcast_bitcast_fusion.1
  10.8 21.2 %gather_fusion = bf16[512,64,128]{2,1,0:T(8,128)(2,1)} fusion(bf16[128,64,128]{2,1,0:T(8,128)(2,1)} %bitcast_bitcast_fusion.1, s32[1024]{0:T(1024)S(1)} %pad_clamp_fusion.1), kind=kCustom, calls=%fused_computation | custom fusion | bytes 16779264 | tf_op jit(solution)/shard_map/jit(_take)/gather | solution.py:20
  32.0 20.2 %fusion.4 = f32[512,64,128]{2,1,0:T(8,128)} fusion(bf16[1,1,512,128,128]{4,3,2,1,0:T(8,128)(2,1)} %param.4, f32[512]{0:T(512)S(1)} %fusion.16, bf16[512,64,128]{2,1,0:T(8,128)(2,1)} %gather_fusion, pred[512]{0:T(512)(128)(4,1)S(1)} %get-tuple-element.9), kind=kOutput, calls=%fused_computation.8 | convolution fusion | flops 1082130432 | bytes 41945600 | tf_op jit(solution)/shard_map/kcb,krb->kcr/dot_general | solution.py:21
  52.3 4.3 broadcast_in_dim.28
  56.5 78.4 %scatter_fusion = f32[256,64,128]{2,1,0:T(8,128)} fusion(f32[256,64,128]{2,1,0:T(8,128)} %broadcast_in_dim.28, s32[512]{0:T(512)S(1)} %bitcast.45, f32[512,64,128]{2,1,0:T(8,128)} %fusion.4), kind=kCustom, calls=%fused_computation.2 | custom fusion | flops 4194304 | bytes 50333696 | tf_op jit(solution)/shard_map/scatter-add | solution.py:23
  134.9 7.1 %copy_bitcast_fusion = f32[64,32768]{1,0:T(8,128)} fusion(f32[256,64,128]{2,1,0:T(8,128)} %scatter_fusion), kind=kLoop, calls=%fused_computation.10 | loop fusion | bytes 16777216 | tf_op jit(solution)/shard_map/reshape | solution.py:24
  142.0 0.0 reduce-scatter.2.cloned.1.call-update
  142.1 0.0 all-gather.2.cloned.1.call-start
  142.1 97.8 %reduce-scatter.2.cloned.1.call-done = f32[64,2048]{1,0:T(8,128)} async-done(((f32[64,32768]{1,0:T(8,128)}), f32[64,2048]{1,0:T(8,128)}) %reduce-scatter.2.cloned.1.call-update) | async-done | bytes 524304 | tf_op jit(solution)/shard_map/reduce_scatter | solution.py:25
  239.9 1.8 convert_element_type.11
  241.7 0.0 all-gather.2.cloned.1.call-update
  241.7 0.2 all-reduce.2.cloned.1.call-start
  242.0 39.5 %all-gather.2.cloned.1.call-done = bf16[64,32768]{1,0:T(8,128)(2,1)} async-done(((bf16[64,2048]{1,0:T(8,128)(2,1)}), bf16[64,32768]{1,0:T(8,128)(2,1)}) %all-gather.2.cloned.1.call-update) | async-done | bytes 4194320 | tf_op jit(solution)/shard_map/all_gather | solution.py:28
  281.4 5.4 %bitcast_bitcast_fusion = bf16[256,64,128]{2,1,0:T(8,128)(2,1)} fusion(bf16[64,32768]{1,0:T(8,128)(2,1)} %all-gather.2.cloned.1.call-done), kind=kLoop, calls=%fused_computation.16 | loop fusion | bytes 8388608 | tf_op jit(solution)/shard_map/transpose | solution.py:29
  286.8 21.8 %gather_fusion.1 = bf16[512,64,128]{2,1,0:T(8,128)(2,1)} fusion(bf16[256,64,128]{2,1,0:T(8,128)(2,1)} %bitcast_bitcast_fusion, s32[1024]{0:T(1024)S(1)} %pad_clamp_fusion), kind=kCustom, calls=%fused_computation.1 | custom fusion | bytes 16779264 | tf_op jit(solution)/shard_map/jit(_take)/gather | solution.py:30
  308.7 14.5 %fusion.7 = f32[512,64,128]{2,1,0:T(8,128)} fusion(bf16[1,1,512,128,128]{4,3,2,1,0:T(8,128)(2,1)} %param.4, bf16[512,64,128]{2,1,0:T(8,128)(2,1)} %gather_fusion.1, f32[512]{0:T(512)S(1)} %fusion.16, pred[512]{0:T(512)(128)(4,1)S(1)} %get-tuple-element.5), kind=kOutput, calls=%fused_computation.9 | convolution fusion | flops 1082130432 | bytes 41945600 | tf_op jit(solution)/shard_map/kcr,krb->kcb/dot_general | solution.py:31
  323.2 2.5 broadcast_in_dim.26
  325.7 77.5 %scatter_fusion.1 = f32[128,64,128]{2,1,0:T(8,128)} fusion(f32[128,64,128]{2,1,0:T(8,128)} %broadcast_in_dim.26, s32[512]{0:T(512)S(1)} %bitcast.44, f32[512,64,128]{2,1,0:T(8,128)} %fusion.7), kind=kCustom, calls=%fused_computation.3 | custom fusion | flops 4194304 | bytes 50333696 | tf_op jit(solution)/shard_map/scatter-add | solution.py:33
  403.2 0.0 copy-start.1
  403.2 4.6 copy_bitcast_fusion.1
  407.8 0.0 all-reduce.2.cloned.1.call-update
  407.8 110.1 %all-reduce.2.cloned.1.call-done = f32[64,16384]{1,0:T(8,128)} async-done(((f32[64,16384]{1,0:T(8,128)}), f32[64,16384]{1,0:T(8,128)}) %all-reduce.2.cloned.1.call-update) | async-done | bytes 4194320 | tf_op jit(solution)/shard_map/psum | solution.py:35
  517.9 4.5 copy.21
  522.4 0.0 copy-done.1
  (3 shorter events, 0.0 us)
Async XLA Ops:
  6.5 1.7 copy-start
  6.5 233.4 %reduce-scatter.2.cloned.1.call-start = ((), (), s32[]{:S(2)}) async-start(), calls=%async_computation.1 | async-start | bytes 8912896 | tf_op jit(solution)/shard_map/reduce_scatter | solution.py:25
  142.1 139.3 %all-gather.2.cloned.1.call-start = ((), (), s32[]{:S(2)}) async-start(), calls=%async_computation.2 | async-start | bytes 4456448 | tf_op jit(solution)/shard_map/all_gather | solution.py:28
  241.7 276.2 %all-reduce.2.cloned.1.call-start = ((), (), s32[]{:S(2)}) async-start(), calls=%async_computation.3 | async-start | bytes 8388608 | tf_op jit(solution)/shard_map/psum | solution.py:35
  403.2 119.2 %copy-start.1 = (bf16[64,16384]{1,0:T(8,128)(2,1)S(1)}, bf16[64,16384]{1,0:T(8,128)(2,1)}, u32[]{:S(2)}) copy-start(bf16[64,16384]{1,0:T(8,128)(2,1)} %param.7) | copy-start | bytes 6291460
Sparse Core Ops, SparseCore 0:
  142.2 97.6 reduce-scatter.1
  241.8 39.5 all-gather.1
  407.9 109.9 all-reduce.1
where the time goes:
time: 532 us; the launch traced here: 529 us
  waiting for transfers between devices  247 us (46%)
  other arithmetic  159 us (30%)
  local copies, waits for them, and re-layouts  74.2 us (14%)
  matrix products  34.7 us (7%)
  between operations  13.8 us (3%)
    psum x1, waiting for transfers between devices, shards(): sketch = lax.psum(column_part, 'row')  110 us
    reduce_scatter x1, waiting for transfers between devices, shards(): lax.psum_scatter(partial_value, 'col', scatter_dimension=1, tiled=True)  97.8 us
    scatter-add x1, other arithmetic, shards(): jax.ops.segment_sum(forward, rows_local, num_segments=blk_row)  78.4 us
    scatter-add x1, other arithmetic, shards(): jax.ops.segment_sum(backward, cols_local, num_segments=blk_col)  77.5 us
    all_gather x1, waiting for transfers between devices, shards(): inner = lax.all_gather(share, 'col', axis=1, tiled=True)  39.5 us
    gather x1, local copies, waits for them, and re-layouts, shards(): gathered = jnp.take(inner_blocks, rows_local, axis=0)  21.8 us
    gather x1, local copies, waits for them, and re-layouts, shards(): picked = jnp.take(omega_blocks, cols_local, axis=0)  21.2 us
    dot_general x1, matrix products, shards(): jnp.einsum('kcb,krb->kcr', picked, blocks, preferred_element_type=jnp.flo...  20.2 us
  transfers between devices with their start and end apart: 3, of which 3 were waited for; matrix products, arithmetic and copies ran while one was open for 0% of the time, Pallas kernels for 0%

commit v1 on v0

v1 whole, which is shorter than its diff:
```python
import functools

import jax
import jax.numpy as jnp
from jax import lax
from jax.experimental import pallas as pl
from jax.experimental.pallas import tpu as pltpu
from jax.sharding import Mesh
from jax.sharding import PartitionSpec as P

TILE = 128
CHUNK = 32
UNROLL = 4
LEVEL = 32700.0
STEPS = 8.0
VMEM = 56 * 1024 * 1024
ROW = ("yh", "z")
CHIPS = ("x", "yl")
F32 = jnp.float32
I16 = jnp.int16


def params():
    return pltpu.CompilerParams(vmem_limit_bytes=VMEM)


def code(block):
    top = jnp.maximum(jnp.max(jnp.abs(block), axis=0, keepdims=True), 1e-30)
    step = jnp.ceil(jnp.log2(top) * STEPS)
    return step, jnp.exp2(step * (-1.0 / STEPS)) * LEVEL


def factor(step):
    return jnp.exp2(step * (1.0 / STEPS)) * (1.0 / LEVEL)


def put_block(block, piece, j, out_ref, steps):
    width = block.shape[0]
    step, gain = code(block)
    whole = jnp.round(block * gain).astype(jnp.int32)
    out_ref[piece, pl.ds(pl.multiple_of(j * width, width), width), :] = whole.astype(I16)
    steps[piece, pl.ds(j, 1), :] = step


def live_chunks(count):
    return lax.div(count + (CHUNK - 1), CHUNK)


def sparse_step(transposed, coords, base, source, tiles_ref, acc):
    def body(i, _):
        products = []
        for u in range(UNROLL):
            k = i * UNROLL + u
            slot = base + k
            r, c = coords[2 * slot], coords[2 * slot + 1]
            if transposed:
                left = source[:, pl.ds(pl.multiple_of(c * TILE, TILE), TILE)]
                value = lax.dot_general(left, tiles_ref[k], (((1,), (1,)), ((), ())), preferred_element_type=F32)
                products.append((r, value))
            else:
                value = jnp.dot(source[r], tiles_ref[k], preferred_element_type=F32)
                products.append((c, value))
        for target, value in products:
            acc[target] += value
        return 0

    lax.fori_loop(0, CHUNK // UNROLL, body, 0)


def forward_kernel(coords, info, omega_ref, tiles_ref, keep_ref, give_ref, acc, sem):
    step = pl.program_id(0)
    half = acc.shape[0] // 2

    @pl.when(step == 0)
    def _():
        acc[...] = jnp.zeros_like(acc)

    @pl.when(step < live_chunks(info[0]))
    def _():
        sparse_step(True, coords, step * CHUNK, omega_ref, tiles_ref, acc)

    @pl.when(step == pl.num_programs(0) - 1)
    def _():
        core = info[1]
        one = pltpu.make_async_copy(acc.at[pl.ds(core * half, half)], keep_ref, sem.at[0])
        two = pltpu.make_async_copy(acc.at[pl.ds((1 - core) * half, half)], give_ref, sem.at[1])
        one.start()
        two.start()
        one.wait()
        two.wait()


def forward(tiles, coords, info, omega, blk_row):
    slots = tiles.shape[0]
    width = omega.shape[0]
    half = jax.ShapeDtypeStruct((blk_row // 2, width, TILE), F32)
    last = lambda i, coords, info: (jnp.minimum(i, live_chunks(info[0]) - 1), 0, 0)
    return pl.pallas_call(
        forward_kernel,
        out_shape=(half, half),
        grid_spec=pltpu.PrefetchScalarGridSpec(
            num_scalar_prefetch=2,
            grid=(slots // CHUNK,),
            in_specs=[
                pl.BlockSpec(omega.shape, lambda i, coords, info: (0, 0)),
                pl.BlockSpec((CHUNK, TILE, TILE), last),
            ],
            out_specs=[pl.BlockSpec(memory_space=pl.ANY)] * 2,
            scratch_shapes=[
                pltpu.VMEM((blk_row, width, TILE), F32),
                pltpu.SemaphoreType.DMA((2,)),
            ],
        ),
        compiler_params=params(),
        name="forward",
    )(coords, info, omega, tiles)


def pair_kernel(keep_ref, got_ref, out_ref, steps):
    count = keep_ref.shape[0]
    width = keep_ref.shape[1]

    def body(j, _):
        put_block(keep_ref[j] + got_ref[j], 0, j, out_ref, steps)
        return 0

    lax.fori_loop(0, count, body, 0)
    out_ref[0, count * width :, :] = steps[0].astype(jnp.int32).astype(I16)


def pair(keep, got, pieces):
    blocks, width, _ = keep.shape
    each = blocks // pieces
    rows = each * width + each
    return pl.pallas_call(
        pair_kernel,
        out_shape=jax.ShapeDtypeStruct((pieces, rows, TILE), I16),
        grid=(pieces,),
        in_specs=[pl.BlockSpec((each, width, TILE), lambda i: (i, 0, 0))] * 2,
        out_specs=pl.BlockSpec((1, rows, TILE), lambda i: (i, 0, 0)),
        scratch_shapes=[pltpu.VMEM((1, each, TILE), F32)],
        compiler_params=params(),
        name="pair",
    )(keep, got)


def gather_sum(in_ref, scale, j, width):
    total = None
    for s in range(in_ref.shape[0]):
        part = in_ref[s, pl.ds(pl.multiple_of(j * width, width), width), :].astype(jnp.int32).astype(F32)
        part = part * scale[s, pl.ds(j, 1), :]
        total = part if total is None else total + part
    return total


def scales(in_ref, scale, rows):
    for s in range(in_ref.shape[0]):
        scale[s] = factor(in_ref[s, rows:, :].astype(jnp.int32).astype(F32))


def share_kernel(in_ref, out_ref, scale):
    each, width, _ = out_ref.shape
    scales(in_ref, scale, each * width)

    def body(j, _):
        out_ref[j] = gather_sum(in_ref, scale, j, width).astype(out_ref.dtype)
        return 0

    lax.fori_loop(0, each, body, 0)


def share(parts, width):
    pieces, rows, _ = parts.shape
    each = rows // (width + 1)
    return pl.pallas_call(
        share_kernel,
        out_shape=jax.ShapeDtypeStruct((each, width, TILE), jnp.bfloat16),
        scratch_shapes=[pltpu.VMEM((pieces, each, TILE), F32)],
        compiler_params=params(),
        name="share",
    )(parts)


def backward_kernel(coords, info, mine_ref, theirs_ref, tiles_ref, out_ref, acc, inner, steps, sem):
    step = pl.program_id(0)
    half = inner.shape[0] // 2
    width = acc.shape[1]
    pieces = out_ref.shape[0]
    each = acc.shape[0] // pieces

    @pl.when(step == 0)
    def _():
        core = info[1]
        one = pltpu.make_async_copy(mine_ref, inner.at[pl.ds(core * half, half)], sem.at[0])
        two = pltpu.make_async_copy(theirs_ref, inner.at[pl.ds((1 - core) * half, half)], sem.at[1])
        one.start()
        two.start()
        acc[...] = jnp.zeros_like(acc)
        one.wait()
        two.wait()

    @pl.when(step < live_chunks(info[0]))
    def _():
        sparse_step(False, coords, step * CHUNK, inner, tiles_ref, acc)

    @pl.when(step == pl.num_programs(0) - 1)
    def _():
        def body(b, _):
            put_block(acc[b], lax.div(b, each), lax.rem(b, each), out_ref, steps)
            return 0

        lax.fori_loop(0, acc.shape[0], body, 0)
        for s in range(pieces):
            out_ref[s, each * width :, :] = steps[s].astype(jnp.int32).astype(I16)


def backward(tiles, coords, info, mine, theirs, blk_col, pieces):
    slots = tiles.shape[0]
    half, width, _ = mine.shape
    each = blk_col // pieces
    rows = each * width + each
    last = lambda i, coords, info: (jnp.minimum(i, live_chunks(info[0]) - 1), 0, 0)
    return pl.pallas_call(
        backward_kernel,
        out_shape=jax.ShapeDtypeStruct((pieces, rows, TILE), I16),
        grid_spec=pltpu.PrefetchScalarGridSpec(
            num_scalar_prefetch=2,
            grid=(slots // CHUNK,),
            in_specs=[
                pl.BlockSpec(memory_space=pl.ANY),
                pl.BlockSpec(memory_space=pl.ANY),
                pl.BlockSpec((CHUNK, TILE, TILE), last),
            ],
            out_specs=pl.BlockSpec((pieces, rows, TILE), lambda i, coords, info: (0, 0, 0)),
            scratch_shapes=[
                pltpu.VMEM((blk_col, width, TILE), F32),
                pltpu.VMEM((2 * half, width, TILE), jnp.bfloat16),
                pltpu.VMEM((pieces, each, TILE), F32),
                pltpu.SemaphoreType.DMA((2,)),
            ],
        ),
        compiler_params=params(),
        name="backward",
    )(coords, info, mine, theirs, tiles)


def again_kernel(in_ref, out_ref, scale, steps):
    each = scale.shape[1]
    width = (out_ref.shape[1] - each) // each
    scales(in_ref, scale, each * width)

    def body(j, _):
        put_block(gather_sum(in_ref, scale, j, width), 0, j, out_ref, steps)
        return 0

    lax.fori_loop(0, each, body, 0)
    out_ref[0, each * width :, :] = steps[0].astype(jnp.int32).astype(I16)


def again(parts, width):
    pieces, rows, _ = parts.shape
    each = rows // (width + 1)
    return pl.pallas_call(
        again_kernel,
        out_shape=jax.ShapeDtypeStruct((1, rows, TILE), I16),
        scratch_shapes=[pltpu.VMEM((pieces, each, TILE), F32), pltpu.VMEM((1, each, TILE), F32)],
        compiler_params=params(),
        name="again",
    )(parts)


def spread_kernel(in_ref, out_ref, scale):
    each = scale.shape[1]
    width = out_ref.shape[0]
    scales(in_ref, scale, each * width)
    for j in range(each):
        part = in_ref[0, j * width : (j + 1) * width, :].astype(jnp.int32).astype(F32)
        out_ref[:, j * TILE : (j + 1) * TILE] = part * scale[0, j : j + 1, :]


def spread(parts, width):
    pieces, rows, _ = parts.shape
    each = rows // (width + 1)
    return pl.pallas_call(
        spread_kernel,
        out_shape=jax.ShapeDtypeStruct((width, pieces * each * TILE), F32),
        grid=(pieces,),
        in_specs=[pl.BlockSpec((1, rows, TILE), lambda i: (i, 0, 0))],
        out_specs=pl.BlockSpec((width, each * TILE), lambda i: (0, i)),
        scratch_shapes=[pltpu.VMEM((1, each, TILE), F32)],
        compiler_params=params(),
        name="spread",
    )(parts)


def to_all(value, axes):
    count = lax.axis_size(axes)
    copies = jnp.broadcast_to(value[None], (count,) + value.shape)
    return lax.all_to_all(copies, axes, 0, 0, tiled=True)


def shards(tiles, tile_coords, tile_counts, omega):
    blocks = tiles[0, 0]
    coords = tile_coords[0, 0].reshape(-1)
    core = lax.axis_index("core")
    info = jnp.stack([tile_counts[0, 0], core.astype(jnp.int32)])
    width = omega.shape[0]
    blk_col = omega.shape[1] // TILE
    rows = lax.axis_size(ROW)
    chips = lax.axis_size(CHIPS)
    blk_row = blk_col * 2 * chips // rows
    swap = [(0, 1), (1, 0)]
    keep, give = forward(blocks, coords, info, omega, blk_row)
    got = lax.ppermute(give, "core", swap)
    parts = lax.all_to_all(pair(keep, got, chips), CHIPS, 0, 0, tiled=True)
    mine = to_all(share(parts, width), CHIPS).reshape(blk_row // 2, width, TILE)
    theirs = lax.ppermute(mine, "core", swap)
    out = backward(blocks, coords, info, mine, theirs, blk_col, rows)
    parts = lax.all_to_all(out, ROW, 0, 0, tiled=True)
    parts = to_all(again(parts, width)[0], ROW)
    return spread(parts, width)


def solution(mesh):
    fine = Mesh(mesh.devices.reshape(2, 4, 4, 2, 2), ("yh", "z", "x", "yl", "core"))
    col = ("x", "yl", "core")
    return jax.shard_map(
        shards,
        mesh=fine,
        in_specs=(
            P(ROW, col, None, None, None),
            P(ROW, col, None, None),
            P(ROW, col),
            P(None, col),
        ),
        out_specs=P(None, col),
        check_vma=False,
    )
```

time: 532 us -> 237 us (0.45)
  waiting for transfers between devices: 247 us -> 11.5 us
  other arithmetic: 159 us -> 0.59 us
  blocking collectives: 0 us -> 129 us
  Pallas kernels: 0 us -> 86.3 us
  local copies, waits for them, and re-layouts: 74.2 us -> 7.5 us
  matrix products: 34.7 us -> 0 us
  between operations: 13.8 us -> 0.7 us
    scatter-add x2 -> x0, other arithmetic: 156 us -> none  [the longest x1 78.4 us: shards(): jax.ops.segment_sum(forward, rows_local, num_segments=blk_row)]
    all_to_all x0 -> x4, blocking collectives: none -> 129 us  [the longest x2 60.7 us: to_all(): return lax.all_to_all(copies, axes, 0, 0, tiled=True)]
    psum x1 -> x0, waiting for transfers between devices: 110 us -> none  [shards(): sketch = lax.psum(column_part, 'row')]
    reduce_scatter x1 -> x0, waiting for transfers between devices: 97.8 us -> none  [shards(): lax.psum_scatter(partial_value, 'col', scatter_dimension=1, tiled=True)]
    pallas_call x0 -> x6, Pallas kernels: none -> 86.3 us  [the longest x1 33 us: forward(): pl.pallas_call(forward_kernel, out_shape=(half, half), grid_spec=pltpu.Pr...]
    gather x2 -> x0, local copies, waits for them, and re-layouts: 43.1 us -> none  [the longest x1 21.8 us: shards(): gathered = jnp.take(inner_blocks, rows_local, axis=0)]
    all_gather x1 -> x0, waiting for transfers between devices: 39.5 us -> none  [shards(): inner = lax.all_gather(share, 'col', axis=1, tiled=True)]
    dot_general x2 -> x0, matrix products: 34.7 us -> none  [the longest x1 20.2 us: shards(): jnp.einsum('kcb,krb->kcr', picked, blocks, preferred_element_type=jnp.flo...]
  transfers between devices with their start and end apart: 3 -> 2, of which waited for: 3 -> 2; matrix products, arithmetic and copies ran while one was open for 0% -> 0% of each run, Pallas kernels for 0% -> 0%
where the time goes in v1:
time: 237 us; the launch traced here: 235 us
  blocking collectives  129 us (54%)
  Pallas kernels  86.3 us (36%)
  waiting for transfers between devices  11.5 us (5%)
  local copies, waits for them, and re-layouts  7.5 us (3%)
    all_to_all x2, blocking collectives, to_all(): return lax.all_to_all(copies, axes, 0, 0, tiled=True)  60.7 us
    all_to_all x1, blocking collectives, shards(): parts = lax.all_to_all(out, ROW, 0, 0, tiled=True)  34.6 us
    all_to_all x1, blocking collectives, shards(): parts = lax.all_to_all(pair(keep, got, chips), CHIPS, 0, 0, tiled=True)  33.3 us
    pallas_call x1, Pallas kernels, forward(): pl.pallas_call(forward_kernel, out_shape=(half, half), grid_spec=pltpu.Pr...  33 us
    pallas_call x1, Pallas kernels, backward(): pl.pallas_call(backward_kernel, out_shape=jax.ShapeDtypeStruct((pieces, r...  32 us
    pallas_call x1, Pallas kernels, pair(): pl.pallas_call(pair_kernel, out_shape=jax.ShapeDtypeStruct((pieces, rows,...  8.91 us
    ppermute x1, waiting for transfers between devices, shards(): got = lax.ppermute(give, 'core', swap)  7.36 us
    pallas_call x1, Pallas kernels, spread(): pl.pallas_call(spread_kernel, out_shape=jax.ShapeDtypeStruct((width, piec...  6.06 us
  transfers between devices with their start and end apart: 2, of which 2 were waited for; matrix products, arithmetic and copies ran while one was open for 0% of the time, Pallas kernels for 0%

profile of v1, /device:TPU:0, one launch (start us, length us, event | category | flops | bytes accessed | tf_op | source)
XLA Modules:
  0.0 235.2 jit_solution(8201231188974794239)
XLA Ops:
  0.7 0.8 copy.5
  1.5 0.8 reshape_squeeze.3.coords
  2.2 0.6 pad_add_fusion.info
  2.8 33.0 %forward.1 = (f32[128,64,128]{2,1,0:T(8,128)}, f32[128,64,128]{2,1,0:T(8,128)}) custom-call(s32[1024]{0:T(1024)} %reshape_squeeze.3.coords, s32[2]{0:T(128)} %pad_add_fusion.info, bf16[64,16384]{1,0:T(8,128)(2,1)} %omega_ref.1, bf16[512,128,128]{2,1,0:T(8,128)(2,1)} %bitcast.8), custom_call_target="tpu_custom_call" | custom-call | tf_op jit(solution)/shard_map/forward/pallas_call | solution.py:98
  35.8 0.1 collective-permute-start
  35.9 7.4 %collective-permute-done.got_ref = f32[128,64,128]{2,1,0:T(8,128)S(1)} collective-permute-done((f32[128,64,128]{2,1,0:T(8,128)}, f32[128,64,128]{2,1,0:T(8,128)S(1)}, u32[]{:S(2)}, u32[]{:S(2)}) %collective-permute-start) | collective-permute-done | bytes 4194336 | tf_op jit(solution)/shard_map/ppermute | solution.py:314
  43.3 0.0 copy-start.1
  43.3 1.9 copy-done.1
  45.2 8.9 %pair.1 = s16[8,1040,128]{2,1,0:T(8,128)(2,1)} custom-call(f32[128,64,128]{2,1,0:T(8,128)} %get-tuple-element.7.keep_ref, f32[128,64,128]{2,1,0:T(8,128)} %copy-done.1), custom_call_target="tpu_custom_call" | custom-call | tf_op jit(solution)/shard_map/pair/pallas_call | solution.py:135
  54.1 33.3 %all_to_all.20.in_ref = s16[8,1040,128]{2,1,0:T(8,128)(2,1)} all-to-all(s16[8,1040,128]{2,1,0:T(8,128)(2,1)} %pair.1), channel_id=1, replica_groups=mesh['yh'=2,'z'=4,'x'=4,'yl'=2,'core'=2] {'x','yl'}, dimensions={0} | all-to-all | bytes 4259840 | tf_op jit(solution)/shard_map/all_to_all | solution.py:315
  87.4 3.0 %share.1 = bf16[16,64,128]{2,1,0:T(8,128)(2,1)} custom-call(s16[8,1040,128]{2,1,0:T(8,128)(2,1)} %all_to_all.20.in_ref), custom_call_target="tpu_custom_call" | custom-call | tf_op jit(solution)/shard_map/share/pallas_call | solution.py:175
  90.3 1.5 broadcast_in_dim.6
  91.8 28.4 %all_to_all.21 = bf16[8,16,64,128]{3,2,1,0:T(8,128)(2,1)S(1)} all-to-all(bf16[8,16,64,128]{3,2,1,0:T(8,128)(2,1)S(1)} %broadcast_in_dim.6), channel_id=1, replica_groups=mesh['yh'=2,'z'=4,'x'=4,'yl'=2,'core'=2] {'x','yl'}, dimensions={0} | all-to-all | bytes 4194304 | tf_op jit(solution)/shard_map/all_to_all | solution.py:299
  120.2 0.0 copy-start
  120.2 0.0 collective-permute-start.1
  120.2 4.2 %collective-permute-done.1.theirs_ref = bf16[128,64,128]{2,1,0:T(8,128)(2,1)S(1)} collective-permute-done((bf16[128,64,128]{2,1,0:T(8,128)(2,1)S(1)}, bf16[128,64,128]{2,1,0:T(8,128)(2,1)S(1)}, u32[]{:S(2)}, u32[]{:S(2)}) %collective-permute-start.1) | collective-permute-done | bytes 2097184 | tf_op jit(solution)/shard_map/ppermute | solution.py:317
  124.3 0.0 copy-done
  124.3 0.0 copy-start.2
  124.3 1.3 copy-done.2
  125.6 32.0 %backward.1 = s16[8,1040,128]{2,1,0:T(8,128)(2,1)} custom-call(s32[1024]{0:T(1024)} %reshape_squeeze.3.coords, s32[2]{0:T(128)} %pad_add_fusion.info, bf16[128,64,128]{2,1,0:T(8,128)(2,1)} %bitcast.11, bf16[128,64,128]{2,1,0:T(8,128)(2,1)} %copy-done.2, bf16[512,128,128]{2,1,0:T(8,128)(2,1)} %bitcast.9), custom_call_target="tpu_custom_call" | custom-call | tf_op jit(solution)/shard_map/backward/pallas_call | solution.py:223
  157.6 34.6 %all_to_all.22.in_ref = s16[8,1040,128]{2,1,0:T(8,128)(2,1)} all-to-all(s16[8,1040,128]{2,1,0:T(8,128)(2,1)} %backward.1), channel_id=1, replica_groups=mesh['yh'=2,'z'=4,'x'=4,'yl'=2,'core'=2] {'yh','z'}, dimensions={0} | all-to-all | bytes 4259840 | tf_op jit(solution)/shard_map/all_to_all | solution.py:319
  192.3 3.4 %again.1 = s16[1,1040,128]{2,1,0:T(8,128)(2,1)} custom-call(s16[8,1040,128]{2,1,0:T(8,128)(2,1)} %all_to_all.22.in_ref), custom_call_target="tpu_custom_call" | custom-call | tf_op jit(solution)/shard_map/again/pallas_call | solution.py:263
  195.6 1.2 broadcast_in_dim.15
  196.9 32.3 %all_to_all.23.in_ref = s16[8,1040,128]{2,1,0:T(8,128)(2,1)} all-to-all(s16[8,1040,128]{2,1,0:T(8,128)(2,1)S(1)} %broadcast_in_dim.15), channel_id=1, replica_groups=mesh['yh'=2,'z'=4,'x'=4,'yl'=2,'core'=2] {'yh','z'}, dimensions={0} | all-to-all | bytes 4259840 | tf_op jit(solution)/shard_map/all_to_all | solution.py:299
  229.2 6.1 %spread.1 = f32[64,16384]{1,0:T(8,128)} custom-call(s16[8,1040,128]{2,1,0:T(8,128)(2,1)} %all_to_all.23.in_ref), custom_call_target="tpu_custom_call" | custom-call | tf_op jit(solution)/shard_map/spread/pallas_call | solution.py:284
Async XLA Ops:
  35.8 7.4 %collective-permute-start = (f32[128,64,128]{2,1,0:T(8,128)}, f32[128,64,128]{2,1,0:T(8,128)S(1)}, u32[]{:S(2)}, u32[]{:S(2)}) collective-permute-start(f32[128,64,128]{2,1,0:T(8,128)} %get-tuple-element.8), channel_id=1, source_target_pairs={{0,1},{1,0},{2,3},{3,2},{4,5},{5,4},{6,7},{7,6},{8,9},{9,8},{10,11... | collective-permute-start | bytes 12582920 | tf_op jit(solution)/shard_map/ppermute | solution.py:314
  43.3 1.9 copy-start.1
  120.2 4.2 %copy-start = (bf16[8,16,64,128]{3,2,1,0:T(8,128)(2,1)}, bf16[8,16,64,128]{3,2,1,0:T(8,128)(2,1)S(1)}, u32[]{:S(2)}) copy-start(bf16[8,16,64,128]{3,2,1,0:T(8,128)(2,1)S(1)} %all_to_all.21) | copy-start | bytes 6291460
  120.2 4.2 %collective-permute-start.1 = (bf16[128,64,128]{2,1,0:T(8,128)(2,1)S(1)}, bf16[128,64,128]{2,1,0:T(8,128)(2,1)S(1)}, u32[]{:S(2)}, u32[]{:S(2)}) collective-permute-start(bf16[128,64,128]{2,1,0:T(8,128)(2,1)S(1)} %bitcast.10), channel_id=1, source_target_pairs={{0,1},{1,0},{2,3},{3,2},{4,5},{5,4},{6,7},{7,6},{8,9},{9,8},{10,11... | collective-permute-start | bytes 6291464 | tf_op jit(solution)/shard_map/ppermute | solution.py:317
  124.3 1.3 copy-start.2

commit v2 on v0

v2 whole, which is shorter than its diff:
```python
import functools

import jax
import jax.numpy as jnp
from jax import lax
from jax.experimental import pallas as pl
from jax.experimental.pallas import tpu as pltpu
from jax.sharding import Mesh
from jax.sharding import PartitionSpec as P

TILE = 128
CHUNK = 64
UNROLL = 64
LAG = 8
BLOCKS = 4
LEVEL = 32700.0
STEPS = 8.0
MIB = 1024 * 1024
ROW = ("yh", "z")
CHIPS = ("x", "yl")
F32 = jnp.float32
I16 = jnp.int16


def params(mib):
    return pltpu.CompilerParams(vmem_limit_bytes=mib * MIB)


def code(block):
    top = jnp.maximum(jnp.max(jnp.abs(block), axis=0, keepdims=True), 1e-30)
    step = jnp.ceil(jnp.log2(top) * STEPS)
    return step, jnp.exp2(step * (-1.0 / STEPS)) * LEVEL


def factor(step):
    return jnp.exp2(step * (1.0 / STEPS)) * (1.0 / LEVEL)


def put_blocks(read, count, piece, out_ref, steps):
    rows = out_ref.shape[1] - count
    width = rows // count

    def body(i, _):
        for u in range(BLOCKS):
            j = i * BLOCKS + u
            block = read(j)
            step, gain = code(block)
            whole = jnp.round(block * gain).astype(jnp.int32)
            out_ref[piece, pl.ds(pl.multiple_of(j * width, width), width), :] = whole.astype(I16)
            steps[pl.ds(j, 1), :] = step
        return 0

    lax.fori_loop(0, count // BLOCKS, body, 0)
    out_ref[piece, rows:, :] = steps[:count].astype(jnp.int32).astype(I16)


def sparse_step(transposed, coords, base, source, tiles_ref, acc):
    def body(i, _):
        waiting = []
        for u in range(UNROLL + LAG):
            if u < UNROLL:
                slot = base + i * UNROLL + u
                r, c = coords[2 * slot], coords[2 * slot + 1]
                if transposed:
                    left = source[:, pl.ds(pl.multiple_of(c * TILE, TILE), TILE)]
                    dims = (((1,), (1,)), ((), ()))
                    value = lax.dot_general(left, tiles_ref[slot], dims, preferred_element_type=F32)
                    waiting.append((r, value))
                else:
                    value = jnp.dot(source[r], tiles_ref[slot], preferred_element_type=F32)
                    waiting.append((c, value))
            if u >= LAG:
                target, value = waiting[u - LAG]
                acc[target] += value
        return 0

    lax.fori_loop(0, CHUNK // UNROLL, body, 0)


def fetch(count, tiles_ref, tiles, sem):
    def part(j):
        rows = pl.ds(j * CHUNK, CHUNK)
        return pltpu.make_async_copy(tiles_ref.at[rows], tiles.at[rows], sem.at[j])

    chunks = lax.div(count + (CHUNK - 1), CHUNK)
    lax.fori_loop(0, chunks, lambda j, _: (part(j).start(), 0)[1], 0)
    return chunks, part


def forward_kernel(coords, info, omega_ref, tiles_ref, keep_ref, give_ref, acc, omega, tiles, steps, tile_sem, sem):
    half = acc.shape[0] // 2
    width = acc.shape[1]
    load = pltpu.make_async_copy(omega_ref, omega, sem.at[0])
    load.start()
    chunks, part = fetch(info[0], tiles_ref, tiles, tile_sem)
    acc[...] = jnp.zeros_like(acc)
    load.wait()

    def chunk(j, _):
        part(j).wait()
        sparse_step(True, coords, j * CHUNK, omega, tiles, acc)
        return 0

    lax.fori_loop(0, chunks, chunk, 0)
    core = info[1]
    keep = pltpu.make_async_copy(acc.at[pl.ds(core * half, half)], keep_ref, sem.at[1])
    keep.start()
    put_blocks(lambda j: acc[(1 - core) * half + j], half, 0, give_ref, steps)
    keep.wait()


def forward(tiles, coords, info, omega, blk_row):
    slots = tiles.shape[0]
    width = omega.shape[0]
    half = blk_row // 2
    give = jax.ShapeDtypeStruct((1, half * (width + 1), TILE), I16)
    return pl.pallas_call(
        forward_kernel,
        out_shape=(jax.ShapeDtypeStruct((half, width, TILE), F32), give),
        in_specs=[pl.BlockSpec(memory_space=pltpu.SMEM)] * 2 + [pl.BlockSpec(memory_space=pl.ANY)] * 2,
        out_specs=[pl.BlockSpec(memory_space=pl.ANY), pl.BlockSpec(memory_space=pltpu.VMEM)],
        scratch_shapes=[
            pltpu.VMEM((blk_row, width, TILE), F32),
            pltpu.VMEM(omega.shape, omega.dtype),
            pltpu.VMEM(tiles.shape, tiles.dtype),
            pltpu.VMEM((half, TILE), F32),
            pltpu.SemaphoreType.DMA((slots // CHUNK,)),
            pltpu.SemaphoreType.DMA((2,)),
        ],
        compiler_params=params(40),
        name="forward",
    )(coords, info, omega, tiles)


def pair_kernel(keep_ref, got_ref, codes_ref, out_ref, scale, steps):
    each, width, _ = keep_ref.shape
    scale[...] = factor(codes_ref[0].astype(jnp.int32).astype(F32))

    def read(j):
        got = got_ref[0, pl.ds(pl.multiple_of(j * width, width), width), :].astype(jnp.int32).astype(F32)
        return keep_ref[j] + got * scale[pl.ds(j, 1), :]

    put_blocks(read, each, 0, out_ref, steps)


def pair(keep, got, pieces):
    blocks, width, _ = keep.shape
    each = blocks // pieces
    rows = each * width + each
    return pl.pallas_call(
        pair_kernel,
        out_shape=jax.ShapeDtypeStruct((pieces, rows, TILE), I16),
        grid=(pieces,),
        in_specs=[
            pl.BlockSpec((each, width, TILE), lambda i: (i, 0, 0)),
            pl.BlockSpec((1, each * width, TILE), lambda i: (0, i, 0)),
            pl.BlockSpec((1, each, TILE), lambda i: (0, pieces * width + i, 0)),
        ],
        out_specs=pl.BlockSpec((1, rows, TILE), lambda i: (i, 0, 0)),
        scratch_shapes=[pltpu.VMEM((each, TILE), F32)] * 2,
        compiler_params=params(12),
        name="pair",
    )(keep, got, got)


def gather_sum(in_ref, scale, j, width):
    total = None
    for s in range(in_ref.shape[0]):
        part = in_ref[s, pl.ds(pl.multiple_of(j * width, width), width), :].astype(jnp.int32).astype(F32)
        part = part * scale[s, pl.ds(j, 1), :]
        total = part if total is None else total + part
    return total


def scales(in_ref, scale, rows):
    for s in range(in_ref.shape[0]):
        scale[s] = factor(in_ref[s, rows:, :].astype(jnp.int32).astype(F32))


def share_kernel(in_ref, out_ref, scale):
    each, width, _ = out_ref.shape
    scales(in_ref, scale, each * width)

    def body(j, _):
        out_ref[j] = gather_sum(in_ref, scale, j, width).astype(out_ref.dtype)
        return 0

    lax.fori_loop(0, each, body, 0)


def share(parts, width):
    pieces, rows, _ = parts.shape
    each = rows // (width + 1)
    return pl.pallas_call(
        share_kernel,
        out_shape=jax.ShapeDtypeStruct((each, width, TILE), jnp.bfloat16),
        scratch_shapes=[pltpu.VMEM((pieces, each, TILE), F32)],
        compiler_params=params(12),
        name="share",
    )(parts)


def backward_kernel(coords, info, *refs):
    shares, (tiles_ref, out_ref, acc, inner, tiles, steps, tile_sem, sem) = refs[:-8], refs[-8:]
    pieces = out_ref.shape[0]
    each = acc.shape[0] // pieces
    size = shares[0].shape[0]
    loads = []
    for n, ref in enumerate(shares):
        to = inner.at[pl.ds(info[1 + n] * size, size)]
        loads.append(pltpu.make_async_copy(ref, to, sem.at[n]))
        loads[-1].start()
    chunks, part = fetch(info[0], tiles_ref, tiles, tile_sem)
    acc[...] = jnp.zeros_like(acc)
    for load in loads:
        load.wait()

    def chunk(j, _):
        part(j).wait()
        sparse_step(False, coords, j * CHUNK, inner, tiles, acc)
        return 0

    lax.fori_loop(0, chunks, chunk, 0)
    for s in range(pieces):
        put_blocks(lambda j: acc[s * each + j], each, s, out_ref, steps)


def backward(tiles, coords, info, shares, blk_col, pieces):
    slots = tiles.shape[0]
    size, width, _ = shares[0].shape
    each = blk_col // pieces
    rows = each * width + each
    return pl.pallas_call(
        backward_kernel,
        out_shape=jax.ShapeDtypeStruct((pieces, rows, TILE), I16),
        in_specs=[pl.BlockSpec(memory_space=pltpu.SMEM)] * 2 + [pl.BlockSpec(memory_space=pl.ANY)] * (len(shares) + 1),
        out_specs=pl.BlockSpec(memory_space=pltpu.VMEM),
        scratch_shapes=[
            pltpu.VMEM((blk_col, width, TILE), F32),
            pltpu.VMEM((len(shares) * size, width, TILE), jnp.bfloat16),
            pltpu.VMEM(tiles.shape, tiles.dtype),
            pltpu.VMEM((each, TILE), F32),
            pltpu.SemaphoreType.DMA((slots // CHUNK,)),
            pltpu.SemaphoreType.DMA((len(shares),)),
        ],
        compiler_params=params(40),
        name="backward",
    )(coords, info, *shares, tiles)


def again_kernel(in_ref, out_ref, scale, steps):
    each = scale.shape[1]
    width = (out_ref.shape[1] - each) // each
    scales(in_ref, scale, each * width)
    put_blocks(lambda j: gather_sum(in_ref, scale, j, width), each, 0, out_ref, steps)


def again(parts, width):
    pieces, rows, _ = parts.shape
    each = rows // (width + 1)
    return pl.pallas_call(
        again_kernel,
        out_shape=jax.ShapeDtypeStruct((1, rows, TILE), I16),
        scratch_shapes=[pltpu.VMEM((pieces, each, TILE), F32), pltpu.VMEM((each, TILE), F32)],
        compiler_params=params(12),
        name="again",
    )(parts)


def spread_kernel(info, *refs):
    parts, (out_ref, scale, buffer, sem) = refs[:-4], refs[-4:]
    each = scale.shape[0]
    width = buffer.shape[1]
    size = each * TILE

    def store(n):
        columns = pl.ds(pl.multiple_of(info[n] * size, size), size)
        return pltpu.make_async_copy(buffer.at[n], out_ref.at[:, columns], sem.at[n])

    for n, ref in enumerate(parts):
        scale[...] = factor(ref[each * width :, :].astype(jnp.int32).astype(F32))
        for j in range(each):
            part = ref[j * width : (j + 1) * width, :].astype(jnp.int32).astype(F32)
            buffer[n, :, j * TILE : (j + 1) * TILE] = part * scale[j : j + 1, :]
        store(n).start()
    for n in range(len(parts)):
        store(n).wait()


def spread(info, parts, width):
    rows = parts[0].shape[0]
    each = rows // (width + 1)
    count = len(parts)
    return pl.pallas_call(
        spread_kernel,
        out_shape=jax.ShapeDtypeStruct((width, count * each * TILE), F32),
        in_specs=[pl.BlockSpec(memory_space=pltpu.SMEM)] + [pl.BlockSpec(memory_space=pltpu.VMEM)] * count,
        out_specs=pl.BlockSpec(memory_space=pl.ANY),
        scratch_shapes=[
            pltpu.VMEM((each, TILE), F32),
            pltpu.VMEM((count, width, each * TILE), F32),
            pltpu.SemaphoreType.DMA((count,)),
        ],
        compiler_params=params(16),
        name="spread",
    )(info, *parts)


def shift(value, axis, by):
    count = lax.axis_size(axis)
    return lax.ppermute(value, axis, [(i, (i + by) % count) for i in range(count)])


def gather(value, ring, pair):
    i, j = lax.axis_index(ring), lax.axis_index(pair)
    across = shift(value, pair, 1)
    up = shift(value, ring, 1)
    down = shift(value, ring, -1)
    down_across = shift(down, pair, 1)
    up_across = shift(across, ring, 1)
    far = shift(down, ring, -1)
    far_across = shift(far, pair, 1)
    shares = [value, across, up, down, up_across, down_across, far, far_across]
    hops = [(0, 0), (0, 1), (-1, 0), (1, 0), (-1, 1), (1, 1), (2, 0), (2, 1)]
    return shares, [lax.rem(i + a + 4, 4) * 2 + lax.rem(j + b, 2) for a, b in hops]


def shards(tiles, tile_coords, tile_counts, omega):
    blocks = tiles[0, 0]
    coords = tile_coords[0, 0].reshape(-1)
    count = tile_counts[0, 0]
    core = lax.axis_index("core")
    width = omega.shape[0]
    blk_col = omega.shape[1] // TILE
    rows = lax.axis_size(ROW)
    chips = lax.axis_size(CHIPS)
    blk_row = blk_col * 2 * chips // rows
    keep, give = forward(blocks, coords, jnp.stack([count, core]), omega, blk_row)
    parts = lax.all_to_all(pair(keep, shift(give, "core", 1), chips), CHIPS, 0, 0, tiled=True)
    mine, places = gather(share(parts, width), *CHIPS)
    theirs = [shift(value, "core", 1) for value in mine]
    places = [core * chips + p for p in places] + [(1 - core) * chips + p for p in places]
    out = backward(blocks, coords, jnp.stack([count, *places]), mine + theirs, blk_col, rows)
    parts = lax.all_to_all(out, ROW, 0, 0, tiled=True)
    parts, places = gather(again(parts, width)[0], "z", "yh")
    places = [lax.rem(p, 2) * 4 + lax.div(p, 2) for p in places]
    return spread(jnp.stack(places), parts, width)


def solution(mesh):
    fine = Mesh(mesh.devices.reshape(2, 4, 4, 2, 2), ("yh", "z", "x", "yl", "core"))
    col = ("x", "yl", "core")
    return jax.shard_map(
        shards,
        mesh=fine,
        in_specs=(
            P(ROW, col, None, None, None),
            P(ROW, col, None, None),
            P(ROW, col),
            P(None, col),
        ),
        out_specs=P(None, col),
        check_vma=False,
    )
```

time: 532 us -> 160 us (0.30)
  waiting for transfers between devices: 247 us -> 43.1 us
  other arithmetic: 159 us -> 0.08 us
  local copies, waits for them, and re-layouts: 74.2 us -> 2.76 us
  blocking collectives: 0 us -> 67.3 us
  matrix products: 34.7 us -> 0 us
  Pallas kernels: 0 us -> 32.5 us
  starting transfers between devices: 0.27 us -> 13.5 us
  between operations: 13.8 us -> 0.77 us
    scatter-add x2 -> x0, other arithmetic: 156 us -> none  [the longest x1 78.4 us: shards(): jax.ops.segment_sum(forward, rows_local, num_segments=blk_row)]
    psum x1 -> x0, waiting for transfers between devices: 110 us -> none  [shards(): sketch = lax.psum(column_part, 'row')]
    reduce_scatter x1 -> x0, waiting for transfers between devices: 97.8 us -> none  [shards(): lax.psum_scatter(partial_value, 'col', scatter_dimension=1, tiled=True)]
    all_to_all x0 -> x2, blocking collectives: none -> 67.3 us  [the longest x1 34.4 us: shards(): parts = lax.all_to_all(out, ROW, 0, 0, tiled=True)]
    ppermute x0 -> x23, waiting for transfers between devices: none -> 43.1 us  [shift(): lax.ppermute(value, axis, [(i, (i + by) % count) for i in range(count)])]
    gather x2 -> x0, local copies, waits for them, and re-layouts: 43.1 us -> none  [the longest x1 21.8 us: shards(): gathered = jnp.take(inner_blocks, rows_local, axis=0)]
    all_gather x1 -> x0, waiting for transfers between devices: 39.5 us -> none  [shards(): inner = lax.all_gather(share, 'col', axis=1, tiled=True)]
    dot_general x2 -> x0, matrix products: 34.7 us -> none  [the longest x1 20.2 us: shards(): jnp.einsum('kcb,krb->kcr', picked, blocks, preferred_element_type=jnp.flo...]
  transfers between devices with their start and end apart: 3 -> 23, of which waited for: 3 -> 13; matrix products, arithmetic and copies ran while one was open for 0% -> 0% of each run, Pallas kernels for 0% -> 0%
where the time goes in v2:
time: 160 us
  blocking collectives  67.3 us (42%)
  waiting for transfers between devices  43.1 us (27%)
  Pallas kernels  32.5 us (20%)
  starting transfers between devices  13.5 us (8%)
  local copies, waits for them, and re-layouts  2.76 us (2%)
    ppermute x23, waiting for transfers between devices, shift(): lax.ppermute(value, axis, [(i, (i + by) % count) for i in range(count)])  43.1 us
    all_to_all x1, blocking collectives, shards(): parts = lax.all_to_all(out, ROW, 0, 0, tiled=True)  34.4 us
    all_to_all x1, blocking collectives, shards(): lax.all_to_all(pair(keep, shift(give, 'core', 1), chips), CHIPS, 0, 0, ti...  33 us
    pallas_call x1, Pallas kernels, forward(): pl.pallas_call(forward_kernel, out_shape=(jax.ShapeDtypeStruct((half, wid...  16.5 us
    ppermute x23, starting transfers between devices, shift(): lax.ppermute(value, axis, [(i, (i + by) % count) for i in range(count)])  13.5 us
    pallas_call x1, Pallas kernels, backward(): pl.pallas_call(backward_kernel, out_shape=jax.ShapeDtypeStruct((pieces, r...  9.85 us
  transfers between devices with their start and end apart: 23, of which 13 were waited for; matrix products, arithmetic and copies ran while one was open for 0% of the time, Pallas kernels for 0%

profile of v2, /device:TPU:0, one launch (start us, length us, event | category | flops | bytes accessed | tf_op | source)
XLA Modules:
  0.0 160.1 jit_solution(10261860391530319286)
XLA Ops:
  0.7 0.8 copy.5
  1.5 0.2 reshape_squeeze.3.coords
  1.7 0.1 pad_add_fusion.info
  1.7 0.0 copy-start
  1.7 1.6 copy-done
  3.3 16.5 %forward.1 = (f32[128,64,128]{2,1,0:T(8,128)S(1)}, s16[1,8320,128]{2,1,0:T(8,128)(2,1)S(1)}) custom-call(s32[1024]{0:T(1024)S(1)} %reshape_squeeze.3.coords, s32[2]{0:T(128)S(1)} %pad_add_fusion.info, bf16[64,16384]{1,0:T(8,128)(2,1)S(1)} %copy-done, bf16[512,128,128]{2,1,0:T(8,128)(2,1)} %bitcast.36), custom_call_target="tpu_custom_call" | custom-call | tf_op jit(solution)/shard_map/forward/pallas_call | solution.py:117
  19.8 0.1 collective-permute-start
  19.9 4.2 %collective-permute-done.got_ref.codes_ref = s16[1,8320,128]{2,1,0:T(8,128)(2,1)S(1)} collective-permute-done((s16[1,8320,128]{2,1,0:T(8,128)(2,1)S(1)}, s16[1,8320,128]{2,1,0:T(8,128)(2,1)S(1)}, u32[]{:S(2)}, u32[]{:S(2)}) %collective-permute-start) | collective-permute-done | bytes 2129952 | tf_op jit(solution)/shard_map/ppermute | solution.py:311
  24.1 2.2 %pair.1 = s16[8,1040,128]{2,1,0:T(8,128)(2,1)S(1)} custom-call(f32[128,64,128]{2,1,0:T(8,128)S(1)} %get-tuple-element.7.keep_ref, s16[1,8320,128]{2,1,0:T(8,128)(2,1)S(1)} %collective-permute-done.got_ref.codes_ref, s16[1,8320,128]{2,1,0:T(8,128)(2,1)S(1)} %collective-permute-done.got_ref.codes_ref), custom_call_target="tpu_custom_call" | custom-call | tf_op jit(solution)/shard_map/pair/pallas_call | solution.py:150
  26.3 33.0 %all_to_all.10.in_ref = s16[8,1040,128]{2,1,0:T(8,128)(2,1)S(1)} all-to-all(s16[8,1040,128]{2,1,0:T(8,128)(2,1)S(1)} %pair.1), channel_id=1, replica_groups=mesh['yh'=2,'z'=4,'x'=4,'yl'=2,'core'=2] {'x','yl'}, dimensions={0} | all-to-all | bytes 4259840 | tf_op jit(solution)/shard_map/all_to_all | solution.py:339
  59.3 0.6 share.1.refs_0_
  59.9 1.2 collective-permute-start.3
  61.1 0.0 collective-permute-start.8
  61.2 0.9 collective-permute-start.2
  62.0 0.7 collective-permute-start.1
  62.7 4.3 %collective-permute-done.3.refs_3_ = bf16[16,64,128]{2,1,0:T(8,128)(2,1)S(1)} collective-permute-done((bf16[16,64,128]{2,1,0:T(8,128)(2,1)S(1)}, bf16[16,64,128]{2,1,0:T(8,128)(2,1)S(1)}, u32[]{:S(2)}, u32[]{:S(2)}) %collective-permute-start.3) | collective-permute-done | bytes 262176 | tf_op jit(solution)/shard_map/ppermute | solution.py:311
  67.0 2.4 %collective-permute-start.6 = (bf16[16,64,128]{2,1,0:T(8,128)(2,1)S(1)}, bf16[16,64,128]{2,1,0:T(8,128)(2,1)S(1)}, u32[]{:S(2)}, u32[]{:S(2)}) collective-permute-start(bf16[16,64,128]{2,1,0:T(8,128)(2,1)S(1)} %collective-permute-done.3.refs_3_), channel_id=1, source_target_pairs={{0,12},{4,0},{8,4},{12,8},{1,13},{5,1},{9,5},{13,9},{2,14},{6,2},{... | collective-permute-start | bytes 786440 | tf_op jit(solution)/shard_map/ppermute | solution.py:311
  69.4 0.0 collective-permute-start.11
  69.4 0.0 collective-permute-done.8.refs_8_
  69.4 0.5 collective-permute-start.5
  70.0 1.1 collective-permute-done.2.refs_2_
  71.1 0.0 collective-permute-start.10
  71.1 0.0 collective-permute-done.1.refs_1_
  71.1 0.0 collective-permute-start.4
  71.1 2.3 %collective-permute-done.6.refs_6_ = bf16[16,64,128]{2,1,0:T(8,128)(2,1)S(1)} collective-permute-done((bf16[16,64,128]{2,1,0:T(8,128)(2,1)S(1)}, bf16[16,64,128]{2,1,0:T(8,128)(2,1)S(1)}, u32[]{:S(2)}, u32[]{:S(2)}) %collective-permute-start.6) | collective-permute-done | bytes 262176 | tf_op jit(solution)/shard_map/ppermute | solution.py:311
  73.4 0.8 collective-permute-start.7
  74.2 0.0 collective-permute-done.11.refs_11_
  74.2 0.0 collective-permute-start.9
  74.2 4.3 %collective-permute-done.5.refs_5_ = bf16[16,64,128]{2,1,0:T(8,128)(2,1)S(1)} collective-permute-done((bf16[16,64,128]{2,1,0:T(8,128)(2,1)S(1)}, bf16[16,64,128]{2,1,0:T(8,128)(2,1)S(1)}, u32[]{:S(2)}, u32[]{:S(2)}) %collective-permute-start.5) | collective-permute-done | bytes 262176 | tf_op jit(solution)/shard_map/ppermute | solution.py:311
  78.5 0.0 collective-permute-start.14
  78.5 0.0 collective-permute-done.10.refs_10_
  78.5 0.5 collective-permute-start.13
  79.0 2.0 %collective-permute-done.4.refs_4_ = bf16[16,64,128]{2,1,0:T(8,128)(2,1)S(1)} collective-permute-done((bf16[16,64,128]{2,1,0:T(8,128)(2,1)S(1)}, bf16[16,64,128]{2,1,0:T(8,128)(2,1)S(1)}, u32[]{:S(2)}, u32[]{:S(2)}) %collective-permute-start.4) | collective-permute-done | bytes 262176 | tf_op jit(solution)/shard_map/ppermute | solution.py:311
  81.0 0.0 collective-permute-start.12
  81.0 2.7 %collective-permute-done.7.refs_7_ = bf16[16,64,128]{2,1,0:T(8,128)(2,1)S(1)} collective-permute-done((bf16[16,64,128]{2,1,0:T(8,128)(2,1)S(1)}, bf16[16,64,128]{2,1,0:T(8,128)(2,1)S(1)}, u32[]{:S(2)}, u32[]{:S(2)}) %collective-permute-start.7) | collective-permute-done | bytes 262176 | tf_op jit(solution)/shard_map/ppermute | solution.py:311
  83.8 0.0 collective-permute-start.15
  83.8 0.1 stack.109.info
  83.9 0.0 collective-permute-done.9.refs_9_
  83.9 0.0 collective-permute-done.14.refs_14_
  83.9 0.0 collective-permute-done.13.refs_13_
  83.9 0.0 collective-permute-done.12.refs_12_
  83.9 1.5 collective-permute-done.15.refs_15_
  85.4 9.9 %backward.1 = s16[8,1040,128]{2,1,0:T(8,128)(2,1)S(1)} custom-call(s32[1024]{0:T(1024)S(1)} %reshape_squeeze.3.coords, s32[17]{0:T(128)S(1)} %stack.109.info, bf16[16,64,128]{2,1,0:T(8,128)(2,1)S(1)} %share.1.refs_0_, bf16[16,64,128]{2,1,0:T(8,128)(2,1)S(1)} %collective-permute-done.1.refs_1_, bf16[16,64,128]{2,1,0:T(8,128)(2,1)S(1)} %collective-permute-done.2.refs_2_, ...), custom_call_target="tpu_custom_call" | custom-call | tf_op jit(solution)/shard_map/backward/pallas_call | solution.py:233
  95.3 34.4 %all_to_all.11.in_ref = s16[8,1040,128]{2,1,0:T(8,128)(2,1)S(1)} all-to-all(s16[8,1040,128]{2,1,0:T(8,128)(2,1)S(1)} %backward.1), channel_id=1, replica_groups=mesh['yh'=2,'z'=4,'x'=4,'yl'=2,'core'=2] {'yh','z'}, dimensions={0} | all-to-all | bytes 4259840 | tf_op jit(solution)/shard_map/all_to_all | solution.py:344
  129.7 0.7 again.1
  130.4 1.2 collective-permute-start.18
  131.6 1.4 collective-permute-start.16
  133.0 6.7 %collective-permute-done.18.refs_3_ = s16[1040,128]{1,0:T(8,128)(2,1)S(1)} collective-permute-done((s16[1040,128]{1,0:T(8,128)(2,1)S(1)}, s16[1040,128]{1,0:T(8,128)(2,1)S(1)}, u32[]{:S(2)}, u32[]{:S(2)}) %collective-permute-start.18) | collective-permute-done | bytes 266272 | tf_op jit(solution)/shard_map/ppermute | solution.py:311
  139.7 2.4 %collective-permute-start.21 = (s16[1040,128]{1,0:T(8,128)(2,1)S(1)}, s16[1040,128]{1,0:T(8,128)(2,1)S(1)}, u32[]{:S(2)}, u32[]{:S(2)}) collective-permute-start(s16[1040,128]{1,0:T(8,128)(2,1)S(1)} %collective-permute-done.18.refs_3_), channel_id=1, source_target_pairs={{0,48},{16,0},{32,16},{48,32},{1,49},{17,1},{33,17},{49,33},{2,50}... | collective-permute-start | bytes 798728 | tf_op jit(solution)/shard_map/ppermute | solution.py:311
  142.1 0.0 collective-permute-start.17
  142.1 0.7 collective-permute-start.20
  142.8 0.0 collective-permute-done.16.refs_1_
  142.8 0.2 collective-permute-start.19
  143.0 5.2 %collective-permute-done.21.refs_6_ = s16[1040,128]{1,0:T(8,128)(2,1)S(1)} collective-permute-done((s16[1040,128]{1,0:T(8,128)(2,1)S(1)}, s16[1040,128]{1,0:T(8,128)(2,1)S(1)}, u32[]{:S(2)}, u32[]{:S(2)}) %collective-permute-start.21) | collective-permute-done | bytes 266272 | tf_op jit(solution)/shard_map/ppermute | solution.py:311
  148.1 0.5 collective-permute-start.22
  148.6 0.1 stack.92.info
  148.7 3.9 %collective-permute-done.17.refs_2_ = s16[1040,128]{1,0:T(8,128)(2,1)S(1)} collective-permute-done((s16[1040,128]{1,0:T(8,128)(2,1)S(1)}, s16[1040,128]{1,0:T(8,128)(2,1)S(1)}, u32[]{:S(2)}, u32[]{:S(2)}) %collective-permute-start.17) | collective-permute-done | bytes 266272 | tf_op jit(solution)/shard_map/ppermute | solution.py:311
  152.6 0.0 collective-permute-done.20.refs_5_
  152.6 4.6 %collective-permute-done.19.refs_4_ = s16[1040,128]{1,0:T(8,128)(2,1)S(1)} collective-permute-done((s16[1040,128]{1,0:T(8,128)(2,1)S(1)}, s16[1040,128]{1,0:T(8,128)(2,1)S(1)}, u32[]{:S(2)}, u32[]{:S(2)}) %collective-permute-start.19) | collective-permute-done | bytes 266272 | tf_op jit(solution)/shard_map/ppermute | solution.py:311
  157.1 0.3 collective-permute-done.22.refs_7_
  157.4 2.7 %spread.1 = f32[64,16384]{1,0:T(8,128)} custom-call(s32[8]{0:T(128)S(1)} %stack.92.info, s16[1040,128]{1,0:T(8,128)(2,1)S(1)} %bitcast.35, s16[1040,128]{1,0:T(8,128)(2,1)S(1)} %collective-permute-done.16.refs_1_, s16[1040,128]{1,0:T(8,128)(2,1)S(1)} %collective-permute-done.17.refs_2_, s16[1040,128]{1,0:T(8,128)(2,1)S(1)} %collective-permute-done.18.refs_3_, ...), custom_call_target="tpu_custom_call" | custom-call | tf_op jit(solution)/shard_map/spread/pallas_call | solution.py:294
Async XLA Ops:
  1.7 1.6 copy-start
  19.8 4.3 %collective-permute-start = (s16[1,8320,128]{2,1,0:T(8,128)(2,1)S(1)}, s16[1,8320,128]{2,1,0:T(8,128)(2,1)S(1)}, u32[]{:S(2)}, u32[]{:S(2)}) collective-permute-start(s16[1,8320,128]{2,1,0:T(8,128)(2,1)S(1)} %get-tuple-element.8), channel_id=1, source_target_pairs={{0,1},{1,0},{2,3},{3,2},{4,5},{5,4},{6,7},{7,6},{8,9},{9,8},{10,11... | collective-permute-start | bytes 6389768 | tf_op jit(solution)/shard_map/ppermute | solution.py:311
  59.9 7.1 %collective-permute-start.3 = (bf16[16,64,128]{2,1,0:T(8,128)(2,1)S(1)}, bf16[16,64,128]{2,1,0:T(8,128)(2,1)S(1)}, u32[]{:S(2)}, u32[]{:S(2)}) collective-permute-start(bf16[16,64,128]{2,1,0:T(8,128)(2,1)S(1)} %share.1.refs_0_), channel_id=1, source_target_pairs={{0,12},{4,0},{8,4},{12,8},{1,13},{5,1},{9,5},{13,9},{2,14},{6,2},{... | collective-permute-start | bytes 786440 | tf_op jit(solution)/shard_map/ppermute | solution.py:311
  61.1 8.3 %collective-permute-start.8 = (bf16[16,64,128]{2,1,0:T(8,128)(2,1)S(1)}, bf16[16,64,128]{2,1,0:T(8,128)(2,1)S(1)}, u32[]{:S(2)}, u32[]{:S(2)}) collective-permute-start(bf16[16,64,128]{2,1,0:T(8,128)(2,1)S(1)} %share.1.refs_0_), channel_id=1, source_target_pairs={{0,1},{1,0},{2,3},{3,2},{4,5},{5,4},{6,7},{7,6},{8,9},{9,8},{10,11... | collective-permute-start | bytes 786440 | tf_op jit(solution)/shard_map/ppermute | solution.py:311
  61.2 9.9 %collective-permute-start.2 = (bf16[16,64,128]{2,1,0:T(8,128)(2,1)S(1)}, bf16[16,64,128]{2,1,0:T(8,128)(2,1)S(1)}, u32[]{:S(2)}, u32[]{:S(2)}) collective-permute-start(bf16[16,64,128]{2,1,0:T(8,128)(2,1)S(1)} %share.1.refs_0_), channel_id=1, source_target_pairs={{0,4},{4,8},{8,12},{12,0},{1,5},{5,9},{9,13},{13,1},{2,6},{6,10},{... | collective-permute-start | bytes 786440 | tf_op jit(solution)/shard_map/ppermute | solution.py:311
  62.0 9.1 %collective-permute-start.1 = (bf16[16,64,128]{2,1,0:T(8,128)(2,1)S(1)}, bf16[16,64,128]{2,1,0:T(8,128)(2,1)S(1)}, u32[]{:S(2)}, u32[]{:S(2)}) collective-permute-start(bf16[16,64,128]{2,1,0:T(8,128)(2,1)S(1)} %share.1.refs_0_), channel_id=1, source_target_pairs={{0,2},{2,0},{1,3},{3,1},{4,6},{6,4},{5,7},{7,5},{8,10},{10,8},{9,1... | collective-permute-start | bytes 786440 | tf_op jit(solution)/shard_map/ppermute | solution.py:311
  67.0 6.4 %collective-permute-start.6 = (bf16[16,64,128]{2,1,0:T(8,128)(2,1)S(1)}, bf16[16,64,128]{2,1,0:T(8,128)(2,1)S(1)}, u32[]{:S(2)}, u32[]{:S(2)}) collective-permute-start(bf16[16,64,128]{2,1,0:T(8,128)(2,1)S(1)} %collective-permute-done.3.refs_3_), channel_id=1, source_target_pairs={{0,12},{4,0},{8,4},{12,8},{1,13},{5,1},{9,5},{13,9},{2,14},{6,2},{... | collective-permute-start | bytes 786440 | tf_op jit(solution)/shard_map/ppermute | solution.py:311
  69.4 4.8 %collective-permute-start.11 = (bf16[16,64,128]{2,1,0:T(8,128)(2,1)S(1)}, bf16[16,64,128]{2,1,0:T(8,128)(2,1)S(1)}, u32[]{:S(2)}, u32[]{:S(2)}) collective-permute-start(bf16[16,64,128]{2,1,0:T(8,128)(2,1)S(1)} %collective-permute-done.3.refs_3_), channel_id=1, source_target_pairs={{0,1},{1,0},{2,3},{3,2},{4,5},{5,4},{6,7},{7,6},{8,9},{9,8},{10,11... | collective-permute-start | bytes 786440 | tf_op jit(solution)/shard_map/ppermute | solution.py:311
  69.4 9.1 %collective-permute-start.5 = (bf16[16,64,128]{2,1,0:T(8,128)(2,1)S(1)}, bf16[16,64,128]{2,1,0:T(8,128)(2,1)S(1)}, u32[]{:S(2)}, u32[]{:S(2)}) collective-permute-start(bf16[16,64,128]{2,1,0:T(8,128)(2,1)S(1)} %collective-permute-done.3.refs_3_), channel_id=1, source_target_pairs={{0,2},{2,0},{1,3},{3,1},{4,6},{6,4},{5,7},{7,5},{8,10},{10,8},{9,1... | collective-permute-start | bytes 786440 | tf_op jit(solution)/shard_map/ppermute | solution.py:311
  71.1 7.5 %collective-permute-start.10 = (bf16[16,64,128]{2,1,0:T(8,128)(2,1)S(1)}, bf16[16,64,128]{2,1,0:T(8,128)(2,1)S(1)}, u32[]{:S(2)}, u32[]{:S(2)}) collective-permute-start(bf16[16,64,128]{2,1,0:T(8,128)(2,1)S(1)} %collective-permute-done.2.refs_2_), channel_id=1, source_target_pairs={{0,1},{1,0},{2,3},{3,2},{4,5},{5,4},{6,7},{7,6},{8,9},{9,8},{10,11... | collective-permute-start | bytes 786440 | tf_op jit(solution)/shard_map/ppermute | solution.py:311
  71.1 9.9 %collective-permute-start.4 = (bf16[16,64,128]{2,1,0:T(8,128)(2,1)S(1)}, bf16[16,64,128]{2,1,0:T(8,128)(2,1)S(1)}, u32[]{:S(2)}, u32[]{:S(2)}) collective-permute-start(bf16[16,64,128]{2,1,0:T(8,128)(2,1)S(1)} %collective-permute-done.1.refs_1_), channel_id=1, source_target_pairs={{0,4},{4,8},{8,12},{12,0},{1,5},{5,9},{9,13},{13,1},{2,6},{6,10},{... | collective-permute-start | bytes 786440 | tf_op jit(solution)/shard_map/ppermute | solution.py:311
  73.4 10.3 %collective-permute-start.7 = (bf16[16,64,128]{2,1,0:T(8,128)(2,1)S(1)}, bf16[16,64,128]{2,1,0:T(8,128)(2,1)S(1)}, u32[]{:S(2)}, u32[]{:S(2)}) collective-permute-start(bf16[16,64,128]{2,1,0:T(8,128)(2,1)S(1)} %collective-permute-done.6.refs_6_), channel_id=1, source_target_pairs={{0,2},{2,0},{1,3},{3,1},{4,6},{6,4},{5,7},{7,5},{8,10},{10,8},{9,1... | collective-permute-start | bytes 786440 | tf_op jit(solution)/shard_map/ppermute | solution.py:311
  74.2 9.6 %collective-permute-start.9 = (bf16[16,64,128]{2,1,0:T(8,128)(2,1)S(1)}, bf16[16,64,128]{2,1,0:T(8,128)(2,1)S(1)}, u32[]{:S(2)}, u32[]{:S(2)}) collective-permute-start(bf16[16,64,128]{2,1,0:T(8,128)(2,1)S(1)} %collective-permute-done.1.refs_1_), channel_id=1, source_target_pairs={{0,1},{1,0},{2,3},{3,2},{4,5},{5,4},{6,7},{7,6},{8,9},{9,8},{10,11... | collective-permute-start | bytes 786440 | tf_op jit(solution)/shard_map/ppermute | solution.py:311
  78.5 5.3 %collective-permute-start.14 = (bf16[16,64,128]{2,1,0:T(8,128)(2,1)S(1)}, bf16[16,64,128]{2,1,0:T(8,128)(2,1)S(1)}, u32[]{:S(2)}, u32[]{:S(2)}) collective-permute-start(bf16[16,64,128]{2,1,0:T(8,128)(2,1)S(1)} %collective-permute-done.6.refs_6_), channel_id=1, source_target_pairs={{0,1},{1,0},{2,3},{3,2},{4,5},{5,4},{6,7},{7,6},{8,9},{9,8},{10,11... | collective-permute-start | bytes 786440 | tf_op jit(solution)/shard_map/ppermute | solution.py:311
  78.5 5.3 %collective-permute-start.13 = (bf16[16,64,128]{2,1,0:T(8,128)(2,1)S(1)}, bf16[16,64,128]{2,1,0:T(8,128)(2,1)}, u32[]{:S(2)}, u32[]{:S(2)}) collective-permute-start(bf16[16,64,128]{2,1,0:T(8,128)(2,1)S(1)} %collective-permute-done.5.refs_5_), channel_id=1, source_target_pairs={{0,1},{1,0},{2,3},{3,2},{4,5},{5,4},{6,7},{7,6},{8,9},{9,8},{10,11... | collective-permute-start | bytes 786440 | tf_op jit(solution)/shard_map/ppermute | solution.py:311
  81.0 2.9 %collective-permute-start.12 = (bf16[16,64,128]{2,1,0:T(8,128)(2,1)S(1)}, bf16[16,64,128]{2,1,0:T(8,128)(2,1)}, u32[]{:S(2)}, u32[]{:S(2)}) collective-permute-start(bf16[16,64,128]{2,1,0:T(8,128)(2,1)S(1)} %collective-permute-done.4.refs_4_), channel_id=1, source_target_pairs={{0,1},{1,0},{2,3},{3,2},{4,5},{5,4},{6,7},{7,6},{8,9},{9,8},{10,11... | collective-permute-start | bytes 786440 | tf_op jit(solution)/shard_map/ppermute | solution.py:311
  83.8 1.7 %collective-permute-start.15 = (bf16[16,64,128]{2,1,0:T(8,128)(2,1)S(1)}, bf16[16,64,128]{2,1,0:T(8,128)(2,1)}, u32[]{:S(2)}, u32[]{:S(2)}) collective-permute-start(bf16[16,64,128]{2,1,0:T(8,128)(2,1)S(1)} %collective-permute-done.7.refs_7_), channel_id=1, source_target_pairs={{0,1},{1,0},{2,3},{3,2},{4,5},{5,4},{6,7},{7,6},{8,9},{9,8},{10,11... | collective-permute-start | bytes 786440 | tf_op jit(solution)/shard_map/ppermute | solution.py:311
  130.4 9.3 %collective-permute-start.18 = (s16[1040,128]{1,0:T(8,128)(2,1)S(1)}, s16[1040,128]{1,0:T(8,128)(2,1)S(1)}, u32[]{:S(2)}, u32[]{:S(2)}) collective-permute-start(s16[1040,128]{1,0:T(8,128)(2,1)S(1)} %bitcast.32), channel_id=1, source_target_pairs={{0,48},{16,0},{32,16},{48,32},{1,49},{17,1},{33,17},{49,33},{2,50}... | collective-permute-start | bytes 798728 | tf_op jit(solution)/shard_map/ppermute | solution.py:311
  131.6 11.1 %collective-permute-start.16 = (s16[1040,128]{1,0:T(8,128)(2,1)S(1)}, s16[1040,128]{1,0:T(8,128)(2,1)S(1)}, u32[]{:S(2)}, u32[]{:S(2)}) collective-permute-start(s16[1040,128]{1,0:T(8,128)(2,1)S(1)} %bitcast.33), channel_id=1, source_target_pairs={{0,64},{64,0},{1,65},{65,1},{2,66},{66,2},{3,67},{67,3},{4,68},{68... | collective-permute-start | bytes 798728 | tf_op jit(solution)/shard_map/ppermute | solution.py:311
  139.7 8.4 %collective-permute-start.21 = (s16[1040,128]{1,0:T(8,128)(2,1)S(1)}, s16[1040,128]{1,0:T(8,128)(2,1)S(1)}, u32[]{:S(2)}, u32[]{:S(2)}) collective-permute-start(s16[1040,128]{1,0:T(8,128)(2,1)S(1)} %collective-permute-done.18.refs_3_), channel_id=1, source_target_pairs={{0,48},{16,0},{32,16},{48,32},{1,49},{17,1},{33,17},{49,33},{2,50}... | collective-permute-start | bytes 798728 | tf_op jit(solution)/shard_map/ppermute | solution.py:311
  142.1 10.5 %collective-permute-start.17 = (s16[1040,128]{1,0:T(8,128)(2,1)S(1)}, s16[1040,128]{1,0:T(8,128)(2,1)S(1)}, u32[]{:S(2)}, u32[]{:S(2)}) collective-permute-start(s16[1040,128]{1,0:T(8,128)(2,1)S(1)} %bitcast.34), channel_id=1, source_target_pairs={{0,16},{16,32},{32,48},{48,0},{1,17},{17,33},{33,49},{49,1},{2,18}... | collective-permute-start | bytes 798728 | tf_op jit(solution)/shard_map/ppermute | solution.py:311
  142.1 10.5 %collective-permute-start.20 = (s16[1040,128]{1,0:T(8,128)(2,1)S(1)}, s16[1040,128]{1,0:T(8,128)(2,1)S(1)}, u32[]{:S(2)}, u32[]{:S(2)}) collective-permute-start(s16[1040,128]{1,0:T(8,128)(2,1)S(1)} %collective-permute-done.18.refs_3_), channel_id=1, source_target_pairs={{0,64},{64,0},{1,65},{65,1},{2,66},{66,2},{3,67},{67,3},{4,68},{68... | collective-permute-start | bytes 798728 | tf_op jit(solution)/shard_map/ppermute | solution.py:311
  142.8 14.4 %collective-permute-start.19 = (s16[1040,128]{1,0:T(8,128)(2,1)S(1)}, s16[1040,128]{1,0:T(8,128)(2,1)S(1)}, u32[]{:S(2)}, u32[]{:S(2)}) collective-permute-start(s16[1040,128]{1,0:T(8,128)(2,1)S(1)} %collective-permute-done.16.refs_1_), channel_id=1, source_target_pairs={{0,16},{16,32},{32,48},{48,0},{1,17},{17,33},{33,49},{49,1},{2,18}... | collective-permute-start | bytes 798728 | tf_op jit(solution)/shard_map/ppermute | solution.py:311
  148.1 9.3 %collective-permute-start.22 = (s16[1040,128]{1,0:T(8,128)(2,1)S(1)}, s16[1040,128]{1,0:T(8,128)(2,1)S(1)}, u32[]{:S(2)}, u32[]{:S(2)}) collective-permute-start(s16[1040,128]{1,0:T(8,128)(2,1)S(1)} %collective-permute-done.21.refs_6_), channel_id=1, source_target_pairs={{0,64},{64,0},{1,65},{65,1},{2,66},{66,2},{3,67},{67,3},{4,68},{68... | collective-permute-start | bytes 798728 | tf_op jit(solution)/shard_map/ppermute | solution.py:311

commit v3 on v2

v3 whole, which is shorter than its diff:
```python
import functools

import jax
import jax.numpy as jnp
from jax import lax
from jax.experimental import pallas as pl
from jax.experimental.pallas import tpu as pltpu
from jax.sharding import Mesh
from jax.sharding import PartitionSpec as P

TILE = 128
CHUNK = 64
UNROLL = 64
LAG = 8
BLOCKS = 32
LEVEL = 32700.0
STEPS = 8.0
MIB = 1024 * 1024
ROW = ("yh", "z")
CHIPS = ("x", "yl")
HOPS = [(0, 0), (0, 1), (-1, 0), (1, 0), (-1, 1), (1, 1), (2, 0), (2, 1)]
SENT = (2, 4, 5, 7)
KEPT = (0, 1, 3, 6)
EARLY = (0, 1, 2, 3)
LATE = (4, 5, 6, 7)
PLACES = 2
LINES = PLACES + len(HOPS)
F32 = jnp.float32
I16 = jnp.int16


def params(mib):
    return pltpu.CompilerParams(vmem_limit_bytes=mib * MIB)


def code(block):
    top = jnp.maximum(jnp.max(jnp.abs(block), axis=0, keepdims=True), 1e-30)
    step = jnp.ceil(jnp.log2(top) * STEPS)
    return step, jnp.exp2(step * (-1.0 / STEPS)) * LEVEL


def factor(step):
    return jnp.exp2(step * (1.0 / STEPS)) * (1.0 / LEVEL)


def put_blocks(read, count, out_ref, steps):
    rows = out_ref.shape[0] - count
    width = rows // count
    unroll = min(BLOCKS, count)

    def body(i, _):
        for u in range(unroll):
            j = i * unroll + u
            block = read(j)
            step, gain = code(block)
            whole = jnp.round(block * gain).astype(jnp.int32)
            out_ref[pl.ds(pl.multiple_of(j * width, width), width), :] = whole.astype(I16)
            steps[pl.ds(j, 1), :] = step
        return 0

    lax.fori_loop(0, count // unroll, body, 0)
    out_ref[rows:, :] = steps[:count].astype(jnp.int32).astype(I16)


def sparse_step(transposed, coords, base, source, tiles_ref, acc):
    def body(i, _):
        waiting = []
        for u in range(UNROLL + LAG):
            if u < UNROLL:
                slot = base + i * UNROLL + u
                r, c = coords[0, slot], coords[1, slot]
                if transposed:
                    left = source[:, pl.ds(pl.multiple_of(c * TILE, TILE), TILE)]
                    dims = (((1,), (1,)), ((), ()))
                    value = lax.dot_general(tiles_ref[slot], left, dims, preferred_element_type=F32)
                    waiting.append((r, value))
                else:
                    value = jnp.dot(source[r], tiles_ref[slot], preferred_element_type=F32)
                    waiting.append((c, value))
            if u >= LAG:
                target, value = waiting[u - LAG]
                acc[target] += value
        return 0

    lax.fori_loop(0, CHUNK // UNROLL, body, 0)


def fetch(count, tiles_ref, tiles, sem):
    def part(j):
        rows = pl.ds(j * CHUNK, CHUNK)
        return pltpu.make_async_copy(tiles_ref.at[rows], tiles.at[rows], sem.at[j])

    chunks = lax.div(count + (CHUNK - 1), CHUNK)
    lax.fori_loop(0, chunks, lambda j, _: (part(j).start(), 0)[1], 0)
    return chunks, part


def forward_kernel(coords, info, omega_ref, tiles_ref, keep_ref, give_ref, acc, omega, tiles, coded, steps, tile_sem, sem):
    half = acc.shape[0] // 2
    load = pltpu.make_async_copy(omega_ref, omega, sem.at[0])
    load.start()
    chunks, part = fetch(info[0], tiles_ref, tiles, tile_sem)
    acc[...] = jnp.zeros_like(acc)
    load.wait()

    def chunk(j, _):
        part(j).wait()
        sparse_step(True, coords, j * CHUNK, omega, tiles, acc)
        return 0

    lax.fori_loop(0, chunks, chunk, 0)
    core = info[1]
    stores = []
    for n, (out_ref, first) in enumerate(((give_ref, (1 - core) * half), (keep_ref, core * half))):
        put_blocks(lambda j: acc[first + j].T, half, coded.at[n], steps)
        stores.append(pltpu.make_async_copy(coded.at[n], out_ref, sem.at[1 + n]))
        stores[-1].start()
    for store in stores:
        store.wait()


def forward(tiles, coords, info, omega, blk_row):
    slots = tiles.shape[0]
    width = omega.shape[0]
    half = blk_row // 2
    coded = jax.ShapeDtypeStruct((half * (width + 1), TILE), I16)
    return pl.pallas_call(
        forward_kernel,
        out_shape=(coded, coded),
        in_specs=[pl.BlockSpec(memory_space=pltpu.SMEM)] * 2 + [pl.BlockSpec(memory_space=pltpu.HBM)] * 2,
        out_specs=[pl.BlockSpec(memory_space=pltpu.HBM)] * 2,
        scratch_shapes=[
            pltpu.VMEM((blk_row, TILE, width), F32),
            pltpu.VMEM(omega.shape, omega.dtype),
            pltpu.VMEM(tiles.shape, tiles.dtype),
            pltpu.VMEM((2, *coded.shape), I16),
            pltpu.VMEM((half, TILE), F32),
            pltpu.SemaphoreType.DMA((slots // CHUNK,)),
            pltpu.SemaphoreType.DMA((3,)),
        ],
        compiler_params=params(60),
        name="forward",
    )(coords, info, omega, tiles)


def plain_kernel(in_ref, out_ref, scale):
    blocks, width, _ = out_ref.shape
    scales((in_ref,), scale, blocks * width)

    def body(j, _):
        part = in_ref[pl.ds(pl.multiple_of(j * width, width), width), :].astype(jnp.int32).astype(F32)
        out_ref[j] = part * scale[0, pl.ds(j, 1), :]
        return 0

    lax.fori_loop(0, blocks, body, 0, unroll=8)


def plain(coded, width):
    blocks = coded.shape[0] // (width + 1)
    return pl.pallas_call(
        plain_kernel,
        out_shape=jax.ShapeDtypeStruct((blocks, width, TILE), F32),
        in_specs=[pl.BlockSpec(memory_space=pltpu.VMEM)],
        out_specs=pl.BlockSpec(memory_space=pltpu.VMEM),
        scratch_shapes=[pltpu.VMEM((1, blocks, TILE), F32)],
        compiler_params=params(14),
        name="plain",
    )(coded)


def pair_kernel(which, sent, info, keep_ref, got_ref, *refs):
    outs, (scale, steps) = refs[:-2], refs[-2:]
    blocks, width, _ = keep_ref.shape
    each = blocks // len(HOPS)
    scales((got_ref,), scale, blocks * width)
    for n, out_ref in zip(which, outs):
        first = info[PLACES + n] * each

        def read(j):
            b = first + j
            got = got_ref[pl.ds(pl.multiple_of(b * width, width), width), :].astype(jnp.int32).astype(F32)
            return keep_ref[b] + got * scale[0, pl.ds(b, 1), :]

        if sent:
            put_blocks(read, each, out_ref, steps)
        else:

            def body(j, _):
                out_ref[j] = read(j)
                return 0

            lax.fori_loop(0, each, body, 0, unroll=8)


def pair(info, keep, got, which, sent):
    blocks, width, _ = keep.shape
    each = blocks // len(HOPS)
    coded = jax.ShapeDtypeStruct((each * width + each, TILE), I16)
    return pl.pallas_call(
        functools.partial(pair_kernel, which, sent),
        out_shape=[coded if sent else jax.ShapeDtypeStruct((each, width, TILE), F32)] * len(which),
        in_specs=[pl.BlockSpec(memory_space=s) for s in (pltpu.SMEM, pltpu.VMEM, pltpu.VMEM)],
        out_specs=[pl.BlockSpec(memory_space=pltpu.VMEM)] * len(which),
        scratch_shapes=[pltpu.VMEM((1, blocks, TILE), F32), pltpu.VMEM((each, TILE), F32)],
        compiler_params=params(14),
        name="pair",
    )(info, keep, got)


def scales(parts, scale, rows):
    for n, ref in enumerate(parts):
        scale[n] = factor(ref[rows:, :].astype(jnp.int32).astype(F32))


def gather_sum(own_ref, parts, scale, j, width):
    total = own_ref[j]
    for n, ref in enumerate(parts):
        part = ref[pl.ds(pl.multiple_of(j * width, width), width), :].astype(jnp.int32).astype(F32)
        total = total + part * scale[n, pl.ds(j, 1), :]
    return total


def share_kernel(own_ref, *refs):
    parts, (out_ref, scale) = refs[:-2], refs[-2:]
    each, width, _ = own_ref.shape
    scales(parts, scale, each * width)

    def body(j, _):
        out_ref[j] = gather_sum(own_ref, parts, scale, j, width).astype(out_ref.dtype)
        return 0

    lax.fori_loop(0, each, body, 0, unroll=8)


def share(own, parts):
    each = own.shape[0]
    return pl.pallas_call(
        share_kernel,
        out_shape=jax.ShapeDtypeStruct(own.shape, jnp.bfloat16),
        scratch_shapes=[pltpu.VMEM((len(parts), each, TILE), F32)],
        compiler_params=params(12),
        name="share",
    )(own, *parts)


def merge_kernel(own_ref, *refs):
    parts, (out_ref, scale, steps) = refs[:-3], refs[-3:]
    each, width, _ = own_ref.shape
    scales(parts, scale, each * width)
    put_blocks(lambda j: gather_sum(own_ref, parts, scale, j, width), each, out_ref, steps)


def merge(own, parts):
    each = own.shape[0]
    return pl.pallas_call(
        merge_kernel,
        out_shape=jax.ShapeDtypeStruct(parts[0].shape, I16),
        scratch_shapes=[pltpu.VMEM((len(parts), each, TILE), F32), pltpu.VMEM((each, TILE), F32)],
        compiler_params=params(12),
        name="merge",
    )(own, *parts)


def backward_kernel(coords, info, *refs):
    acc, inner, tiles, steps, tile_sem, sem, out_sem = refs[-7:]
    count = inner.shape[0] // refs[0].shape[0]
    shares, tiles_ref, outs = refs[:count], refs[count], refs[count + 1 : -7]
    each = acc.shape[0] // len(outs)
    size = shares[0].shape[0]
    core = info[1]
    loads = []
    for n, ref in enumerate(shares):
        half = core if n < len(HOPS) else 1 - core
        place = half * len(HOPS) + info[PLACES + n % len(HOPS)]
        loads.append(pltpu.make_async_copy(ref, inner.at[pl.ds(place * size, size)], sem.at[n]))
        loads[-1].start()
    chunks, part = fetch(info[0], tiles_ref, tiles, tile_sem)
    acc[...] = jnp.zeros_like(acc)
    for load in loads:
        load.wait()

    def chunk(j, _):
        part(j).wait()
        sparse_step(False, coords, j * CHUNK, inner, tiles, acc)
        return 0

    lax.fori_loop(0, chunks, chunk, 0)
    stores = []
    for n, out_ref in zip(KEPT, outs[len(SENT) :]):
        first = info[LINES + n] * each
        stores.append(pltpu.make_async_copy(acc.at[pl.ds(first, each)], out_ref, out_sem.at[len(stores)]))
        stores[-1].start()
    for n, out_ref in zip(SENT, outs):
        first = info[LINES + n] * each
        put_blocks(lambda j: acc[first + j], each, out_ref, steps)
    for store in stores:
        store.wait()


def backward(tiles, coords, info, shares, blk_col):
    slots = tiles.shape[0]
    size, width, _ = shares[0].shape
    each = blk_col // len(HOPS)
    coded = jax.ShapeDtypeStruct((each * width + each, TILE), I16)
    plain = jax.ShapeDtypeStruct((each, width, TILE), F32)
    return pl.pallas_call(
        backward_kernel,
        out_shape=[coded] * len(SENT) + [plain] * len(KEPT),
        in_specs=[pl.BlockSpec(memory_space=pltpu.SMEM)] * 2 + [pl.BlockSpec(memory_space=pl.ANY)] * len(shares) + [pl.BlockSpec(memory_space=pltpu.HBM)],
        out_specs=[pl.BlockSpec(memory_space=pltpu.VMEM)] * len(SENT) + [pl.BlockSpec(memory_space=pl.ANY)] * len(KEPT),
        scratch_shapes=[
            pltpu.VMEM((blk_col, width, TILE), F32),
            pltpu.VMEM((len(shares) * size, width, TILE), jnp.bfloat16),
            pltpu.VMEM(tiles.shape, tiles.dtype),
            pltpu.VMEM((each, TILE), F32),
            pltpu.SemaphoreType.DMA((slots // CHUNK,)),
            pltpu.SemaphoreType.DMA((len(shares),)),
            pltpu.SemaphoreType.DMA((len(KEPT),)),
        ],
        compiler_params=params(40),
        name="backward",
    )(coords, info, *shares, tiles)


def spread_kernel(which, info, *refs):
    parts, (out_ref, scale, buffer, sem) = refs[: len(which)], refs[-4:]
    each = scale.shape[0]
    width = buffer.shape[1]
    size = each * TILE
    stores = []
    for k, (n, ref) in enumerate(zip(which, parts)):
        scale[...] = factor(ref[each * width :, :].astype(jnp.int32).astype(F32))
        for j in range(each):
            part = ref[j * width : (j + 1) * width, :].astype(jnp.int32).astype(F32)
            buffer[k, :, j * TILE : (j + 1) * TILE] = part * scale[j : j + 1, :]
        columns = pl.ds(pl.multiple_of(info[LINES + n] * size, size), size)
        stores.append(pltpu.make_async_copy(buffer.at[k], out_ref.at[:, columns], sem.at[k]))
        stores[-1].start()
    for store in stores:
        store.wait()


def spread(info, parts, width, which, out=None):
    rows = parts[0].shape[0]
    each = rows // (width + 1)
    vmem, hbm = pl.BlockSpec(memory_space=pltpu.VMEM), pl.BlockSpec(memory_space=pl.ANY)
    given = [] if out is None else [out]
    return pl.pallas_call(
        functools.partial(spread_kernel, which),
        out_shape=jax.ShapeDtypeStruct((width, len(HOPS) * each * TILE), F32),
        in_specs=[pl.BlockSpec(memory_space=pltpu.SMEM)] + [vmem] * len(which) + [hbm] * len(given),
        out_specs=hbm,
        scratch_shapes=[
            pltpu.VMEM((each, TILE), F32),
            pltpu.VMEM((len(which), width, each * TILE), F32),
            pltpu.SemaphoreType.DMA((len(which),)),
        ],
        input_output_aliases={1 + len(which): 0} if given else {},
        compiler_params=params(16),
        name="spread",
    )(info, *[parts[n] for n in which], *given)


def shift(value, axis, by):
    count = lax.axis_size(axis)
    return lax.ppermute(value, axis, [(i, (i + by) % count) for i in range(count)])


def gather(value, ring, pair, direct):
    across = shift(value, pair, 1)
    up = shift(value, ring, 1)
    down = shift(value, ring, -1)
    down_across = shift(down, pair, 1)
    up_across = shift(across, ring, 1)
    far = shift(value, ring, 2) if direct else shift(down, ring, -1)
    far_across = shift(far, pair, 1)
    return [value, across, up, down, up_across, down_across, far, far_across]


def numbers(ring, pair):
    i, j = lax.axis_index(ring), lax.axis_index(pair)
    return [lax.rem(i + a + 4, 4) * 2 + lax.rem(j + b, 2) for a, b in HOPS]


def scatter(sent, kept, ring, pair, last):
    down, down_across, up_across, far_across = sent
    own, across, up, far = kept
    far_across = shift(far_across, pair, 1)
    up_across = shift(up_across, pair, 1)
    down_across = shift(down_across, ring, -1)
    down = shift(down, ring, -1)
    far = shift(merge(far, [far_across]), ring, 2)
    up = shift(merge(up, [up_across]), ring, 1)
    across = shift(merge(across, [down_across]), pair, 1)
    return last(own, [down, across, up, far])


def shards(tiles, tile_coords, tile_counts, omega):
    blocks = tiles[0, 0]
    coords = tile_coords[0, 0].T
    core = lax.axis_index("core")
    width = omega.shape[0]
    blk_col = omega.shape[1] // TILE
    rows = lax.axis_size(ROW)
    chips = lax.axis_size(CHIPS)
    blk_row = blk_col * 2 * chips // rows
    lines = [lax.rem(p, 2) * 4 + lax.div(p, 2) for p in numbers("z", "yh")]
    info = jnp.stack([tile_counts[0, 0], core, *numbers(*CHIPS), *lines])
    keep, give = forward(blocks, coords, info, omega, blk_row)
    got = shift(give, "core", 1)
    keep = plain(keep, width)
    sent = pair(info, keep, got, SENT, True)
    kept = pair(info, keep, got, KEPT, False)
    mine = gather(scatter(sent, kept, *CHIPS, share), *CHIPS, False)
    theirs = [shift(value, "core", 1) for value in mine]
    out = backward(blocks, coords, info, mine + theirs, blk_col)
    parts = gather(scatter(out[: len(SENT)], out[len(SENT) :], "z", "yh", merge), "z", "yh", True)
    return spread(info, parts, width, LATE, spread(info, parts, width, EARLY))


def solution(mesh):
    fine = Mesh(mesh.devices.reshape(2, 4, 4, 2, 2), ("yh", "z", "x", "yl", "core"))
    col = ("x", "yl", "core")
    return jax.shard_map(
        shards,
        mesh=fine,
        in_specs=(
            P(ROW, col, None, None, None),
            P(ROW, col, None, None),
            P(ROW, col),
            P(None, col),
        ),
        out_specs=P(None, col),
        check_vma=False,
    )
```

time: 160 us -> 138 us (0.86)
  blocking collectives: 67.3 us -> 0 us
  starting transfers between devices: 13.5 us -> 44 us
  waiting for transfers between devices: 43.1 us -> 56.7 us
    all_to_all x2 -> x0, blocking collectives: 67.3 us -> none  [the longest x1 34.4 us: shards(): parts = lax.all_to_all(out, ROW, 0, 0, tiled=True)]
    ppermute x23 -> x37, starting transfers between devices: 13.5 us -> 44 us  [shift(): lax.ppermute(value, axis, [(i, (i + by) % count) for i in range(count)])]
    ppermute x23 -> x37, waiting for transfers between devices: 43.1 us -> 56.7 us  [shift(): lax.ppermute(value, axis, [(i, (i + by) % count) for i in range(count)])]
    pallas_call x6 -> x15, Pallas kernels: 32.5 us -> 32.7 us  [the longest x1 15.5 us: forward(): pl.pallas_call(forward_kernel, out_shape=(coded, coded), in_specs=[pl.Blo...]
  transfers between devices with their start and end apart: 23 -> 37, of which waited for: 13 -> 23; matrix products, arithmetic and copies ran while one was open for 0% -> 0% of each run, Pallas kernels for 0% -> 3%
where the time goes in v3:
time: 138 us; the launch traced here: 137 us
  waiting for transfers between devices  56.7 us (41%)
  starting transfers between devices  44 us (32%)
  Pallas kernels  32.7 us (24%)
  local copies, waits for them, and re-layouts  2.19 us (2%)
    ppermute x37, waiting for transfers between devices, shift(): lax.ppermute(value, axis, [(i, (i + by) % count) for i in range(count)])  56.7 us
    ppermute x37, starting transfers between devices, shift(): lax.ppermute(value, axis, [(i, (i + by) % count) for i in range(count)])  44 us
    pallas_call x1, Pallas kernels, forward(): pl.pallas_call(forward_kernel, out_shape=(coded, coded), in_specs=[pl.Blo...  15.5 us
    pallas_call x1, Pallas kernels, backward(): pl.pallas_call(backward_kernel, out_shape=[coded] * len(SENT) + [plain] *...  8.87 us
    pallas_call x2, Pallas kernels, spread(): pl.pallas_call(functools.partial(spread_kernel, which), out_shape=jax.Sha...  3.88 us
  transfers between devices with their start and end apart: 37, of which 23 were waited for; matrix products, arithmetic and copies ran while one was open for 0% of the time, Pallas kernels for 3%

profile of v3, /device:TPU:0, one launch (start us, length us, event | category | flops | bytes accessed | tf_op | source)
XLA Modules:
  0.0 136.6 jit_solution(14732033631275059413)
XLA Ops:
  0.7 0.6 stack.71.info
  1.2 15.5 %forward.1 = (s16[8320,128]{1,0:T(8,128)(2,1)}, s16[8320,128]{1,0:T(8,128)(2,1)}) custom-call(s32[2,512]{1,0:T(2,128)} %bitcast.23, s32[18]{0:T(128)} %stack.71.info, bf16[64,16384]{1,0:T(8,128)(2,1)} %omega_ref.1, bf16[512,128,128]{2,1,0:T(8,128)(2,1)} %bitcast.25), custom_call_target="tpu_custom_call" | custom-call | tf_op jit(solution)/shard_map/forward/pallas_call | solution.py:127
  16.8 1.6 %copy-done = s16[8320,128]{1,0:T(8,128)(2,1)S(1)} copy-done((s16[8320,128]{1,0:T(8,128)(2,1)S(1)}, s16[8320,128]{1,0:T(8,128)(2,1)}, u32[]{:S(2)}) %copy-start) | copy-done | bytes 2129944
  18.4 0.5 plain.1.keep_ref
  18.9 2.3 %collective-permute-done.got_ref = s16[8320,128]{1,0:T(8,128)(2,1)S(1)} collective-permute-done((s16[8320,128]{1,0:T(8,128)(2,1)}, s16[8320,128]{1,0:T(8,128)(2,1)S(1)}, u32[]{:S(2)}, u32[]{:S(2)}) %collective-permute-start) | collective-permute-done | bytes 2129952 | tf_op jit(solution)/shard_map/ppermute | solution.py:366
  21.2 1.2 pair.3
  22.5 3.9 %collective-permute-start.4 = (s16[1040,128]{1,0:T(8,128)(2,1)S(1)}, s16[1040,128]{1,0:T(8,128)(2,1)S(1)}, u32[]{:S(2)}, u32[]{:S(2)}) collective-permute-start(s16[1040,128]{1,0:T(8,128)(2,1)S(1)} %get-tuple-element.30), channel_id=1, source_target_pairs={{0,2},{2,0},{1,3},{3,1},{4,6},{6,4},{5,7},{7,5},{8,10},{10,8},{9,1... | collective-permute-start | bytes 798728 | tf_op jit(solution)/shard_map/ppermute | solution.py:366
  26.5 1.4 collective-permute-start.1
  27.8 0.9 pair.2
  28.7 3.1 %collective-permute-done.2.refs_0_ = s16[1040,128]{1,0:T(8,128)(2,1)S(1)} collective-permute-done((s16[1040,128]{1,0:T(8,128)(2,1)S(1)}, s16[1040,128]{1,0:T(8,128)(2,1)S(1)}, u32[]{:S(2)}, u32[]{:S(2)}) %collective-permute-start.2) | collective-permute-done | bytes 266272 | tf_op jit(solution)/shard_map/ppermute | solution.py:366
  31.8 0.2 merge.7
  31.9 1.5 %collective-permute-start.3 = (s16[1040,128]{1,0:T(8,128)(2,1)S(1)}, s16[1040,128]{1,0:T(8,128)(2,1)S(1)}, u32[]{:S(2)}, u32[]{:S(2)}) collective-permute-start(s16[1040,128]{1,0:T(8,128)(2,1)S(1)} %merge.7), channel_id=1, source_target_pairs={{0,2},{2,0},{1,3},{3,1},{4,6},{6,4},{5,7},{7,5},{8,10},{10,8},{9,1... | collective-permute-start | bytes 798728 | tf_op jit(solution)/shard_map/ppermute | solution.py:366
  33.4 0.2 collective-permute-done.4.refs_0_
  33.6 0.2 merge.8
  33.8 1.1 collective-permute-start.5
  34.9 4.4 %collective-permute-done.6.refs_0_ = s16[1040,128]{1,0:T(8,128)(2,1)S(1)} collective-permute-done((s16[1040,128]{1,0:T(8,128)(2,1)S(1)}, s16[1040,128]{1,0:T(8,128)(2,1)S(1)}, u32[]{:S(2)}, u32[]{:S(2)}) %collective-permute-start.6) | collective-permute-done | bytes 266272 | tf_op jit(solution)/shard_map/ppermute | solution.py:366
  39.3 0.2 merge.9
  39.5 1.3 collective-permute-start.7
  40.9 3.6 %collective-permute-done.3.refs_1_ = s16[1040,128]{1,0:T(8,128)(2,1)S(1)} collective-permute-done((s16[1040,128]{1,0:T(8,128)(2,1)S(1)}, s16[1040,128]{1,0:T(8,128)(2,1)S(1)}, u32[]{:S(2)}, u32[]{:S(2)}) %collective-permute-start.3) | collective-permute-done | bytes 266272 | tf_op jit(solution)/shard_map/ppermute | solution.py:366
  44.5 5.1 %collective-permute-done.7.refs_3_ = s16[1040,128]{1,0:T(8,128)(2,1)S(1)} collective-permute-done((s16[1040,128]{1,0:T(8,128)(2,1)S(1)}, s16[1040,128]{1,0:T(8,128)(2,1)S(1)}, u32[]{:S(2)}, u32[]{:S(2)}) %collective-permute-start.7) | collective-permute-done | bytes 266272 | tf_op jit(solution)/shard_map/ppermute | solution.py:366
  49.6 0.3 share.1.refs_0_
  50.0 0.1 collective-permute-start.15
  50.1 1.9 %collective-permute-start.9 = (bf16[16,64,128]{2,1,0:T(8,128)(2,1)S(1)}, bf16[16,64,128]{2,1,0:T(8,128)(2,1)S(1)}, u32[]{:S(2)}, u32[]{:S(2)}) collective-permute-start(bf16[16,64,128]{2,1,0:T(8,128)(2,1)S(1)} %share.1.refs_0_), channel_id=1, source_target_pairs={{0,4},{4,8},{8,12},{12,0},{1,5},{5,9},{9,13},{13,1},{2,6},{6,10},{... | collective-permute-start | bytes 786440 | tf_op jit(solution)/shard_map/ppermute | solution.py:366
  52.0 0.3 collective-permute-start.8
  52.3 4.9 %collective-permute-done.10.refs_3_ = bf16[16,64,128]{2,1,0:T(8,128)(2,1)S(1)} collective-permute-done((bf16[16,64,128]{2,1,0:T(8,128)(2,1)S(1)}, bf16[16,64,128]{2,1,0:T(8,128)(2,1)S(1)}, u32[]{:S(2)}, u32[]{:S(2)}) %collective-permute-start.10) | collective-permute-done | bytes 262176 | tf_op jit(solution)/shard_map/ppermute | solution.py:366
  57.2 1.5 %collective-permute-start.13 = (bf16[16,64,128]{2,1,0:T(8,128)(2,1)S(1)}, bf16[16,64,128]{2,1,0:T(8,128)(2,1)S(1)}, u32[]{:S(2)}, u32[]{:S(2)}) collective-permute-start(bf16[16,64,128]{2,1,0:T(8,128)(2,1)S(1)} %collective-permute-done.10.refs_3_), channel_id=1, source_target_pairs={{0,12},{4,0},{8,4},{12,8},{1,13},{5,1},{9,5},{13,9},{2,14},{6,2},{... | collective-permute-start | bytes 786440 | tf_op jit(solution)/shard_map/ppermute | solution.py:366
  58.7 0.3 collective-permute-start.12
  58.9 1.0 collective-permute-done.9.refs_2_
  60.0 0.4 collective-permute-done.8.refs_1_
  60.4 0.3 collective-permute-start.11
  60.7 2.9 %collective-permute-done.13.refs_6_ = bf16[16,64,128]{2,1,0:T(8,128)(2,1)S(1)} collective-permute-done((bf16[16,64,128]{2,1,0:T(8,128)(2,1)S(1)}, bf16[16,64,128]{2,1,0:T(8,128)(2,1)S(1)}, u32[]{:S(2)}, u32[]{:S(2)}) %collective-permute-start.13) | collective-permute-done | bytes 262176 | tf_op jit(solution)/shard_map/ppermute | solution.py:366
  63.6 4.2 %collective-permute-done.12.refs_5_ = bf16[16,64,128]{2,1,0:T(8,128)(2,1)S(1)} collective-permute-done((bf16[16,64,128]{2,1,0:T(8,128)(2,1)S(1)}, bf16[16,64,128]{2,1,0:T(8,128)(2,1)S(1)}, u32[]{:S(2)}, u32[]{:S(2)}) %collective-permute-start.12) | collective-permute-done | bytes 262176 | tf_op jit(solution)/shard_map/ppermute | solution.py:366
  67.8 0.5 collective-permute-start.20
  68.3 1.6 %collective-permute-done.11.refs_4_ = bf16[16,64,128]{2,1,0:T(8,128)(2,1)S(1)} collective-permute-done((bf16[16,64,128]{2,1,0:T(8,128)(2,1)S(1)}, bf16[16,64,128]{2,1,0:T(8,128)(2,1)S(1)}, u32[]{:S(2)}, u32[]{:S(2)}) %collective-permute-start.11) | collective-permute-done | bytes 262176 | tf_op jit(solution)/shard_map/ppermute | solution.py:366
  69.9 3.1 %collective-permute-done.14.refs_7_ = bf16[16,64,128]{2,1,0:T(8,128)(2,1)S(1)} collective-permute-done((bf16[16,64,128]{2,1,0:T(8,128)(2,1)S(1)}, bf16[16,64,128]{2,1,0:T(8,128)(2,1)S(1)}, u32[]{:S(2)}, u32[]{:S(2)}) %collective-permute-start.14) | collective-permute-done | bytes 262176 | tf_op jit(solution)/shard_map/ppermute | solution.py:366
  73.1 1.5 %collective-permute-done.22.refs_15_ = bf16[16,64,128]{2,1,0:T(8,128)(2,1)S(1)} collective-permute-done((bf16[16,64,128]{2,1,0:T(8,128)(2,1)S(1)}, bf16[16,64,128]{2,1,0:T(8,128)(2,1)S(1)}, u32[]{:S(2)}, u32[]{:S(2)}) %collective-permute-start.22) | collective-permute-done | bytes 262176 | tf_op jit(solution)/shard_map/ppermute | solution.py:366
  74.6 8.9 %backward.1 = (s16[1040,128]{1,0:T(8,128)(2,1)S(1)}, s16[1040,128]{1,0:T(8,128)(2,1)S(1)}, s16[1040,128]{1,0:T(8,128)(2,1)S(1)}, s16[1040,128]{1,0:T(8,128)(2,1)...) custom-call(s32[2,512]{1,0:T(2,128)S(1)} %bitcast.24, ...), custom_call_target="tpu_custom_call" | custom-call | tf_op jit(solution)/shard_map/backward/pallas_call | solution.py:306
  83.5 3.0 %collective-permute-start.26 = (s16[1040,128]{1,0:T(8,128)(2,1)S(1)}, s16[1040,128]{1,0:T(8,128)(2,1)S(1)}, u32[]{:S(2)}, u32[]{:S(2)}) collective-permute-start(s16[1040,128]{1,0:T(8,128)(2,1)S(1)} %get-tuple-element.38), channel_id=1, source_target_pairs={{0,64},{64,0},{1,65},{65,1},{2,66},{66,2},{3,67},{67,3},{4,68},{68... | collective-permute-start | bytes 798728 | tf_op jit(solution)/shard_map/ppermute | solution.py:366
  86.6 0.6 collective-permute-start.28
  87.1 4.2 %collective-permute-start.23 = (s16[1040,128]{1,0:T(8,128)(2,1)S(1)}, s16[1040,128]{1,0:T(8,128)(2,1)S(1)}, u32[]{:S(2)}, u32[]{:S(2)}) collective-permute-start(s16[1040,128]{1,0:T(8,128)(2,1)S(1)} %get-tuple-element.34), channel_id=1, source_target_pairs={{0,48},{16,0},{32,16},{48,32},{1,49},{17,1},{33,17},{49,33},{2,50}... | collective-permute-start | bytes 798728 | tf_op jit(solution)/shard_map/ppermute | solution.py:366
  91.3 1.4 %collective-permute-done.24.refs_0_ = s16[1040,128]{1,0:T(8,128)(2,1)S(1)} collective-permute-done((s16[1040,128]{1,0:T(8,128)(2,1)S(1)}, s16[1040,128]{1,0:T(8,128)(2,1)S(1)}, u32[]{:S(2)}, u32[]{:S(2)}) %collective-permute-start.24) | collective-permute-done | bytes 266272 | tf_op jit(solution)/shard_map/ppermute | solution.py:366
  92.7 0.2 merge.10
  92.9 0.6 collective-permute-start.25
  93.6 0.8 collective-permute-done.26.refs_0_
  94.3 0.2 merge.11
  94.5 2.0 %collective-permute-start.27 = (s16[1040,128]{1,0:T(8,128)(2,1)S(1)}, s16[1040,128]{1,0:T(8,128)(2,1)S(1)}, u32[]{:S(2)}, u32[]{:S(2)}) collective-permute-start(s16[1040,128]{1,0:T(8,128)(2,1)S(1)} %merge.11), channel_id=1, source_target_pairs={{0,16},{16,32},{32,48},{48,0},{1,17},{17,33},{33,49},{49,1},{2,18}... | collective-permute-start | bytes 798728 | tf_op jit(solution)/shard_map/ppermute | solution.py:366
  96.6 3.5 %collective-permute-done.28.refs_0_ = s16[1040,128]{1,0:T(8,128)(2,1)S(1)} collective-permute-done((s16[1040,128]{1,0:T(8,128)(2,1)S(1)}, s16[1040,128]{1,0:T(8,128)(2,1)S(1)}, u32[]{:S(2)}, u32[]{:S(2)}) %collective-permute-start.28) | collective-permute-done | bytes 266272 | tf_op jit(solution)/shard_map/ppermute | solution.py:366
  100.0 0.2 merge.12
  100.2 3.9 %collective-permute-start.29 = (s16[1040,128]{1,0:T(8,128)(2,1)S(1)}, s16[1040,128]{1,0:T(8,128)(2,1)S(1)}, u32[]{:S(2)}, u32[]{:S(2)}) collective-permute-start(s16[1040,128]{1,0:T(8,128)(2,1)S(1)} %merge.12), channel_id=1, source_target_pairs={{0,32},{16,48},{32,0},{48,16},{1,33},{17,49},{33,1},{49,17},{2,34}... | collective-permute-start | bytes 798728 | tf_op jit(solution)/shard_map/ppermute | solution.py:366
  104.1 0.8 collective-permute-done.25.refs_1_
  105.0 4.4 %collective-permute-done.29.refs_3_ = s16[1040,128]{1,0:T(8,128)(2,1)S(1)} collective-permute-done((s16[1040,128]{1,0:T(8,128)(2,1)S(1)}, s16[1040,128]{1,0:T(8,128)(2,1)S(1)}, u32[]{:S(2)}, u32[]{:S(2)}) %collective-permute-start.29) | collective-permute-done | bytes 266272 | tf_op jit(solution)/shard_map/ppermute | solution.py:366
  109.4 0.4 merge.13.refs_0_
  109.8 2.7 %collective-permute-start.34 = (s16[1040,128]{1,0:T(8,128)(2,1)S(1)}, s16[1040,128]{1,0:T(8,128)(2,1)S(1)}, u32[]{:S(2)}, u32[]{:S(2)}) collective-permute-start(s16[1040,128]{1,0:T(8,128)(2,1)S(1)} %merge.13.refs_0_), channel_id=1, source_target_pairs={{0,32},{16,48},{32,0},{48,16},{1,33},{17,49},{33,1},{49,17},{2,34}... | collective-permute-start | bytes 798728 | tf_op jit(solution)/shard_map/ppermute | solution.py:366
  112.5 0.9 collective-permute-start.32
  113.4 2.5 %collective-permute-start.30 = (s16[1040,128]{1,0:T(8,128)(2,1)S(1)}, s16[1040,128]{1,0:T(8,128)(2,1)S(1)}, u32[]{:S(2)}, u32[]{:S(2)}) collective-permute-start(s16[1040,128]{1,0:T(8,128)(2,1)S(1)} %merge.13.refs_0_), channel_id=1, source_target_pairs={{0,64},{64,0},{1,65},{65,1},{2,66},{66,2},{3,67},{67,3},{4,68},{68... | collective-permute-start | bytes 798728 | tf_op jit(solution)/shard_map/ppermute | solution.py:366
  115.9 2.3 %collective-permute-done.34.refs_2_ = s16[1040,128]{1,0:T(8,128)(2,1)S(1)} collective-permute-done((s16[1040,128]{1,0:T(8,128)(2,1)S(1)}, s16[1040,128]{1,0:T(8,128)(2,1)S(1)}, u32[]{:S(2)}, u32[]{:S(2)}) %collective-permute-start.34) | collective-permute-done | bytes 266272 | tf_op jit(solution)/shard_map/ppermute | solution.py:366
  118.1 3.6 %collective-permute-start.35 = (s16[1040,128]{1,0:T(8,128)(2,1)S(1)}, s16[1040,128]{1,0:T(8,128)(2,1)S(1)}, u32[]{:S(2)}, u32[]{:S(2)}) collective-permute-start(s16[1040,128]{1,0:T(8,128)(2,1)S(1)} %collective-permute-done.34.refs_2_), channel_id=1, source_target_pairs={{0,64},{64,0},{1,65},{65,1},{2,66},{66,2},{3,67},{67,3},{4,68},{68... | collective-permute-start | bytes 798728 | tf_op jit(solution)/shard_map/ppermute | solution.py:366
  121.7 3.9 %collective-permute-start.33 = (s16[1040,128]{1,0:T(8,128)(2,1)S(1)}, s16[1040,128]{1,0:T(8,128)(2,1)S(1)}, u32[]{:S(2)}, u32[]{:S(2)}) collective-permute-start(s16[1040,128]{1,0:T(8,128)(2,1)S(1)} %collective-permute-done.32.refs_3_), channel_id=1, source_target_pairs={{0,64},{64,0},{1,65},{65,1},{2,66},{66,2},{3,67},{67,3},{4,68},{68... | collective-permute-start | bytes 798728 | tf_op jit(solution)/shard_map/ppermute | solution.py:366
  125.6 1.8 %collective-permute-start.31 = (s16[1040,128]{1,0:T(8,128)(2,1)S(1)}, s16[1040,128]{1,0:T(8,128)(2,1)S(1)}, u32[]{:S(2)}, u32[]{:S(2)}) collective-permute-start(s16[1040,128]{1,0:T(8,128)(2,1)S(1)} %collective-permute-done.30.refs_1_), channel_id=1, source_target_pairs={{0,16},{16,32},{32,48},{48,0},{1,17},{17,33},{33,49},{49,1},{2,18}... | collective-permute-start | bytes 798728 | tf_op jit(solution)/shard_map/ppermute | solution.py:366
  127.4 1.9 %spread.2.refs_4_ = f32[64,16384]{1,0:T(8,128)} custom-call(s32[18]{0:T(128)S(1)} %copy-done.1, s16[1040,128]{1,0:T(8,128)(2,1)S(1)} %merge.13.refs_0_, s16[1040,128]{1,0:T(8,128)(2,1)S(1)} %collective-permute-done.30.refs_1_, s16[1040,128]{1,0:T(8,128)(2,1)S(1)} %collective-permute-done.36.refs_2_, s16[1040,128]{1,0:T(8,128)(2,1)S(1)} %collective-permute-done.32.refs_3_), custom_call_target="tpu_custom_call" | custom-call | tf_op jit(solution)/shard_map/spread/pallas_call | solution.py:348
  129.3 0.5 collective-permute-done.35.refs_3_
  129.8 3.5 %collective-permute-done.33.refs_1_ = s16[1040,128]{1,0:T(8,128)(2,1)S(1)} collective-permute-done((s16[1040,128]{1,0:T(8,128)(2,1)S(1)}, s16[1040,128]{1,0:T(8,128)(2,1)S(1)}, u32[]{:S(2)}, u32[]{:S(2)}) %collective-permute-start.33) | collective-permute-done | bytes 266272 | tf_op jit(solution)/shard_map/ppermute | solution.py:366
  133.3 1.2 collective-permute-done.31.refs_0_
  134.5 1.9 %spread.3 = f32[64,16384]{1,0:T(8,128)} custom-call(s32[18]{0:T(128)S(1)} %copy-done.1, s16[1040,128]{1,0:T(8,128)(2,1)S(1)} %collective-permute-done.31.refs_0_, s16[1040,128]{1,0:T(8,128)(2,1)S(1)} %collective-permute-done.33.refs_1_, s16[1040,128]{1,0:T(8,128)(2,1)S(1)} %collective-permute-done.34.refs_2_, ...), custom_call_target="tpu_custom_call", output_to_operand_aliasing={{}: (5, {})} | custom-call | tf_op jit(solution)/shard_map/spread/pallas_call | solution.py:348
  (32 shorter events, 0.4 us)
Async XLA Ops:
  16.7 4.5 %copy-start.1 = (s32[18]{0:T(128)S(1)}, s32[18]{0:T(128)}, u32[]{:S(2)}) copy-start(s32[18]{0:T(128)} %stack.71.info) | copy-start | bytes 220
  16.7 4.5 %collective-permute-start = (s16[8320,128]{1,0:T(8,128)(2,1)}, s16[8320,128]{1,0:T(8,128)(2,1)S(1)}, u32[]{:S(2)}, u32[]{:S(2)}) collective-permute-start(s16[8320,128]{1,0:T(8,128)(2,1)} %get-tuple-element.24), channel_id=1, source_target_pairs={{0,1},{1,0},{2,3},{3,2},{4,5},{5,4},{6,7},{7,6},{8,9},{9,8},{10,11... | collective-permute-start | bytes 6389768 | tf_op jit(solution)/shard_map/ppermute | solution.py:366
  16.8 1.6 %copy-start = (s16[8320,128]{1,0:T(8,128)(2,1)S(1)}, s16[8320,128]{1,0:T(8,128)(2,1)}, u32[]{:S(2)}) copy-start(s16[8320,128]{1,0:T(8,128)(2,1)} %get-tuple-element.23.in_ref) | copy-start | bytes 6389764
  22.4 9.3 %collective-permute-start.2 = (s16[1040,128]{1,0:T(8,128)(2,1)S(1)}, s16[1040,128]{1,0:T(8,128)(2,1)S(1)}, u32[]{:S(2)}, u32[]{:S(2)}) collective-permute-start(s16[1040,128]{1,0:T(8,128)(2,1)S(1)} %get-tuple-element.28), channel_id=1, source_target_pairs={{0,12},{4,0},{8,4},{12,8},{1,13},{5,1},{9,5},{13,9},{2,14},{6,2},{... | collective-permute-start | bytes 798728 | tf_op jit(solution)/shard_map/ppermute | solution.py:366
  22.5 11.1 %collective-permute-start.4 = (s16[1040,128]{1,0:T(8,128)(2,1)S(1)}, s16[1040,128]{1,0:T(8,128)(2,1)S(1)}, u32[]{:S(2)}, u32[]{:S(2)}) collective-permute-start(s16[1040,128]{1,0:T(8,128)(2,1)S(1)} %get-tuple-element.30), channel_id=1, source_target_pairs={{0,2},{2,0},{1,3},{3,1},{4,6},{6,4},{5,7},{7,5},{8,10},{10,8},{9,1... | collective-permute-start | bytes 798728 | tf_op jit(solution)/shard_map/ppermute | solution.py:366
  26.4 12.9 %collective-permute-start.6 = (s16[1040,128]{1,0:T(8,128)(2,1)S(1)}, s16[1040,128]{1,0:T(8,128)(2,1)S(1)}, u32[]{:S(2)}, u32[]{:S(2)}) collective-permute-start(s16[1040,128]{1,0:T(8,128)(2,1)S(1)} %get-tuple-element.32), channel_id=1, source_target_pairs={{0,2},{2,0},{1,3},{3,1},{4,6},{6,4},{5,7},{7,5},{8,10},{10,8},{9,1... | collective-permute-start | bytes 798728 | tf_op jit(solution)/shard_map/ppermute | solution.py:366
  26.5 48.1 %copy-start.2 = (s32[1,1,512,2]{2,3,1,0:T(2,128)S(1)}, s32[1,1,512,2]{2,3,1,0:T(2,128)}, u32[]{:S(2)}) copy-start(s32[1,1,512,2]{2,3,1,0:T(2,128)} %param.5) | copy-start | bytes 12292
  26.5 14.4 %collective-permute-start.1 = (s16[1040,128]{1,0:T(8,128)(2,1)S(1)}, s16[1040,128]{1,0:T(8,128)(2,1)S(1)}, u32[]{:S(2)}, u32[]{:S(2)}) collective-permute-start(s16[1040,128]{1,0:T(8,128)(2,1)S(1)} %get-tuple-element.26), channel_id=1, source_target_pairs={{0,12},{4,0},{8,4},{12,8},{1,13},{5,1},{9,5},{13,9},{2,14},{6,2},{... | collective-permute-start | bytes 798728 | tf_op jit(solution)/shard_map/ppermute | solution.py:366
  31.9 12.5 %collective-permute-start.3 = (s16[1040,128]{1,0:T(8,128)(2,1)S(1)}, s16[1040,128]{1,0:T(8,128)(2,1)S(1)}, u32[]{:S(2)}, u32[]{:S(2)}) collective-permute-start(s16[1040,128]{1,0:T(8,128)(2,1)S(1)} %merge.7), channel_id=1, source_target_pairs={{0,2},{2,0},{1,3},{3,1},{4,6},{6,4},{5,7},{7,5},{8,10},{10,8},{9,1... | collective-permute-start | bytes 798728 | tf_op jit(solution)/shard_map/ppermute | solution.py:366
  33.8 10.7 %collective-permute-start.5 = (s16[1040,128]{1,0:T(8,128)(2,1)S(1)}, s16[1040,128]{1,0:T(8,128)(2,1)S(1)}, u32[]{:S(2)}, u32[]{:S(2)}) collective-permute-start(s16[1040,128]{1,0:T(8,128)(2,1)S(1)} %merge.8), channel_id=1, source_target_pairs={{0,4},{4,8},{8,12},{12,0},{1,5},{5,9},{9,13},{13,1},{2,6},{6,10},{... | collective-permute-start | bytes 798728 | tf_op jit(solution)/shard_map/ppermute | solution.py:366
  39.5 10.0 %collective-permute-start.7 = (s16[1040,128]{1,0:T(8,128)(2,1)S(1)}, s16[1040,128]{1,0:T(8,128)(2,1)S(1)}, u32[]{:S(2)}, u32[]{:S(2)}) collective-permute-start(s16[1040,128]{1,0:T(8,128)(2,1)S(1)} %merge.9), channel_id=1, source_target_pairs={{0,8},{4,12},{8,0},{12,4},{1,9},{5,13},{9,1},{13,5},{2,10},{6,14},... | collective-permute-start | bytes 798728 | tf_op jit(solution)/shard_map/ppermute | solution.py:366
  49.9 7.3 %collective-permute-start.10 = (bf16[16,64,128]{2,1,0:T(8,128)(2,1)S(1)}, bf16[16,64,128]{2,1,0:T(8,128)(2,1)S(1)}, u32[]{:S(2)}, u32[]{:S(2)}) collective-permute-start(bf16[16,64,128]{2,1,0:T(8,128)(2,1)S(1)} %share.1.refs_0_), channel_id=1, source_target_pairs={{0,12},{4,0},{8,4},{12,8},{1,13},{5,1},{9,5},{13,9},{2,14},{6,2},{... | collective-permute-start | bytes 786440 | tf_op jit(solution)/shard_map/ppermute | solution.py:366
  50.0 8.7 %collective-permute-start.15 = (bf16[16,64,128]{2,1,0:T(8,128)(2,1)S(1)}, bf16[16,64,128]{2,1,0:T(8,128)(2,1)S(1)}, u32[]{:S(2)}, u32[]{:S(2)}) collective-permute-start(bf16[16,64,128]{2,1,0:T(8,128)(2,1)S(1)} %share.1.refs_0_), channel_id=1, source_target_pairs={{0,1},{1,0},{2,3},{3,2},{4,5},{5,4},{6,7},{7,6},{8,9},{9,8},{10,11... | collective-permute-start | bytes 786440 | tf_op jit(solution)/shard_map/ppermute | solution.py:366
  50.1 9.9 %collective-permute-start.9 = (bf16[16,64,128]{2,1,0:T(8,128)(2,1)S(1)}, bf16[16,64,128]{2,1,0:T(8,128)(2,1)S(1)}, u32[]{:S(2)}, u32[]{:S(2)}) collective-permute-start(bf16[16,64,128]{2,1,0:T(8,128)(2,1)S(1)} %share.1.refs_0_), channel_id=1, source_target_pairs={{0,4},{4,8},{8,12},{12,0},{1,5},{5,9},{9,13},{13,1},{2,6},{6,10},{... | collective-permute-start | bytes 786440 | tf_op jit(solution)/shard_map/ppermute | solution.py:366
  52.0 8.4 %collective-permute-start.8 = (bf16[16,64,128]{2,1,0:T(8,128)(2,1)S(1)}, bf16[16,64,128]{2,1,0:T(8,128)(2,1)S(1)}, u32[]{:S(2)}, u32[]{:S(2)}) collective-permute-start(bf16[16,64,128]{2,1,0:T(8,128)(2,1)S(1)} %share.1.refs_0_), channel_id=1, source_target_pairs={{0,2},{2,0},{1,3},{3,1},{4,6},{6,4},{5,7},{7,5},{8,10},{10,8},{9,1... | collective-permute-start | bytes 786440 | tf_op jit(solution)/shard_map/ppermute | solution.py:366
  57.2 6.4 %collective-permute-start.13 = (bf16[16,64,128]{2,1,0:T(8,128)(2,1)S(1)}, bf16[16,64,128]{2,1,0:T(8,128)(2,1)S(1)}, u32[]{:S(2)}, u32[]{:S(2)}) collective-permute-start(bf16[16,64,128]{2,1,0:T(8,128)(2,1)S(1)} %collective-permute-done.10.refs_3_), channel_id=1, source_target_pairs={{0,12},{4,0},{8,4},{12,8},{1,13},{5,1},{9,5},{13,9},{2,14},{6,2},{... | collective-permute-start | bytes 786440 | tf_op jit(solution)/shard_map/ppermute | solution.py:366
  58.7 4.9 %collective-permute-start.18 = (bf16[16,64,128]{2,1,0:T(8,128)(2,1)S(1)}, bf16[16,64,128]{2,1,0:T(8,128)(2,1)S(1)}, u32[]{:S(2)}, u32[]{:S(2)}) collective-permute-start(bf16[16,64,128]{2,1,0:T(8,128)(2,1)S(1)} %collective-permute-done.10.refs_3_), channel_id=1, source_target_pairs={{0,1},{1,0},{2,3},{3,2},{4,5},{5,4},{6,7},{7,6},{8,9},{9,8},{10,11... | collective-permute-start | bytes 786440 | tf_op jit(solution)/shard_map/ppermute | solution.py:366
  58.7 9.1 %collective-permute-start.12 = (bf16[16,64,128]{2,1,0:T(8,128)(2,1)S(1)}, bf16[16,64,128]{2,1,0:T(8,128)(2,1)S(1)}, u32[]{:S(2)}, u32[]{:S(2)}) collective-permute-start(bf16[16,64,128]{2,1,0:T(8,128)(2,1)S(1)} %collective-permute-done.10.refs_3_), channel_id=1, source_target_pairs={{0,2},{2,0},{1,3},{3,1},{4,6},{6,4},{5,7},{7,5},{8,10},{10,8},{9,1... | collective-permute-start | bytes 786440 | tf_op jit(solution)/shard_map/ppermute | solution.py:366
  60.0 7.8 %collective-permute-start.17 = (bf16[16,64,128]{2,1,0:T(8,128)(2,1)S(1)}, bf16[16,64,128]{2,1,0:T(8,128)(2,1)S(1)}, u32[]{:S(2)}, u32[]{:S(2)}) collective-permute-start(bf16[16,64,128]{2,1,0:T(8,128)(2,1)S(1)} %collective-permute-done.9.refs_2_), channel_id=1, source_target_pairs={{0,1},{1,0},{2,3},{3,2},{4,5},{5,4},{6,7},{7,6},{8,9},{9,8},{10,11... | collective-permute-start | bytes 786440 | tf_op jit(solution)/shard_map/ppermute | solution.py:366
  60.4 9.5 %collective-permute-start.11 = (bf16[16,64,128]{2,1,0:T(8,128)(2,1)S(1)}, bf16[16,64,128]{2,1,0:T(8,128)(2,1)S(1)}, u32[]{:S(2)}, u32[]{:S(2)}) collective-permute-start(bf16[16,64,128]{2,1,0:T(8,128)(2,1)S(1)} %collective-permute-done.8.refs_1_), channel_id=1, source_target_pairs={{0,4},{4,8},{8,12},{12,0},{1,5},{5,9},{9,13},{13,1},{2,6},{6,10},{... | collective-permute-start | bytes 786440 | tf_op jit(solution)/shard_map/ppermute | solution.py:366
  63.6 9.5 %collective-permute-start.14 = (bf16[16,64,128]{2,1,0:T(8,128)(2,1)S(1)}, bf16[16,64,128]{2,1,0:T(8,128)(2,1)S(1)}, u32[]{:S(2)}, u32[]{:S(2)}) collective-permute-start(bf16[16,64,128]{2,1,0:T(8,128)(2,1)S(1)} %collective-permute-done.13.refs_6_), channel_id=1, source_target_pairs={{0,2},{2,0},{1,3},{3,1},{4,6},{6,4},{5,7},{7,5},{8,10},{10,8},{9,1... | collective-permute-start | bytes 786440 | tf_op jit(solution)/shard_map/ppermute | solution.py:366
  63.6 9.5 %collective-permute-start.16 = (bf16[16,64,128]{2,1,0:T(8,128)(2,1)S(1)}, bf16[16,64,128]{2,1,0:T(8,128)(2,1)S(1)}, u32[]{:S(2)}, u32[]{:S(2)}) collective-permute-start(bf16[16,64,128]{2,1,0:T(8,128)(2,1)S(1)} %collective-permute-done.8.refs_1_), channel_id=1, source_target_pairs={{0,1},{1,0},{2,3},{3,2},{4,5},{5,4},{6,7},{7,6},{8,9},{9,8},{10,11... | collective-permute-start | bytes 786440 | tf_op jit(solution)/shard_map/ppermute | solution.py:366
  67.8 5.2 %collective-permute-start.21 = (bf16[16,64,128]{2,1,0:T(8,128)(2,1)S(1)}, bf16[16,64,128]{2,1,0:T(8,128)(2,1)S(1)}, u32[]{:S(2)}, u32[]{:S(2)}) collective-permute-start(bf16[16,64,128]{2,1,0:T(8,128)(2,1)S(1)} %collective-permute-done.13.refs_6_), channel_id=1, source_target_pairs={{0,1},{1,0},{2,3},{3,2},{4,5},{5,4},{6,7},{7,6},{8,9},{9,8},{10,11... | collective-permute-start | bytes 786440 | tf_op jit(solution)/shard_map/ppermute | solution.py:366
  67.8 5.2 %collective-permute-start.20 = (bf16[16,64,128]{2,1,0:T(8,128)(2,1)S(1)}, bf16[16,64,128]{2,1,0:T(8,128)(2,1)S(1)}, u32[]{:S(2)}, u32[]{:S(2)}) collective-permute-start(bf16[16,64,128]{2,1,0:T(8,128)(2,1)S(1)} %collective-permute-done.12.refs_5_), channel_id=1, source_target_pairs={{0,1},{1,0},{2,3},{3,2},{4,5},{5,4},{6,7},{7,6},{8,9},{9,8},{10,11... | collective-permute-start | bytes 786440 | tf_op jit(solution)/shard_map/ppermute | solution.py:366
  69.9 3.1 %collective-permute-start.19 = (bf16[16,64,128]{2,1,0:T(8,128)(2,1)S(1)}, bf16[16,64,128]{2,1,0:T(8,128)(2,1)S(1)}, u32[]{:S(2)}, u32[]{:S(2)}) collective-permute-start(bf16[16,64,128]{2,1,0:T(8,128)(2,1)S(1)} %collective-permute-done.11.refs_4_), channel_id=1, source_target_pairs={{0,1},{1,0},{2,3},{3,2},{4,5},{5,4},{6,7},{7,6},{8,9},{9,8},{10,11... | collective-permute-start | bytes 786440 | tf_op jit(solution)/shard_map/ppermute | solution.py:366
  73.0 1.5 %collective-permute-start.22 = (bf16[16,64,128]{2,1,0:T(8,128)(2,1)S(1)}, bf16[16,64,128]{2,1,0:T(8,128)(2,1)S(1)}, u32[]{:S(2)}, u32[]{:S(2)}) collective-permute-start(bf16[16,64,128]{2,1,0:T(8,128)(2,1)S(1)} %collective-permute-done.14.refs_7_), channel_id=1, source_target_pairs={{0,1},{1,0},{2,3},{3,2},{4,5},{5,4},{6,7},{7,6},{8,9},{9,8},{10,11... | collective-permute-start | bytes 786440 | tf_op jit(solution)/shard_map/ppermute | solution.py:366
  83.4 9.3 %collective-permute-start.24 = (s16[1040,128]{1,0:T(8,128)(2,1)S(1)}, s16[1040,128]{1,0:T(8,128)(2,1)S(1)}, u32[]{:S(2)}, u32[]{:S(2)}) collective-permute-start(s16[1040,128]{1,0:T(8,128)(2,1)S(1)} %get-tuple-element.36), channel_id=1, source_target_pairs={{0,48},{16,0},{32,16},{48,32},{1,49},{17,1},{33,17},{49,33},{2,50}... | collective-permute-start | bytes 798728 | tf_op jit(solution)/shard_map/ppermute | solution.py:366
  83.5 10.8 %collective-permute-start.26 = (s16[1040,128]{1,0:T(8,128)(2,1)S(1)}, s16[1040,128]{1,0:T(8,128)(2,1)S(1)}, u32[]{:S(2)}, u32[]{:S(2)}) collective-permute-start(s16[1040,128]{1,0:T(8,128)(2,1)S(1)} %get-tuple-element.38), channel_id=1, source_target_pairs={{0,64},{64,0},{1,65},{65,1},{2,66},{66,2},{3,67},{67,3},{4,68},{68... | collective-permute-start | bytes 798728 | tf_op jit(solution)/shard_map/ppermute | solution.py:366
  86.6 13.5 %collective-permute-start.28 = (s16[1040,128]{1,0:T(8,128)(2,1)S(1)}, s16[1040,128]{1,0:T(8,128)(2,1)S(1)}, u32[]{:S(2)}, u32[]{:S(2)}) collective-permute-start(s16[1040,128]{1,0:T(8,128)(2,1)S(1)} %get-tuple-element.40), channel_id=1, source_target_pairs={{0,64},{64,0},{1,65},{65,1},{2,66},{66,2},{3,67},{67,3},{4,68},{68... | collective-permute-start | bytes 798728 | tf_op jit(solution)/shard_map/ppermute | solution.py:366
  87.1 17.0 %collective-permute-start.23 = (s16[1040,128]{1,0:T(8,128)(2,1)S(1)}, s16[1040,128]{1,0:T(8,128)(2,1)S(1)}, u32[]{:S(2)}, u32[]{:S(2)}) collective-permute-start(s16[1040,128]{1,0:T(8,128)(2,1)S(1)} %get-tuple-element.34), channel_id=1, source_target_pairs={{0,48},{16,0},{32,16},{48,32},{1,49},{17,1},{33,17},{49,33},{2,50}... | collective-permute-start | bytes 798728 | tf_op jit(solution)/shard_map/ppermute | solution.py:366
  92.9 12.0 %collective-permute-start.25 = (s16[1040,128]{1,0:T(8,128)(2,1)S(1)}, s16[1040,128]{1,0:T(8,128)(2,1)S(1)}, u32[]{:S(2)}, u32[]{:S(2)}) collective-permute-start(s16[1040,128]{1,0:T(8,128)(2,1)S(1)} %merge.10), channel_id=1, source_target_pairs={{0,64},{64,0},{1,65},{65,1},{2,66},{66,2},{3,67},{67,3},{4,68},{68... | collective-permute-start | bytes 798728 | tf_op jit(solution)/shard_map/ppermute | solution.py:366
  94.5 10.4 %collective-permute-start.27 = (s16[1040,128]{1,0:T(8,128)(2,1)S(1)}, s16[1040,128]{1,0:T(8,128)(2,1)S(1)}, u32[]{:S(2)}, u32[]{:S(2)}) collective-permute-start(s16[1040,128]{1,0:T(8,128)(2,1)S(1)} %merge.11), channel_id=1, source_target_pairs={{0,16},{16,32},{32,48},{48,0},{1,17},{17,33},{33,49},{49,1},{2,18}... | collective-permute-start | bytes 798728 | tf_op jit(solution)/shard_map/ppermute | solution.py:366
  100.2 9.1 %collective-permute-start.29 = (s16[1040,128]{1,0:T(8,128)(2,1)S(1)}, s16[1040,128]{1,0:T(8,128)(2,1)S(1)}, u32[]{:S(2)}, u32[]{:S(2)}) collective-permute-start(s16[1040,128]{1,0:T(8,128)(2,1)S(1)} %merge.12), channel_id=1, source_target_pairs={{0,32},{16,48},{32,0},{48,16},{1,33},{17,49},{33,1},{49,17},{2,34}... | collective-permute-start | bytes 798728 | tf_op jit(solution)/shard_map/ppermute | solution.py:366
  109.8 8.3 %collective-permute-start.34 = (s16[1040,128]{1,0:T(8,128)(2,1)S(1)}, s16[1040,128]{1,0:T(8,128)(2,1)S(1)}, u32[]{:S(2)}, u32[]{:S(2)}) collective-permute-start(s16[1040,128]{1,0:T(8,128)(2,1)S(1)} %merge.13.refs_0_), channel_id=1, source_target_pairs={{0,32},{16,48},{32,0},{48,16},{1,33},{17,49},{33,1},{49,17},{2,34}... | collective-permute-start | bytes 798728 | tf_op jit(solution)/shard_map/ppermute | solution.py:366
  112.5 9.1 %collective-permute-start.32 = (s16[1040,128]{1,0:T(8,128)(2,1)S(1)}, s16[1040,128]{1,0:T(8,128)(2,1)S(1)}, u32[]{:S(2)}, u32[]{:S(2)}) collective-permute-start(s16[1040,128]{1,0:T(8,128)(2,1)S(1)} %merge.13.refs_0_), channel_id=1, source_target_pairs={{0,48},{16,0},{32,16},{48,32},{1,49},{17,1},{33,17},{49,33},{2,50}... | collective-permute-start | bytes 798728 | tf_op jit(solution)/shard_map/ppermute | solution.py:366
  113.4 12.2 %collective-permute-start.30 = (s16[1040,128]{1,0:T(8,128)(2,1)S(1)}, s16[1040,128]{1,0:T(8,128)(2,1)S(1)}, u32[]{:S(2)}, u32[]{:S(2)}) collective-permute-start(s16[1040,128]{1,0:T(8,128)(2,1)S(1)} %merge.13.refs_0_), channel_id=1, source_target_pairs={{0,64},{64,0},{1,65},{65,1},{2,66},{66,2},{3,67},{67,3},{4,68},{68... | collective-permute-start | bytes 798728 | tf_op jit(solution)/shard_map/ppermute | solution.py:366
  115.8 11.5 %collective-permute-start.36 = (s16[1040,128]{1,0:T(8,128)(2,1)S(1)}, s16[1040,128]{1,0:T(8,128)(2,1)S(1)}, u32[]{:S(2)}, u32[]{:S(2)}) collective-permute-start(s16[1040,128]{1,0:T(8,128)(2,1)S(1)} %merge.13.refs_0_), channel_id=1, source_target_pairs={{0,16},{16,32},{32,48},{48,0},{1,17},{17,33},{33,49},{49,1},{2,18}... | collective-permute-start | bytes 798728 | tf_op jit(solution)/shard_map/ppermute | solution.py:366
  118.1 11.7 %collective-permute-start.35 = (s16[1040,128]{1,0:T(8,128)(2,1)S(1)}, s16[1040,128]{1,0:T(8,128)(2,1)S(1)}, u32[]{:S(2)}, u32[]{:S(2)}) collective-permute-start(s16[1040,128]{1,0:T(8,128)(2,1)S(1)} %collective-permute-done.34.refs_2_), channel_id=1, source_target_pairs={{0,64},{64,0},{1,65},{65,1},{2,66},{66,2},{3,67},{67,3},{4,68},{68... | collective-permute-start | bytes 798728 | tf_op jit(solution)/shard_map/ppermute | solution.py:366
  121.7 11.7 %collective-permute-start.33 = (s16[1040,128]{1,0:T(8,128)(2,1)S(1)}, s16[1040,128]{1,0:T(8,128)(2,1)S(1)}, u32[]{:S(2)}, u32[]{:S(2)}) collective-permute-start(s16[1040,128]{1,0:T(8,128)(2,1)S(1)} %collective-permute-done.32.refs_3_), channel_id=1, source_target_pairs={{0,64},{64,0},{1,65},{65,1},{2,66},{66,2},{3,67},{67,3},{4,68},{68... | collective-permute-start | bytes 798728 | tf_op jit(solution)/shard_map/ppermute | solution.py:366
  125.6 8.9 %collective-permute-start.31 = (s16[1040,128]{1,0:T(8,128)(2,1)S(1)}, s16[1040,128]{1,0:T(8,128)(2,1)S(1)}, u32[]{:S(2)}, u32[]{:S(2)}) collective-permute-start(s16[1040,128]{1,0:T(8,128)(2,1)S(1)} %collective-permute-done.30.refs_1_), channel_id=1, source_target_pairs={{0,16},{16,32},{32,48},{48,0},{1,17},{17,33},{33,49},{49,1},{2,18}... | collective-permute-start | bytes 798728 | tf_op jit(solution)/shard_map/ppermute | solution.py:366

commit v4 on v3

--- a/solution.py
+++ b/solution.py
@@ -19,8 +19,9 @@
 ROW = ("yh", "z")
 CHIPS = ("x", "yl")
 HOPS = [(0, 0), (0, 1), (-1, 0), (1, 0), (-1, 1), (1, 1), (2, 0), (2, 1)]
-SENT = (2, 4, 5, 7)
-KEPT = (0, 1, 3, 6)
+SENT = (7, 5, 4, 3, 2)
+KEPT = (0, 1, 6)
+FIRST = 3
 EARLY = (0, 1, 2, 3)
 LATE = (4, 5, 6, 7)
 PLACES = 2
@@ -173,7 +174,7 @@
     blocks, width, _ = keep_ref.shape
     each = blocks // len(HOPS)
     scales((got_ref,), scale, blocks * width)
-    for n, out_ref in zip(which, outs):
+    for k, (n, out_ref) in enumerate(zip(which, outs)):
         first = info[PLACES + n] * each
 
         def read(j):
@@ -181,7 +182,7 @@
             got = got_ref[pl.ds(pl.multiple_of(b * width, width), width), :].astype(jnp.int32).astype(F32)
             return keep_ref[b] + got * scale[0, pl.ds(b, 1), :]
 
-        if sent:
+        if k < sent:
             put_blocks(read, each, out_ref, steps)
         else:
 
@@ -198,7 +199,7 @@
     coded = jax.ShapeDtypeStruct((each * width + each, TILE), I16)
     return pl.pallas_call(
         functools.partial(pair_kernel, which, sent),
-        out_shape=[coded if sent else jax.ShapeDtypeStruct((each, width, TILE), F32)] * len(which),
+        out_shape=[coded] * sent + [jax.ShapeDtypeStruct((each, width, TILE), F32)] * (len(which) - sent),
         in_specs=[pl.BlockSpec(memory_space=s) for s in (pltpu.SMEM, pltpu.VMEM, pltpu.VMEM)],
         out_specs=[pl.BlockSpec(memory_space=pltpu.VMEM)] * len(which),
         scratch_shapes=[pltpu.VMEM((1, blocks, TILE), F32), pltpu.VMEM((each, TILE), F32)],
@@ -366,13 +367,15 @@
     return lax.ppermute(value, axis, [(i, (i + by) % count) for i in range(count)])
 
 
-def gather(value, ring, pair, direct):
+def gather(value, ring, pair, hold):
     across = shift(value, pair, 1)
+    far = shift(value, ring, 2)
     up = shift(value, ring, 1)
+    if hold:
+        value, across = lax.optimization_barrier((value, across))
     down = shift(value, ring, -1)
-    down_across = shift(down, pair, 1)
     up_across = shift(across, ring, 1)
-    far = shift(value, ring, 2) if direct else shift(down, ring, -1)
+    down_across = shift(across, ring, -1)
     far_across = shift(far, pair, 1)
     return [value, across, up, down, up_across, down_across, far, far_across]
 
@@ -383,16 +386,16 @@
 
 
 def scatter(sent, kept, ring, pair, last):
-    down, down_across, up_across, far_across = sent
-    own, across, up, far = kept
+    far_across, up_across, down_across, up, down = sent
+    own, across, far = kept
     far_across = shift(far_across, pair, 1)
-    up_across = shift(up_across, pair, 1)
+    up_across = shift(up_across, ring, 1)
     down_across = shift(down_across, ring, -1)
+    up = shift(up, ring, 1)
     down = shift(down, ring, -1)
     far = shift(merge(far, [far_across]), ring, 2)
-    up = shift(merge(up, [up_across]), ring, 1)
-    across = shift(merge(across, [down_across]), pair, 1)
-    return last(own, [down, across, up, far])
+    across = shift(merge(across, [up_across, down_across]), pair, 1)
+    return last(own, [up, down, far, across])
 
 
 def shards(tiles, tile_coords, tile_counts, omega):
@@ -409,12 +412,15 @@
     keep, give = forward(blocks, coords, info, omega, blk_row)
     got = shift(give, "core", 1)
     keep = plain(keep, width)
-    sent = pair(info, keep, got, SENT, True)
-    kept = pair(info, keep, got, KEPT, False)
-    mine = gather(scatter(sent, kept, *CHIPS, share), *CHIPS, False)
-    theirs = [shift(value, "core", 1) for value in mine]
+    sent = pair(info, keep, got, SENT[:FIRST], FIRST)
+    rest = pair(info, keep, got, SENT[FIRST:] + KEPT, len(SENT) - FIRST)
+    sent, kept = sent + rest[: len(SENT) - FIRST], rest[len(SENT) - FIRST :]
+    mine = gather(scatter(sent, kept, *CHIPS, share), *CHIPS, True)
+    early = lax.optimization_barrier([mine[n] for n in EARLY + (6,)])
+    given = [*early[:-1], mine[4], mine[5], early[-1], mine[7]]
+    theirs = [shift(value, "core", 1) for value in given]
     out = backward(blocks, coords, info, mine + theirs, blk_col)
-    parts = gather(scatter(out[: len(SENT)], out[len(SENT) :], "z", "yh", merge), "z", "yh", True)
+    parts = gather(scatter(out[: len(SENT)], out[len(SENT) :], "z", "yh", merge), "z", "yh", False)
     return spread(info, parts, width, LATE, spread(info, parts, width, EARLY))
 
 

time: 138 us -> 129 us (0.935)
  Pallas kernels: 32.7 us -> 23.9 us
  waiting for transfers between devices: 56.7 us -> 51.3 us
  starting transfers between devices: 44 us -> 49.4 us
    ppermute x37, starting transfers between devices: 44 us -> 49.4 us  [shift(): lax.ppermute(value, axis, [(i, (i + by) % count) for i in range(count)])]
    ppermute x37, waiting for transfers between devices: 56.7 us -> 51.3 us  [shift(): lax.ppermute(value, axis, [(i, (i + by) % count) for i in range(count)])]
    pallas_call x1, Pallas kernels: 15.5 us -> 10.9 us  [forward(): pl.pallas_call(forward_kernel, out_shape=(coded, coded), in_specs=[pl.Blo...]
    pallas_call x1, Pallas kernels: 8.87 us -> 4.79 us  [backward(): pl.pallas_call(backward_kernel, out_shape=[coded] * len(SENT) + [plain] *...]
  transfers between devices with their start and end apart: 37 -> 37, of which waited for: 23 -> 25; matrix products, arithmetic and copies ran while one was open for 0% -> 0% of each run, Pallas kernels for 3% -> 4%
where the time goes in v4:
time: 129 us; the launch traced here: 128 us
  waiting for transfers between devices  51.3 us (40%)
  starting transfers between devices  49.4 us (38%)
  Pallas kernels  23.9 us (19%)
  local copies, waits for them, and re-layouts  2.19 us (2%)
    ppermute x37, waiting for transfers between devices, shift(): lax.ppermute(value, axis, [(i, (i + by) % count) for i in range(count)])  51.3 us
    ppermute x37, starting transfers between devices, shift(): lax.ppermute(value, axis, [(i, (i + by) % count) for i in range(count)])  49.4 us
    pallas_call x1, Pallas kernels, forward(): pl.pallas_call(forward_kernel, out_shape=(coded, coded), in_specs=[pl.Blo...  10.9 us
    pallas_call x1, Pallas kernels, backward(): pl.pallas_call(backward_kernel, out_shape=[coded] * len(SENT) + [plain] *...  4.79 us
    pallas_call x2, Pallas kernels, spread(): pl.pallas_call(functools.partial(spread_kernel, which), out_shape=jax.Sha...  3.88 us
  transfers between devices with their start and end apart: 37, of which 25 were waited for; matrix products, arithmetic and copies ran while one was open for 0% of the time, Pallas kernels for 4%

profile of v4, /device:TPU:0, one launch (start us, length us, event | category | flops | bytes accessed | tf_op | source)
XLA Modules:
  0.0 127.7 jit_solution(3036616669320538710)
XLA Ops:
  0.7 0.6 stack.71.info
  1.2 10.9 %forward.1 = (s16[8320,128]{1,0:T(8,128)(2,1)}, s16[8320,128]{1,0:T(8,128)(2,1)}) custom-call(s32[2,512]{1,0:T(2,128)} %bitcast.23, s32[18]{0:T(128)} %stack.71.info, bf16[64,16384]{1,0:T(8,128)(2,1)} %omega_ref.1, bf16[512,128,128]{2,1,0:T(8,128)(2,1)} %bitcast.25), custom_call_target="tpu_custom_call" | custom-call | tf_op jit(solution)/shard_map/forward/pallas_call | solution.py:128
  12.1 0.7 collective-permute-start
  12.9 1.6 %copy-done = s16[8320,128]{1,0:T(8,128)(2,1)S(1)} copy-done((s16[8320,128]{1,0:T(8,128)(2,1)S(1)}, s16[8320,128]{1,0:T(8,128)(2,1)}, u32[]{:S(2)}) %copy-start) | copy-done | bytes 2129944
  14.5 0.5 plain.1.keep_ref
  15.0 1.9 %collective-permute-done.got_ref = s16[8320,128]{1,0:T(8,128)(2,1)S(1)} collective-permute-done((s16[8320,128]{1,0:T(8,128)(2,1)}, s16[8320,128]{1,0:T(8,128)(2,1)S(1)}, u32[]{:S(2)}, u32[]{:S(2)}) %collective-permute-start) | collective-permute-done | bytes 2129952 | tf_op jit(solution)/shard_map/ppermute | solution.py:367
  16.9 1.1 pair.3
  18.0 2.5 %collective-permute-start.3 = (s16[1040,128]{1,0:T(8,128)(2,1)S(1)}, s16[1040,128]{1,0:T(8,128)(2,1)S(1)}, u32[]{:S(2)}, u32[]{:S(2)}) collective-permute-start(s16[1040,128]{1,0:T(8,128)(2,1)S(1)} %get-tuple-element.36), channel_id=1, source_target_pairs={{0,2},{2,0},{1,3},{3,1},{4,6},{6,4},{5,7},{7,5},{8,10},{10,8},{9,1... | collective-permute-start | bytes 798728 | tf_op jit(solution)/shard_map/ppermute | solution.py:367
  20.5 0.5 collective-permute-start.5
  20.9 3.9 %collective-permute-start.6 = (s16[1040,128]{1,0:T(8,128)(2,1)S(1)}, s16[1040,128]{1,0:T(8,128)(2,1)S(1)}, u32[]{:S(2)}, u32[]{:S(2)}) collective-permute-start(s16[1040,128]{1,0:T(8,128)(2,1)S(1)} %get-tuple-element.39), channel_id=1, source_target_pairs={{0,12},{4,0},{8,4},{12,8},{1,13},{5,1},{9,5},{13,9},{2,14},{6,2},{... | collective-permute-start | bytes 798728 | tf_op jit(solution)/shard_map/ppermute | solution.py:367
  24.9 1.1 pair.2
  26.1 3.2 %collective-permute-start.2 = (s16[1040,128]{1,0:T(8,128)(2,1)S(1)}, s16[1040,128]{1,0:T(8,128)(2,1)S(1)}, u32[]{:S(2)}, u32[]{:S(2)}) collective-permute-start(s16[1040,128]{1,0:T(8,128)(2,1)S(1)} %get-tuple-element.34), channel_id=1, source_target_pairs={{0,12},{4,0},{8,4},{12,8},{1,13},{5,1},{9,5},{13,9},{2,14},{6,2},{... | collective-permute-start | bytes 798728 | tf_op jit(solution)/shard_map/ppermute | solution.py:367
  29.5 1.6 %collective-permute-start.4 = (s16[1040,128]{1,0:T(8,128)(2,1)S(1)}, s16[1040,128]{1,0:T(8,128)(2,1)S(1)}, u32[]{:S(2)}, u32[]{:S(2)}) collective-permute-start(s16[1040,128]{1,0:T(8,128)(2,1)S(1)} %merge.5), channel_id=1, source_target_pairs={{0,8},{4,12},{8,0},{12,4},{1,9},{5,13},{9,1},{13,5},{2,10},{6,14},... | collective-permute-start | bytes 798728 | tf_op jit(solution)/shard_map/ppermute | solution.py:367
  31.1 0.8 collective-permute-done.5.refs_0_
  32.0 0.3 merge.6
  32.3 2.0 %collective-permute-start.7 = (s16[1040,128]{1,0:T(8,128)(2,1)S(1)}, s16[1040,128]{1,0:T(8,128)(2,1)S(1)}, u32[]{:S(2)}, u32[]{:S(2)}) collective-permute-start(s16[1040,128]{1,0:T(8,128)(2,1)S(1)} %merge.6), channel_id=1, source_target_pairs={{0,2},{2,0},{1,3},{3,1},{4,6},{6,4},{5,7},{7,5},{8,10},{10,8},{9,1... | collective-permute-start | bytes 798728 | tf_op jit(solution)/shard_map/ppermute | solution.py:367
  34.2 3.1 %collective-permute-done.1.refs_0_ = s16[1040,128]{1,0:T(8,128)(2,1)S(1)} collective-permute-done((s16[1040,128]{1,0:T(8,128)(2,1)S(1)}, s16[1040,128]{1,0:T(8,128)(2,1)S(1)}, u32[]{:S(2)}, u32[]{:S(2)}) %collective-permute-start.1) | collective-permute-done | bytes 266272 | tf_op jit(solution)/shard_map/ppermute | solution.py:367
  37.4 5.1 %collective-permute-done.2.refs_1_ = s16[1040,128]{1,0:T(8,128)(2,1)S(1)} collective-permute-done((s16[1040,128]{1,0:T(8,128)(2,1)S(1)}, s16[1040,128]{1,0:T(8,128)(2,1)S(1)}, u32[]{:S(2)}, u32[]{:S(2)}) %collective-permute-start.2) | collective-permute-done | bytes 266272 | tf_op jit(solution)/shard_map/ppermute | solution.py:367
  42.4 1.8 %collective-permute-done.4.refs_2_ = s16[1040,128]{1,0:T(8,128)(2,1)S(1)} collective-permute-done((s16[1040,128]{1,0:T(8,128)(2,1)S(1)}, s16[1040,128]{1,0:T(8,128)(2,1)S(1)}, u32[]{:S(2)}, u32[]{:S(2)}) %collective-permute-start.4) | collective-permute-done | bytes 266272 | tf_op jit(solution)/shard_map/ppermute | solution.py:367
  44.3 0.3 share.1.refs_0_
  44.7 1.7 %collective-permute-start.8 = (bf16[16,64,128]{2,1,0:T(8,128)(2,1)S(1)}, bf16[16,64,128]{2,1,0:T(8,128)(2,1)S(1)}, u32[]{:S(2)}, u32[]{:S(2)}) collective-permute-start(bf16[16,64,128]{2,1,0:T(8,128)(2,1)S(1)} %share.1.refs_0_), channel_id=1, source_target_pairs={{0,2},{2,0},{1,3},{3,1},{4,6},{6,4},{5,7},{7,5},{8,10},{10,8},{9,1... | collective-permute-start | bytes 786440 | tf_op jit(solution)/shard_map/ppermute | solution.py:367
  46.4 2.5 %collective-permute-start.9 = (bf16[16,64,128]{2,1,0:T(8,128)(2,1)S(1)}, bf16[16,64,128]{2,1,0:T(8,128)(2,1)S(1)}, u32[]{:S(2)}, u32[]{:S(2)}) collective-permute-start(bf16[16,64,128]{2,1,0:T(8,128)(2,1)S(1)} %share.1.refs_0_), channel_id=1, source_target_pairs={{0,4},{4,8},{8,12},{12,0},{1,5},{5,9},{9,13},{13,1},{2,6},{6,10},{... | collective-permute-start | bytes 786440 | tf_op jit(solution)/shard_map/ppermute | solution.py:367
  49.0 6.5 %collective-permute-done.13.refs_6_ = bf16[16,64,128]{2,1,0:T(8,128)(2,1)S(1)} collective-permute-done((bf16[16,64,128]{2,1,0:T(8,128)(2,1)S(1)}, bf16[16,64,128]{2,1,0:T(8,128)(2,1)S(1)}, u32[]{:S(2)}, u32[]{:S(2)}) %collective-permute-start.13) | collective-permute-done | bytes 262176 | tf_op jit(solution)/shard_map/ppermute | solution.py:367
  55.4 1.7 %collective-permute-start.14 = (bf16[16,64,128]{2,1,0:T(8,128)(2,1)S(1)}, bf16[16,64,128]{2,1,0:T(8,128)(2,1)S(1)}, u32[]{:S(2)}, u32[]{:S(2)}) collective-permute-start(bf16[16,64,128]{2,1,0:T(8,128)(2,1)S(1)} %collective-permute-done.13.refs_6_), channel_id=1, source_target_pairs={{0,2},{2,0},{1,3},{3,1},{4,6},{6,4},{5,7},{7,5},{8,10},{10,8},{9,1... | collective-permute-start | bytes 786440 | tf_op jit(solution)/shard_map/ppermute | solution.py:367
  57.1 0.6 collective-permute-start.12
  57.7 1.5 %collective-permute-start.11 = (bf16[16,64,128]{2,1,0:T(8,128)(2,1)S(1)}, bf16[16,64,128]{2,1,0:T(8,128)(2,1)S(1)}, u32[]{:S(2)}, u32[]{:S(2)}) collective-permute-start(bf16[16,64,128]{2,1,0:T(8,128)(2,1)S(1)} %collective-permute-done.8.refs_1_), channel_id=1, source_target_pairs={{0,4},{4,8},{8,12},{12,0},{1,5},{5,9},{9,13},{13,1},{2,6},{6,10},{... | collective-permute-start | bytes 786440 | tf_op jit(solution)/shard_map/ppermute | solution.py:367
  59.2 2.6 %collective-permute-done.14.refs_7_ = bf16[16,64,128]{2,1,0:T(8,128)(2,1)S(1)} collective-permute-done((bf16[16,64,128]{2,1,0:T(8,128)(2,1)S(1)}, bf16[16,64,128]{2,1,0:T(8,128)(2,1)S(1)}, u32[]{:S(2)}, u32[]{:S(2)}) %collective-permute-start.14) | collective-permute-done | bytes 262176 | tf_op jit(solution)/shard_map/ppermute | solution.py:367
  61.8 2.6 %collective-permute-done.10.refs_3_ = bf16[16,64,128]{2,1,0:T(8,128)(2,1)S(1)} collective-permute-done((bf16[16,64,128]{2,1,0:T(8,128)(2,1)S(1)}, bf16[16,64,128]{2,1,0:T(8,128)(2,1)S(1)}, u32[]{:S(2)}, u32[]{:S(2)}) %collective-permute-start.10) | collective-permute-done | bytes 262176 | tf_op jit(solution)/shard_map/ppermute | solution.py:367
  64.4 0.5 collective-permute-start.16
  64.9 2.3 %collective-permute-done.12.refs_5_ = bf16[16,64,128]{2,1,0:T(8,128)(2,1)S(1)} collective-permute-done((bf16[16,64,128]{2,1,0:T(8,128)(2,1)S(1)}, bf16[16,64,128]{2,1,0:T(8,128)(2,1)S(1)}, u32[]{:S(2)}, u32[]{:S(2)}) %collective-permute-start.12) | collective-permute-done | bytes 262176 | tf_op jit(solution)/shard_map/ppermute | solution.py:367
  67.2 0.5 collective-permute-start.18
  67.8 0.4 collective-permute-start.20
  68.2 0.3 collective-permute-start.19
  68.5 0.2 collective-permute-done.17.refs_10_
  68.7 0.4 collective-permute-done.18.refs_11_
  69.1 0.4 collective-permute-done.21.refs_14_
  69.5 0.4 collective-permute-done.20.refs_13_
  69.9 0.4 collective-permute-done.19.refs_12_
  70.2 4.8 %backward.1 = (s16[1040,128]{1,0:T(8,128)(2,1)S(1)}, s16[1040,128]{1,0:T(8,128)(2,1)S(1)}, s16[1040,128]{1,0:T(8,128)(2,1)S(1)}, s16[1040,128]{1,0:T(8,128)(2,1)...) custom-call(s32[2,512]{1,0:T(2,128)S(1)} %bitcast.24, ...), custom_call_target="tpu_custom_call" | custom-call | tf_op jit(solution)/shard_map/backward/pallas_call | solution.py:307
  75.0 7.4 %collective-permute-start.25 = (s16[1040,128]{1,0:T(8,128)(2,1)S(1)}, s16[1040,128]{1,0:T(8,128)(2,1)S(1)}, u32[]{:S(2)}, u32[]{:S(2)}) collective-permute-start(s16[1040,128]{1,0:T(8,128)(2,1)S(1)} %get-tuple-element.51), channel_id=1, source_target_pairs={{0,64},{64,0},{1,65},{65,1},{2,66},{66,2},{3,67},{67,3},{4,68},{68... | collective-permute-start | bytes 798728 | tf_op jit(solution)/shard_map/ppermute | solution.py:367
  82.4 1.7 %collective-permute-start.27 = (s16[1040,128]{1,0:T(8,128)(2,1)S(1)}, s16[1040,128]{1,0:T(8,128)(2,1)S(1)}, u32[]{:S(2)}, u32[]{:S(2)}) collective-permute-start(s16[1040,128]{1,0:T(8,128)(2,1)S(1)} %get-tuple-element.53), channel_id=1, source_target_pairs={{0,16},{16,32},{32,48},{48,0},{1,17},{17,33},{33,49},{49,1},{2,18}... | collective-permute-start | bytes 798728 | tf_op jit(solution)/shard_map/ppermute | solution.py:367
  84.1 2.3 %collective-permute-start.28 = (s16[1040,128]{1,0:T(8,128)(2,1)S(1)}, s16[1040,128]{1,0:T(8,128)(2,1)S(1)}, u32[]{:S(2)}, u32[]{:S(2)}) collective-permute-start(s16[1040,128]{1,0:T(8,128)(2,1)S(1)} %get-tuple-element.54), channel_id=1, source_target_pairs={{0,48},{16,0},{32,16},{48,32},{1,49},{17,1},{33,17},{49,33},{2,50}... | collective-permute-start | bytes 798728 | tf_op jit(solution)/shard_map/ppermute | solution.py:367
  86.5 3.2 %collective-permute-start.24 = (s16[1040,128]{1,0:T(8,128)(2,1)S(1)}, s16[1040,128]{1,0:T(8,128)(2,1)S(1)}, u32[]{:S(2)}, u32[]{:S(2)}) collective-permute-start(s16[1040,128]{1,0:T(8,128)(2,1)S(1)} %get-tuple-element.49), channel_id=1, source_target_pairs={{0,48},{16,0},{32,16},{48,32},{1,49},{17,1},{33,17},{49,33},{2,50}... | collective-permute-start | bytes 798728 | tf_op jit(solution)/shard_map/ppermute | solution.py:367
  89.7 0.2 merge.7
  89.9 1.7 %collective-permute-start.26 = (s16[1040,128]{1,0:T(8,128)(2,1)S(1)}, s16[1040,128]{1,0:T(8,128)(2,1)S(1)}, u32[]{:S(2)}, u32[]{:S(2)}) collective-permute-start(s16[1040,128]{1,0:T(8,128)(2,1)S(1)} %merge.7), channel_id=1, source_target_pairs={{0,32},{16,48},{32,0},{48,16},{1,33},{17,49},{33,1},{49,17},{2,34}... | collective-permute-start | bytes 798728 | tf_op jit(solution)/shard_map/ppermute | solution.py:367
  91.6 1.3 %collective-permute-done.27.refs_0_ = s16[1040,128]{1,0:T(8,128)(2,1)S(1)} collective-permute-done((s16[1040,128]{1,0:T(8,128)(2,1)S(1)}, s16[1040,128]{1,0:T(8,128)(2,1)S(1)}, u32[]{:S(2)}, u32[]{:S(2)}) %collective-permute-start.27) | collective-permute-done | bytes 266272 | tf_op jit(solution)/shard_map/ppermute | solution.py:367
  93.0 1.3 collective-permute-done.28.refs_1_
  94.3 0.3 merge.8
  94.6 4.0 %collective-permute-done.23.refs_0_ = s16[1040,128]{1,0:T(8,128)(2,1)S(1)} collective-permute-done((s16[1040,128]{1,0:T(8,128)(2,1)S(1)}, s16[1040,128]{1,0:T(8,128)(2,1)S(1)}, u32[]{:S(2)}, u32[]{:S(2)}) %collective-permute-start.23) | collective-permute-done | bytes 266272 | tf_op jit(solution)/shard_map/ppermute | solution.py:367
  98.6 5.4 %collective-permute-done.24.refs_1_ = s16[1040,128]{1,0:T(8,128)(2,1)S(1)} collective-permute-done((s16[1040,128]{1,0:T(8,128)(2,1)S(1)}, s16[1040,128]{1,0:T(8,128)(2,1)S(1)}, u32[]{:S(2)}, u32[]{:S(2)}) %collective-permute-start.24) | collective-permute-done | bytes 266272 | tf_op jit(solution)/shard_map/ppermute | solution.py:367
  104.0 0.4 merge.9.refs_0_
  104.4 1.6 %collective-permute-start.33 = (s16[1040,128]{1,0:T(8,128)(2,1)S(1)}, s16[1040,128]{1,0:T(8,128)(2,1)S(1)}, u32[]{:S(2)}, u32[]{:S(2)}) collective-permute-start(s16[1040,128]{1,0:T(8,128)(2,1)S(1)} %merge.9.refs_0_), channel_id=1, source_target_pairs={{0,32},{16,48},{32,0},{48,16},{1,33},{17,49},{33,1},{49,17},{2,34}... | collective-permute-start | bytes 798728 | tf_op jit(solution)/shard_map/ppermute | solution.py:367
  106.2 2.3 %collective-permute-start.36 = (s16[1040,128]{1,0:T(8,128)(2,1)S(1)}, s16[1040,128]{1,0:T(8,128)(2,1)S(1)}, u32[]{:S(2)}, u32[]{:S(2)}) collective-permute-start(s16[1040,128]{1,0:T(8,128)(2,1)S(1)} %merge.9.refs_0_), channel_id=1, source_target_pairs={{0,48},{16,0},{32,16},{48,32},{1,49},{17,1},{33,17},{49,33},{2,50}... | collective-permute-start | bytes 798728 | tf_op jit(solution)/shard_map/ppermute | solution.py:367
  108.5 0.7 collective-permute-start.35
  109.2 3.7 %collective-permute-done.33.refs_2_ = s16[1040,128]{1,0:T(8,128)(2,1)S(1)} collective-permute-done((s16[1040,128]{1,0:T(8,128)(2,1)S(1)}, s16[1040,128]{1,0:T(8,128)(2,1)S(1)}, u32[]{:S(2)}, u32[]{:S(2)}) %collective-permute-start.33) | collective-permute-done | bytes 266272 | tf_op jit(solution)/shard_map/ppermute | solution.py:367
  112.9 1.4 %collective-permute-start.34 = (s16[1040,128]{1,0:T(8,128)(2,1)S(1)}, s16[1040,128]{1,0:T(8,128)(2,1)S(1)}, u32[]{:S(2)}, u32[]{:S(2)}) collective-permute-start(s16[1040,128]{1,0:T(8,128)(2,1)S(1)} %collective-permute-done.33.refs_2_), channel_id=1, source_target_pairs={{0,64},{64,0},{1,65},{65,1},{2,66},{66,2},{3,67},{67,3},{4,68},{68... | collective-permute-start | bytes 798728 | tf_op jit(solution)/shard_map/ppermute | solution.py:367
  114.3 1.4 %collective-permute-done.30.refs_1_ = s16[1040,128]{1,0:T(8,128)(2,1)S(1)} collective-permute-done((s16[1040,128]{1,0:T(8,128)(2,1)S(1)}, s16[1040,128]{1,0:T(8,128)(2,1)S(1)}, u32[]{:S(2)}, u32[]{:S(2)}) %collective-permute-start.30) | collective-permute-done | bytes 266272 | tf_op jit(solution)/shard_map/ppermute | solution.py:367
  115.7 2.3 %collective-permute-start.32 = (s16[1040,128]{1,0:T(8,128)(2,1)S(1)}, s16[1040,128]{1,0:T(8,128)(2,1)S(1)}, u32[]{:S(2)}, u32[]{:S(2)}) collective-permute-start(s16[1040,128]{1,0:T(8,128)(2,1)S(1)} %collective-permute-done.30.refs_1_), channel_id=1, source_target_pairs={{0,48},{16,0},{32,16},{48,32},{1,49},{17,1},{33,17},{49,33},{2,50}... | collective-permute-start | bytes 798728 | tf_op jit(solution)/shard_map/ppermute | solution.py:367
  118.1 0.4 collective-permute-done.35.refs_2_
  118.5 1.9 %spread.2.refs_4_ = f32[64,16384]{1,0:T(8,128)} custom-call(s32[18]{0:T(128)S(1)} %copy-done.1, s16[1040,128]{1,0:T(8,128)(2,1)S(1)} %merge.9.refs_0_, s16[1040,128]{1,0:T(8,128)(2,1)S(1)} %collective-permute-done.30.refs_1_, s16[1040,128]{1,0:T(8,128)(2,1)S(1)} %collective-permute-done.35.refs_2_, s16[1040,128]{1,0:T(8,128)(2,1)S(1)} %collective-permute-done.36.refs_3_), custom_call_target="tpu_custom_call" | custom-call | tf_op jit(solution)/shard_map/spread/pallas_call | solution.py:349
  120.4 0.4 collective-permute-done.34.refs_3_
  120.8 1.3 %collective-permute-done.32.refs_1_ = s16[1040,128]{1,0:T(8,128)(2,1)S(1)} collective-permute-done((s16[1040,128]{1,0:T(8,128)(2,1)S(1)}, s16[1040,128]{1,0:T(8,128)(2,1)S(1)}, u32[]{:S(2)}, u32[]{:S(2)}) %collective-permute-start.32) | collective-permute-done | bytes 266272 | tf_op jit(solution)/shard_map/ppermute | solution.py:367
  122.1 3.5 %collective-permute-done.31.refs_0_ = s16[1040,128]{1,0:T(8,128)(2,1)S(1)} collective-permute-done((s16[1040,128]{1,0:T(8,128)(2,1)S(1)}, s16[1040,128]{1,0:T(8,128)(2,1)S(1)}, u32[]{:S(2)}, u32[]{:S(2)}) %collective-permute-start.31) | collective-permute-done | bytes 266272 | tf_op jit(solution)/shard_map/ppermute | solution.py:367
  125.6 1.9 %spread.3 = f32[64,16384]{1,0:T(8,128)} custom-call(s32[18]{0:T(128)S(1)} %copy-done.1, s16[1040,128]{1,0:T(8,128)(2,1)S(1)} %collective-permute-done.31.refs_0_, s16[1040,128]{1,0:T(8,128)(2,1)S(1)} %collective-permute-done.32.refs_1_, s16[1040,128]{1,0:T(8,128)(2,1)S(1)} %collective-permute-done.33.refs_2_, ...), custom_call_target="tpu_custom_call", output_to_operand_aliasing={{}: (5, {})} | custom-call | tf_op jit(solution)/shard_map/spread/pallas_call | solution.py:349
  (30 shorter events, 0.8 us)
Async XLA Ops:
  12.1 4.8 %copy-start.1 = (s32[18]{0:T(128)S(1)}, s32[18]{0:T(128)}, u32[]{:S(2)}) copy-start(s32[18]{0:T(128)} %stack.71.info) | copy-start | bytes 220
  12.1 4.8 %collective-permute-start = (s16[8320,128]{1,0:T(8,128)(2,1)}, s16[8320,128]{1,0:T(8,128)(2,1)S(1)}, u32[]{:S(2)}, u32[]{:S(2)}) collective-permute-start(s16[8320,128]{1,0:T(8,128)(2,1)} %get-tuple-element.31), channel_id=1, source_target_pairs={{0,1},{1,0},{2,3},{3,2},{4,5},{5,4},{6,7},{7,6},{8,9},{9,8},{10,11... | collective-permute-start | bytes 6389768 | tf_op jit(solution)/shard_map/ppermute | solution.py:367
  12.9 1.6 %copy-start = (s16[8320,128]{1,0:T(8,128)(2,1)S(1)}, s16[8320,128]{1,0:T(8,128)(2,1)}, u32[]{:S(2)}) copy-start(s16[8320,128]{1,0:T(8,128)(2,1)} %get-tuple-element.30.in_ref) | copy-start | bytes 6389764
  18.0 11.3 %collective-permute-start.3 = (s16[1040,128]{1,0:T(8,128)(2,1)S(1)}, s16[1040,128]{1,0:T(8,128)(2,1)S(1)}, u32[]{:S(2)}, u32[]{:S(2)}) collective-permute-start(s16[1040,128]{1,0:T(8,128)(2,1)S(1)} %get-tuple-element.36), channel_id=1, source_target_pairs={{0,2},{2,0},{1,3},{3,1},{4,6},{6,4},{5,7},{7,5},{8,10},{10,8},{9,1... | collective-permute-start | bytes 798728 | tf_op jit(solution)/shard_map/ppermute | solution.py:367
  20.5 11.5 %collective-permute-start.5 = (s16[1040,128]{1,0:T(8,128)(2,1)S(1)}, s16[1040,128]{1,0:T(8,128)(2,1)S(1)}, u32[]{:S(2)}, u32[]{:S(2)}) collective-permute-start(s16[1040,128]{1,0:T(8,128)(2,1)S(1)} %get-tuple-element.38), channel_id=1, source_target_pairs={{0,4},{4,8},{8,12},{12,0},{1,5},{5,9},{9,13},{13,1},{2,6},{6,10},{... | collective-permute-start | bytes 798728 | tf_op jit(solution)/shard_map/ppermute | solution.py:367
  20.9 49.3 %copy-start.2 = (s32[1,1,512,2]{2,3,1,0:T(2,128)S(1)}, s32[1,1,512,2]{2,3,1,0:T(2,128)}, u32[]{:S(2)}) copy-start(s32[1,1,512,2]{2,3,1,0:T(2,128)} %param.5) | copy-start | bytes 12292
  20.9 11.1 %collective-permute-start.6 = (s16[1040,128]{1,0:T(8,128)(2,1)S(1)}, s16[1040,128]{1,0:T(8,128)(2,1)S(1)}, u32[]{:S(2)}, u32[]{:S(2)}) collective-permute-start(s16[1040,128]{1,0:T(8,128)(2,1)S(1)} %get-tuple-element.39), channel_id=1, source_target_pairs={{0,12},{4,0},{8,4},{12,8},{1,13},{5,1},{9,5},{13,9},{2,14},{6,2},{... | collective-permute-start | bytes 798728 | tf_op jit(solution)/shard_map/ppermute | solution.py:367
  26.0 11.4 %collective-permute-start.1 = (s16[1040,128]{1,0:T(8,128)(2,1)S(1)}, s16[1040,128]{1,0:T(8,128)(2,1)S(1)}, u32[]{:S(2)}, u32[]{:S(2)}) collective-permute-start(s16[1040,128]{1,0:T(8,128)(2,1)S(1)} %get-tuple-element.33), channel_id=1, source_target_pairs={{0,4},{4,8},{8,12},{12,0},{1,5},{5,9},{9,13},{13,1},{2,6},{6,10},{... | collective-permute-start | bytes 798728 | tf_op jit(solution)/shard_map/ppermute | solution.py:367
  26.1 16.4 %collective-permute-start.2 = (s16[1040,128]{1,0:T(8,128)(2,1)S(1)}, s16[1040,128]{1,0:T(8,128)(2,1)S(1)}, u32[]{:S(2)}, u32[]{:S(2)}) collective-permute-start(s16[1040,128]{1,0:T(8,128)(2,1)S(1)} %get-tuple-element.34), channel_id=1, source_target_pairs={{0,12},{4,0},{8,4},{12,8},{1,13},{5,1},{9,5},{13,9},{2,14},{6,2},{... | collective-permute-start | bytes 798728 | tf_op jit(solution)/shard_map/ppermute | solution.py:367
  29.5 14.8 %collective-permute-start.4 = (s16[1040,128]{1,0:T(8,128)(2,1)S(1)}, s16[1040,128]{1,0:T(8,128)(2,1)S(1)}, u32[]{:S(2)}, u32[]{:S(2)}) collective-permute-start(s16[1040,128]{1,0:T(8,128)(2,1)S(1)} %merge.5), channel_id=1, source_target_pairs={{0,8},{4,12},{8,0},{12,4},{1,9},{5,13},{9,1},{13,5},{2,10},{6,14},... | collective-permute-start | bytes 798728 | tf_op jit(solution)/shard_map/ppermute | solution.py:367
  32.3 12.0 %collective-permute-start.7 = (s16[1040,128]{1,0:T(8,128)(2,1)S(1)}, s16[1040,128]{1,0:T(8,128)(2,1)S(1)}, u32[]{:S(2)}, u32[]{:S(2)}) collective-permute-start(s16[1040,128]{1,0:T(8,128)(2,1)S(1)} %merge.6), channel_id=1, source_target_pairs={{0,2},{2,0},{1,3},{3,1},{4,6},{6,4},{5,7},{7,5},{8,10},{10,8},{9,1... | collective-permute-start | bytes 798728 | tf_op jit(solution)/shard_map/ppermute | solution.py:367
  44.6 10.9 %collective-permute-start.13 = (bf16[16,64,128]{2,1,0:T(8,128)(2,1)S(1)}, bf16[16,64,128]{2,1,0:T(8,128)(2,1)S(1)}, u32[]{:S(2)}, u32[]{:S(2)}) collective-permute-start(bf16[16,64,128]{2,1,0:T(8,128)(2,1)S(1)} %share.1.refs_0_), channel_id=1, source_target_pairs={{0,8},{4,12},{8,0},{12,4},{1,9},{5,13},{9,1},{13,5},{2,10},{6,14},... | collective-permute-start | bytes 786440 | tf_op jit(solution)/shard_map/ppermute | solution.py:367
  44.7 12.4 %collective-permute-start.8 = (bf16[16,64,128]{2,1,0:T(8,128)(2,1)S(1)}, bf16[16,64,128]{2,1,0:T(8,128)(2,1)S(1)}, u32[]{:S(2)}, u32[]{:S(2)}) collective-permute-start(bf16[16,64,128]{2,1,0:T(8,128)(2,1)S(1)} %share.1.refs_0_), channel_id=1, source_target_pairs={{0,2},{2,0},{1,3},{3,1},{4,6},{6,4},{5,7},{7,5},{8,10},{10,8},{9,1... | collective-permute-start | bytes 786440 | tf_op jit(solution)/shard_map/ppermute | solution.py:367
  46.4 15.4 %collective-permute-start.9 = (bf16[16,64,128]{2,1,0:T(8,128)(2,1)S(1)}, bf16[16,64,128]{2,1,0:T(8,128)(2,1)S(1)}, u32[]{:S(2)}, u32[]{:S(2)}) collective-permute-start(bf16[16,64,128]{2,1,0:T(8,128)(2,1)S(1)} %share.1.refs_0_), channel_id=1, source_target_pairs={{0,4},{4,8},{8,12},{12,0},{1,5},{5,9},{9,13},{13,1},{2,6},{6,10},{... | collective-permute-start | bytes 786440 | tf_op jit(solution)/shard_map/ppermute | solution.py:367
  55.4 6.4 %collective-permute-start.14 = (bf16[16,64,128]{2,1,0:T(8,128)(2,1)S(1)}, bf16[16,64,128]{2,1,0:T(8,128)(2,1)S(1)}, u32[]{:S(2)}, u32[]{:S(2)}) collective-permute-start(bf16[16,64,128]{2,1,0:T(8,128)(2,1)S(1)} %collective-permute-done.13.refs_6_), channel_id=1, source_target_pairs={{0,2},{2,0},{1,3},{3,1},{4,6},{6,4},{5,7},{7,5},{8,10},{10,8},{9,1... | collective-permute-start | bytes 786440 | tf_op jit(solution)/shard_map/ppermute | solution.py:367
  57.1 7.3 %collective-permute-start.10 = (bf16[16,64,128]{2,1,0:T(8,128)(2,1)S(1)}, bf16[16,64,128]{2,1,0:T(8,128)(2,1)S(1)}, u32[]{:S(2)}, u32[]{:S(2)}) collective-permute-start(bf16[16,64,128]{2,1,0:T(8,128)(2,1)S(1)} %share.1.refs_0_), channel_id=1, source_target_pairs={{0,12},{4,0},{8,4},{12,8},{1,13},{5,1},{9,5},{13,9},{2,14},{6,2},{... | collective-permute-start | bytes 786440 | tf_op jit(solution)/shard_map/ppermute | solution.py:367
  57.1 10.1 %collective-permute-start.12 = (bf16[16,64,128]{2,1,0:T(8,128)(2,1)S(1)}, bf16[16,64,128]{2,1,0:T(8,128)(2,1)S(1)}, u32[]{:S(2)}, u32[]{:S(2)}) collective-permute-start(bf16[16,64,128]{2,1,0:T(8,128)(2,1)S(1)} %collective-permute-done.8.refs_1_), channel_id=1, source_target_pairs={{0,12},{4,0},{8,4},{12,8},{1,13},{5,1},{9,5},{13,9},{2,14},{6,2},{... | collective-permute-start | bytes 786440 | tf_op jit(solution)/shard_map/ppermute | solution.py:367
  57.7 9.5 %collective-permute-start.11 = (bf16[16,64,128]{2,1,0:T(8,128)(2,1)S(1)}, bf16[16,64,128]{2,1,0:T(8,128)(2,1)S(1)}, u32[]{:S(2)}, u32[]{:S(2)}) collective-permute-start(bf16[16,64,128]{2,1,0:T(8,128)(2,1)S(1)} %collective-permute-done.8.refs_1_), channel_id=1, source_target_pairs={{0,4},{4,8},{8,12},{12,0},{1,5},{5,9},{9,13},{13,1},{2,6},{6,10},{... | collective-permute-start | bytes 786440 | tf_op jit(solution)/shard_map/ppermute | solution.py:367
  61.8 5.9 %collective-permute-start.22 = (bf16[16,64,128]{2,1,0:T(8,128)(2,1)S(1)}, bf16[16,64,128]{2,1,0:T(8,128)(2,1)S(1)}, u32[]{:S(2)}, u32[]{:S(2)}) collective-permute-start(bf16[16,64,128]{2,1,0:T(8,128)(2,1)S(1)} %collective-permute-done.14.refs_7_), channel_id=1, source_target_pairs={{0,1},{1,0},{2,3},{3,2},{4,5},{5,4},{6,7},{7,6},{8,9},{9,8},{10,11... | collective-permute-start | bytes 786440 | tf_op jit(solution)/shard_map/ppermute | solution.py:367
  64.4 3.4 %collective-permute-start.15 = (bf16[16,64,128]{2,1,0:T(8,128)(2,1)S(1)}, bf16[16,64,128]{2,1,0:T(8,128)(2,1)S(1)}, u32[]{:S(2)}, u32[]{:S(2)}) collective-permute-start(bf16[16,64,128]{2,1,0:T(8,128)(2,1)S(1)} %share.1.refs_0_), channel_id=1, source_target_pairs={{0,1},{1,0},{2,3},{3,2},{4,5},{5,4},{6,7},{7,6},{8,9},{9,8},{10,11... | collective-permute-start | bytes 786440 | tf_op jit(solution)/shard_map/ppermute | solution.py:367
  64.4 3.8 %collective-permute-start.16 = (bf16[16,64,128]{2,1,0:T(8,128)(2,1)S(1)}, bf16[16,64,128]{2,1,0:T(8,128)(2,1)S(1)}, u32[]{:S(2)}, u32[]{:S(2)}) collective-permute-start(bf16[16,64,128]{2,1,0:T(8,128)(2,1)S(1)} %collective-permute-done.8.refs_1_), channel_id=1, source_target_pairs={{0,1},{1,0},{2,3},{3,2},{4,5},{5,4},{6,7},{7,6},{8,9},{9,8},{10,11... | collective-permute-start | bytes 786440 | tf_op jit(solution)/shard_map/ppermute | solution.py:367
  67.2 1.5 %collective-permute-start.17 = (bf16[16,64,128]{2,1,0:T(8,128)(2,1)S(1)}, bf16[16,64,128]{2,1,0:T(8,128)(2,1)S(1)}, u32[]{:S(2)}, u32[]{:S(2)}) collective-permute-start(bf16[16,64,128]{2,1,0:T(8,128)(2,1)S(1)} %collective-permute-done.9.refs_2_), channel_id=1, source_target_pairs={{0,1},{1,0},{2,3},{3,2},{4,5},{5,4},{6,7},{7,6},{8,9},{9,8},{10,11... | collective-permute-start | bytes 786440 | tf_op jit(solution)/shard_map/ppermute | solution.py:367
  67.2 1.9 %collective-permute-start.18 = (bf16[16,64,128]{2,1,0:T(8,128)(2,1)S(1)}, bf16[16,64,128]{2,1,0:T(8,128)(2,1)S(1)}, u32[]{:S(2)}, u32[]{:S(2)}) collective-permute-start(bf16[16,64,128]{2,1,0:T(8,128)(2,1)S(1)} %collective-permute-done.10.refs_3_), channel_id=1, source_target_pairs={{0,1},{1,0},{2,3},{3,2},{4,5},{5,4},{6,7},{7,6},{8,9},{9,8},{10,11... | collective-permute-start | bytes 786440 | tf_op jit(solution)/shard_map/ppermute | solution.py:367
  67.7 1.8 %collective-permute-start.21 = (bf16[16,64,128]{2,1,0:T(8,128)(2,1)S(1)}, bf16[16,64,128]{2,1,0:T(8,128)(2,1)S(1)}, u32[]{:S(2)}, u32[]{:S(2)}) collective-permute-start(bf16[16,64,128]{2,1,0:T(8,128)(2,1)S(1)} %collective-permute-done.13.refs_6_), channel_id=1, source_target_pairs={{0,1},{1,0},{2,3},{3,2},{4,5},{5,4},{6,7},{7,6},{8,9},{9,8},{10,11... | collective-permute-start | bytes 786440 | tf_op jit(solution)/shard_map/ppermute | solution.py:367
  67.8 2.1 %collective-permute-start.20 = (bf16[16,64,128]{2,1,0:T(8,128)(2,1)S(1)}, bf16[16,64,128]{2,1,0:T(8,128)(2,1)S(1)}, u32[]{:S(2)}, u32[]{:S(2)}) collective-permute-start(bf16[16,64,128]{2,1,0:T(8,128)(2,1)S(1)} %collective-permute-done.12.refs_5_), channel_id=1, source_target_pairs={{0,1},{1,0},{2,3},{3,2},{4,5},{5,4},{6,7},{7,6},{8,9},{9,8},{10,11... | collective-permute-start | bytes 786440 | tf_op jit(solution)/shard_map/ppermute | solution.py:367
  68.2 2.0 %collective-permute-start.19 = (bf16[16,64,128]{2,1,0:T(8,128)(2,1)S(1)}, bf16[16,64,128]{2,1,0:T(8,128)(2,1)S(1)}, u32[]{:S(2)}, u32[]{:S(2)}) collective-permute-start(bf16[16,64,128]{2,1,0:T(8,128)(2,1)S(1)} %collective-permute-done.11.refs_4_), channel_id=1, source_target_pairs={{0,1},{1,0},{2,3},{3,2},{4,5},{5,4},{6,7},{7,6},{8,9},{9,8},{10,11... | collective-permute-start | bytes 786440 | tf_op jit(solution)/shard_map/ppermute | solution.py:367
  75.0 14.7 %collective-permute-start.25 = (s16[1040,128]{1,0:T(8,128)(2,1)S(1)}, s16[1040,128]{1,0:T(8,128)(2,1)S(1)}, u32[]{:S(2)}, u32[]{:S(2)}) collective-permute-start(s16[1040,128]{1,0:T(8,128)(2,1)S(1)} %get-tuple-element.51), channel_id=1, source_target_pairs={{0,64},{64,0},{1,65},{65,1},{2,66},{66,2},{3,67},{67,3},{4,68},{68... | collective-permute-start | bytes 798728 | tf_op jit(solution)/shard_map/ppermute | solution.py:367
  82.4 10.6 %collective-permute-start.27 = (s16[1040,128]{1,0:T(8,128)(2,1)S(1)}, s16[1040,128]{1,0:T(8,128)(2,1)S(1)}, u32[]{:S(2)}, u32[]{:S(2)}) collective-permute-start(s16[1040,128]{1,0:T(8,128)(2,1)S(1)} %get-tuple-element.53), channel_id=1, source_target_pairs={{0,16},{16,32},{32,48},{48,0},{1,17},{17,33},{33,49},{49,1},{2,18}... | collective-permute-start | bytes 798728 | tf_op jit(solution)/shard_map/ppermute | solution.py:367
  84.1 10.1 %collective-permute-start.28 = (s16[1040,128]{1,0:T(8,128)(2,1)S(1)}, s16[1040,128]{1,0:T(8,128)(2,1)S(1)}, u32[]{:S(2)}, u32[]{:S(2)}) collective-permute-start(s16[1040,128]{1,0:T(8,128)(2,1)S(1)} %get-tuple-element.54), channel_id=1, source_target_pairs={{0,48},{16,0},{32,16},{48,32},{1,49},{17,1},{33,17},{49,33},{2,50}... | collective-permute-start | bytes 798728 | tf_op jit(solution)/shard_map/ppermute | solution.py:367
  86.5 12.1 %collective-permute-start.23 = (s16[1040,128]{1,0:T(8,128)(2,1)S(1)}, s16[1040,128]{1,0:T(8,128)(2,1)S(1)}, u32[]{:S(2)}, u32[]{:S(2)}) collective-permute-start(s16[1040,128]{1,0:T(8,128)(2,1)S(1)} %get-tuple-element.48), channel_id=1, source_target_pairs={{0,16},{16,32},{32,48},{48,0},{1,17},{17,33},{33,49},{49,1},{2,18}... | collective-permute-start | bytes 798728 | tf_op jit(solution)/shard_map/ppermute | solution.py:367
  86.5 17.5 %collective-permute-start.24 = (s16[1040,128]{1,0:T(8,128)(2,1)S(1)}, s16[1040,128]{1,0:T(8,128)(2,1)S(1)}, u32[]{:S(2)}, u32[]{:S(2)}) collective-permute-start(s16[1040,128]{1,0:T(8,128)(2,1)S(1)} %get-tuple-element.49), channel_id=1, source_target_pairs={{0,48},{16,0},{32,16},{48,32},{1,49},{17,1},{33,17},{49,33},{2,50}... | collective-permute-start | bytes 798728 | tf_op jit(solution)/shard_map/ppermute | solution.py:367
  89.9 14.1 %collective-permute-start.26 = (s16[1040,128]{1,0:T(8,128)(2,1)S(1)}, s16[1040,128]{1,0:T(8,128)(2,1)S(1)}, u32[]{:S(2)}, u32[]{:S(2)}) collective-permute-start(s16[1040,128]{1,0:T(8,128)(2,1)S(1)} %merge.7), channel_id=1, source_target_pairs={{0,32},{16,48},{32,0},{48,16},{1,33},{17,49},{33,1},{49,17},{2,34}... | collective-permute-start | bytes 798728 | tf_op jit(solution)/shard_map/ppermute | solution.py:367
  94.5 9.5 %collective-permute-start.29 = (s16[1040,128]{1,0:T(8,128)(2,1)S(1)}, s16[1040,128]{1,0:T(8,128)(2,1)S(1)}, u32[]{:S(2)}, u32[]{:S(2)}) collective-permute-start(s16[1040,128]{1,0:T(8,128)(2,1)S(1)} %merge.8), channel_id=1, source_target_pairs={{0,64},{64,0},{1,65},{65,1},{2,66},{66,2},{3,67},{67,3},{4,68},{68... | collective-permute-start | bytes 798728 | tf_op jit(solution)/shard_map/ppermute | solution.py:367
  104.4 8.5 %collective-permute-start.33 = (s16[1040,128]{1,0:T(8,128)(2,1)S(1)}, s16[1040,128]{1,0:T(8,128)(2,1)S(1)}, u32[]{:S(2)}, u32[]{:S(2)}) collective-permute-start(s16[1040,128]{1,0:T(8,128)(2,1)S(1)} %merge.9.refs_0_), channel_id=1, source_target_pairs={{0,32},{16,48},{32,0},{48,16},{1,33},{17,49},{33,1},{49,17},{2,34}... | collective-permute-start | bytes 798728 | tf_op jit(solution)/shard_map/ppermute | solution.py:367
  106.0 9.7 %collective-permute-start.30 = (s16[1040,128]{1,0:T(8,128)(2,1)S(1)}, s16[1040,128]{1,0:T(8,128)(2,1)S(1)}, u32[]{:S(2)}, u32[]{:S(2)}) collective-permute-start(s16[1040,128]{1,0:T(8,128)(2,1)S(1)} %merge.9.refs_0_), channel_id=1, source_target_pairs={{0,64},{64,0},{1,65},{65,1},{2,66},{66,2},{3,67},{67,3},{4,68},{68... | collective-permute-start | bytes 798728 | tf_op jit(solution)/shard_map/ppermute | solution.py:367
  106.2 12.0 %collective-permute-start.36 = (s16[1040,128]{1,0:T(8,128)(2,1)S(1)}, s16[1040,128]{1,0:T(8,128)(2,1)S(1)}, u32[]{:S(2)}, u32[]{:S(2)}) collective-permute-start(s16[1040,128]{1,0:T(8,128)(2,1)S(1)} %merge.9.refs_0_), channel_id=1, source_target_pairs={{0,48},{16,0},{32,16},{48,32},{1,49},{17,1},{33,17},{49,33},{2,50}... | collective-permute-start | bytes 798728 | tf_op jit(solution)/shard_map/ppermute | solution.py:367
  108.5 10.0 %collective-permute-start.35 = (s16[1040,128]{1,0:T(8,128)(2,1)S(1)}, s16[1040,128]{1,0:T(8,128)(2,1)S(1)}, u32[]{:S(2)}, u32[]{:S(2)}) collective-permute-start(s16[1040,128]{1,0:T(8,128)(2,1)S(1)} %merge.9.refs_0_), channel_id=1, source_target_pairs={{0,16},{16,32},{32,48},{48,0},{1,17},{17,33},{33,49},{49,1},{2,18}... | collective-permute-start | bytes 798728 | tf_op jit(solution)/shard_map/ppermute | solution.py:367
  112.9 7.9 %collective-permute-start.34 = (s16[1040,128]{1,0:T(8,128)(2,1)S(1)}, s16[1040,128]{1,0:T(8,128)(2,1)S(1)}, u32[]{:S(2)}, u32[]{:S(2)}) collective-permute-start(s16[1040,128]{1,0:T(8,128)(2,1)S(1)} %collective-permute-done.33.refs_2_), channel_id=1, source_target_pairs={{0,64},{64,0},{1,65},{65,1},{2,66},{66,2},{3,67},{67,3},{4,68},{68... | collective-permute-start | bytes 798728 | tf_op jit(solution)/shard_map/ppermute | solution.py:367
  115.7 6.4 %collective-permute-start.32 = (s16[1040,128]{1,0:T(8,128)(2,1)S(1)}, s16[1040,128]{1,0:T(8,128)(2,1)S(1)}, u32[]{:S(2)}, u32[]{:S(2)}) collective-permute-start(s16[1040,128]{1,0:T(8,128)(2,1)S(1)} %collective-permute-done.30.refs_1_), channel_id=1, source_target_pairs={{0,48},{16,0},{32,16},{48,32},{1,49},{17,1},{33,17},{49,33},{2,50}... | collective-permute-start | bytes 798728 | tf_op jit(solution)/shard_map/ppermute | solution.py:367
  118.0 7.6 %collective-permute-start.31 = (s16[1040,128]{1,0:T(8,128)(2,1)S(1)}, s16[1040,128]{1,0:T(8,128)(2,1)S(1)}, u32[]{:S(2)}, u32[]{:S(2)}) collective-permute-start(s16[1040,128]{1,0:T(8,128)(2,1)S(1)} %collective-permute-done.30.refs_1_), channel_id=1, source_target_pairs={{0,16},{16,32},{32,48},{48,0},{1,17},{17,33},{33,49},{49,1},{2,18}... | collective-permute-start | bytes 798728 | tf_op jit(solution)/shard_map/ppermute | solution.py:367

commit v5 on v4

--- a/solution.py
+++ b/solution.py
@@ -22,8 +22,8 @@
 SENT = (7, 5, 4, 3, 2)
 KEPT = (0, 1, 6)
 FIRST = 3
-EARLY = (0, 1, 2, 3)
-LATE = (4, 5, 6, 7)
+EARLY = (0, 1, 2, 3, 6)
+LATE = (4, 5, 7)
 PLACES = 2
 LINES = PLACES + len(HOPS)
 F32 = jnp.float32
@@ -111,13 +111,13 @@
 
     lax.fori_loop(0, chunks, chunk, 0)
     core = info[1]
-    stores = []
-    for n, (out_ref, first) in enumerate(((give_ref, (1 - core) * half), (keep_ref, core * half))):
-        put_blocks(lambda j: acc[first + j].T, half, coded.at[n], steps)
-        stores.append(pltpu.make_async_copy(coded.at[n], out_ref, sem.at[1 + n]))
-        stores[-1].start()
-    for store in stores:
-        store.wait()
+    keep = pltpu.make_async_copy(acc.at[pl.ds(core * half, half)], keep_ref, sem.at[1])
+    keep.start()
+    put_blocks(lambda j: acc[(1 - core) * half + j].T, half, coded, steps)
+    give = pltpu.make_async_copy(coded, give_ref, sem.at[2])
+    give.start()
+    keep.wait()
+    give.wait()
 
 
 def forward(tiles, coords, info, omega, blk_row):
@@ -127,14 +127,14 @@
     coded = jax.ShapeDtypeStruct((half * (width + 1), TILE), I16)
     return pl.pallas_call(
         forward_kernel,
-        out_shape=(coded, coded),
+        out_shape=(jax.ShapeDtypeStruct((half, TILE, width), F32), coded),
         in_specs=[pl.BlockSpec(memory_space=pltpu.SMEM)] * 2 + [pl.BlockSpec(memory_space=pltpu.HBM)] * 2,
         out_specs=[pl.BlockSpec(memory_space=pltpu.HBM)] * 2,
         scratch_shapes=[
             pltpu.VMEM((blk_row, TILE, width), F32),
             pltpu.VMEM(omega.shape, omega.dtype),
             pltpu.VMEM(tiles.shape, tiles.dtype),
-            pltpu.VMEM((2, *coded.shape), I16),
+            pltpu.VMEM(coded.shape, I16),
             pltpu.VMEM((half, TILE), F32),
             pltpu.SemaphoreType.DMA((slots // CHUNK,)),
             pltpu.SemaphoreType.DMA((3,)),
@@ -144,35 +144,34 @@
     )(coords, info, omega, tiles)
 
 
-def plain_kernel(in_ref, out_ref, scale):
-    blocks, width, _ = out_ref.shape
-    scales((in_ref,), scale, blocks * width)
-
-    def body(j, _):
-        part = in_ref[pl.ds(pl.multiple_of(j * width, width), width), :].astype(jnp.int32).astype(F32)
-        out_ref[j] = part * scale[0, pl.ds(j, 1), :]
-        return 0
-
-    lax.fori_loop(0, blocks, body, 0, unroll=8)
-
-
-def plain(coded, width):
-    blocks = coded.shape[0] // (width + 1)
-    return pl.pallas_call(
-        plain_kernel,
-        out_shape=jax.ShapeDtypeStruct((blocks, width, TILE), F32),
-        in_specs=[pl.BlockSpec(memory_space=pltpu.VMEM)],
+def turn_kernel(which, info, in_ref, out_ref):
+    each = out_ref.shape[1]
+    for k, n in enumerate(which):
+        first = info[PLACES + n] * each
+
+        def body(j, _):
+            out_ref[k, j] = in_ref[first + j].T
+            return 0
+
+        lax.fori_loop(0, each, body, 0, unroll=True)
+
+
+def turn(info, blocks, which):
+    count, rows, columns = blocks.shape
+    return pl.pallas_call(
+        functools.partial(turn_kernel, which),
+        out_shape=jax.ShapeDtypeStruct((len(which), count // len(HOPS), columns, rows), F32),
+        in_specs=[pl.BlockSpec(memory_space=pltpu.SMEM), pl.BlockSpec(memory_space=pltpu.VMEM)],
         out_specs=pl.BlockSpec(memory_space=pltpu.VMEM),
-        scratch_shapes=[pltpu.VMEM((1, blocks, TILE), F32)],
         compiler_params=params(14),
-        name="plain",
-    )(coded)
+        name="turn",
+    )(info, blocks)
 
 
 def pair_kernel(which, sent, info, keep_ref, got_ref, *refs):
     outs, (scale, steps) = refs[:-2], refs[-2:]
-    blocks, width, _ = keep_ref.shape
-    each = blocks // len(HOPS)
+    _, each, width, _ = keep_ref.shape
+    blocks = each * len(HOPS)
     scales((got_ref,), scale, blocks * width)
     for k, (n, out_ref) in enumerate(zip(which, outs)):
         first = info[PLACES + n] * each
@@ -180,7 +179,7 @@
         def read(j):
             b = first + j
             got = got_ref[pl.ds(pl.multiple_of(b * width, width), width), :].astype(jnp.int32).astype(F32)
-            return keep_ref[b] + got * scale[0, pl.ds(b, 1), :]
+            return keep_ref[k, j] + got * scale[0, pl.ds(b, 1), :]
 
         if k < sent:
             put_blocks(read, each, out_ref, steps)
@@ -194,8 +193,8 @@
 
 
 def pair(info, keep, got, which, sent):
-    blocks, width, _ = keep.shape
-    each = blocks // len(HOPS)
+    _, each, width, _ = keep.shape
+    blocks = each * len(HOPS)
     coded = jax.ShapeDtypeStruct((each * width + each, TILE), I16)
     return pl.pallas_call(
         functools.partial(pair_kernel, which, sent),
@@ -411,12 +410,12 @@
     info = jnp.stack([tile_counts[0, 0], core, *numbers(*CHIPS), *lines])
     keep, give = forward(blocks, coords, info, omega, blk_row)
     got = shift(give, "core", 1)
-    keep = plain(keep, width)
-    sent = pair(info, keep, got, SENT[:FIRST], FIRST)
-    rest = pair(info, keep, got, SENT[FIRST:] + KEPT, len(SENT) - FIRST)
+    others = SENT[FIRST:] + KEPT
+    sent = pair(info, turn(info, keep, SENT[:FIRST]), got, SENT[:FIRST], FIRST)
+    rest = pair(info, turn(info, keep, others), got, others, len(SENT) - FIRST)
     sent, kept = sent + rest[: len(SENT) - FIRST], rest[len(SENT) - FIRST :]
     mine = gather(scatter(sent, kept, *CHIPS, share), *CHIPS, True)
-    early = lax.optimization_barrier([mine[n] for n in EARLY + (6,)])
+    early = lax.optimization_barrier([mine[n] for n in EARLY])
     given = [*early[:-1], mine[4], mine[5], early[-1], mine[7]]
     theirs = [shift(value, "core", 1) for value in given]
     out = backward(blocks, coords, info, mine + theirs, blk_col)

time: 129 us -> 126 us (0.977)
  waiting for transfers between devices: 51.3 us -> 34.7 us
  starting transfers between devices: 49.4 us -> 58.7 us
  Pallas kernels: 23.9 us -> 27.5 us
  local copies, waits for them, and re-layouts: 2.19 us -> 4.04 us
    ppermute x37, waiting for transfers between devices: 51.3 us -> 34.7 us  [shift(): lax.ppermute(value, axis, [(i, (i + by) % count) for i in range(count)])]
    ppermute x37, starting transfers between devices: 49.4 us -> 58.7 us  [shift(): lax.ppermute(value, axis, [(i, (i + by) % count) for i in range(count)])]
    pallas_call x2 -> x3, Pallas kernels: 11.4 us -> 13.6 us  [the longest x1 10.3 us: forward(): pl.pallas_call(forward_kernel, out_shape=(jax.ShapeDtypeStruct((half, TIL...]
    unnamed x6 -> x8, local copies, waits for them, and re-layouts: 1.61 us -> 3.39 us
    pallas_call x1, Pallas kernels: 4.79 us -> 6.16 us  [backward(): pl.pallas_call(backward_kernel, out_shape=[coded] * len(SENT) + [plain] *...]
  transfers between devices with their start and end apart: 37 -> 37, of which waited for: 25 -> 21; matrix products, arithmetic and copies ran while one was open for 0% -> 0% of each run, Pallas kernels for 4% -> 6%
where the time goes in v5:
time: 126 us
  starting transfers between devices  58.7 us (47%)
  waiting for transfers between devices  34.7 us (28%)
  Pallas kernels  27.5 us (22%)
  local copies, waits for them, and re-layouts  4.04 us (3%)
    ppermute x37, starting transfers between devices, shift(): lax.ppermute(value, axis, [(i, (i + by) % count) for i in range(count)])  58.7 us
    ppermute x37, waiting for transfers between devices, shift(): lax.ppermute(value, axis, [(i, (i + by) % count) for i in range(count)])  34.7 us
    pallas_call x1, Pallas kernels, forward(): pl.pallas_call(forward_kernel, out_shape=(jax.ShapeDtypeStruct((half, TIL...  10.3 us
    pallas_call x1, Pallas kernels, backward(): pl.pallas_call(backward_kernel, out_shape=[coded] * len(SENT) + [plain] *...  6.16 us
    pallas_call x2, Pallas kernels, spread(): pl.pallas_call(functools.partial(spread_kernel, which), out_shape=jax.Sha...  3.88 us
    unnamed x8, local copies, waits for them, and re-layouts  3.39 us
    pallas_call x2, Pallas kernels, turn(): pl.pallas_call(functools.partial(turn_kernel, which), out_shape=jax.Shape...  3.33 us
  transfers between devices with their start and end apart: 37, of which 21 were waited for; matrix products, arithmetic and copies ran while one was open for 0% of the time, Pallas kernels for 6%

profile of v5, /device:TPU:0, one launch (start us, length us, event | category | flops | bytes accessed | tf_op | source)
XLA Modules:
  0.0 125.8 jit_solution(5609914810212904416)
XLA Ops:
  0.7 0.6 stack.71.info
  1.3 10.3 %forward.1 = (f32[128,128,64]{2,1,0:T(8,128)}, s16[8320,128]{1,0:T(8,128)(2,1)}) custom-call(s32[2,512]{1,0:T(2,128)} %bitcast.23, s32[18]{0:T(128)} %stack.71.info, bf16[64,16384]{1,0:T(8,128)(2,1)} %omega_ref.1, bf16[512,128,128]{2,1,0:T(8,128)(2,1)} %bitcast.25), custom_call_target="tpu_custom_call" | custom-call | tf_op jit(solution)/shard_map/forward/pallas_call | solution.py:128
  11.7 3.4 %copy-done = f32[128,128,64]{2,1,0:T(8,128)S(1)} copy-done((f32[128,128,64]{2,1,0:T(8,128)S(1)}, f32[128,128,64]{2,1,0:T(8,128)}, u32[]{:S(2)}) %copy-start) | copy-done | bytes 4194328
  15.1 1.4 %turn.3.keep_ref = f32[3,16,64,128]{3,2,1,0:T(8,128)S(1)} custom-call(s32[18]{0:T(128)S(1)} %copy-done.2, f32[128,128,64]{2,1,0:T(8,128)S(1)} %copy-done), custom_call_target="tpu_custom_call" | custom-call | tf_op jit(solution)/shard_map/turn/pallas_call | solution.py:161
  16.5 1.1 pair.3
  17.6 1.7 %collective-permute-start.5 = (s16[1040,128]{1,0:T(8,128)(2,1)S(1)}, s16[1040,128]{1,0:T(8,128)(2,1)S(1)}, u32[]{:S(2)}, u32[]{:S(2)}) collective-permute-start(s16[1040,128]{1,0:T(8,128)(2,1)S(1)} %get-tuple-element.38), channel_id=1, source_target_pairs={{0,4},{4,8},{8,12},{12,0},{1,5},{5,9},{9,13},{13,1},{2,6},{6,10},{... | collective-permute-start | bytes 798728 | tf_op jit(solution)/shard_map/ppermute | solution.py:366
  19.2 4.4 %collective-permute-start.6 = (s16[1040,128]{1,0:T(8,128)(2,1)S(1)}, s16[1040,128]{1,0:T(8,128)(2,1)S(1)}, u32[]{:S(2)}, u32[]{:S(2)}) collective-permute-start(s16[1040,128]{1,0:T(8,128)(2,1)S(1)} %get-tuple-element.39), channel_id=1, source_target_pairs={{0,12},{4,0},{8,4},{12,8},{1,13},{5,1},{9,5},{13,9},{2,14},{6,2},{... | collective-permute-start | bytes 798728 | tf_op jit(solution)/shard_map/ppermute | solution.py:366
  23.7 1.4 %collective-permute-start.3 = (s16[1040,128]{1,0:T(8,128)(2,1)S(1)}, s16[1040,128]{1,0:T(8,128)(2,1)S(1)}, u32[]{:S(2)}, u32[]{:S(2)}) collective-permute-start(s16[1040,128]{1,0:T(8,128)(2,1)S(1)} %get-tuple-element.36), channel_id=1, source_target_pairs={{0,2},{2,0},{1,3},{3,1},{4,6},{6,4},{5,7},{7,5},{8,10},{10,8},{9,1... | collective-permute-start | bytes 798728 | tf_op jit(solution)/shard_map/ppermute | solution.py:366
  25.0 1.9 %turn.2.keep_ref = f32[5,16,64,128]{3,2,1,0:T(8,128)S(1)} custom-call(s32[18]{0:T(128)S(1)} %copy-done.2, f32[128,128,64]{2,1,0:T(8,128)S(1)} %copy-done.1), custom_call_target="tpu_custom_call" | custom-call | tf_op jit(solution)/shard_map/turn/pallas_call | solution.py:161
  27.0 1.1 pair.2
  28.1 0.4 collective-permute-start.1
  28.5 2.9 %collective-permute-start.2 = (s16[1040,128]{1,0:T(8,128)(2,1)S(1)}, s16[1040,128]{1,0:T(8,128)(2,1)S(1)}, u32[]{:S(2)}, u32[]{:S(2)}) collective-permute-start(s16[1040,128]{1,0:T(8,128)(2,1)S(1)} %get-tuple-element.34), channel_id=1, source_target_pairs={{0,12},{4,0},{8,4},{12,8},{1,13},{5,1},{9,5},{13,9},{2,14},{6,2},{... | collective-permute-start | bytes 798728 | tf_op jit(solution)/shard_map/ppermute | solution.py:366
  31.4 0.3 merge.6
  31.7 1.2 collective-permute-start.7
  33.1 2.1 %collective-permute-start.4 = (s16[1040,128]{1,0:T(8,128)(2,1)S(1)}, s16[1040,128]{1,0:T(8,128)(2,1)S(1)}, u32[]{:S(2)}, u32[]{:S(2)}) collective-permute-start(s16[1040,128]{1,0:T(8,128)(2,1)S(1)} %merge.5), channel_id=1, source_target_pairs={{0,8},{4,12},{8,0},{12,4},{1,9},{5,13},{9,1},{13,5},{2,10},{6,14},... | collective-permute-start | bytes 798728 | tf_op jit(solution)/shard_map/ppermute | solution.py:366
  35.2 2.8 %collective-permute-done.1.refs_0_ = s16[1040,128]{1,0:T(8,128)(2,1)S(1)} collective-permute-done((s16[1040,128]{1,0:T(8,128)(2,1)S(1)}, s16[1040,128]{1,0:T(8,128)(2,1)S(1)}, u32[]{:S(2)}, u32[]{:S(2)}) %collective-permute-start.1) | collective-permute-done | bytes 266272 | tf_op jit(solution)/shard_map/ppermute | solution.py:366
  38.0 4.2 %collective-permute-done.2.refs_1_ = s16[1040,128]{1,0:T(8,128)(2,1)S(1)} collective-permute-done((s16[1040,128]{1,0:T(8,128)(2,1)S(1)}, s16[1040,128]{1,0:T(8,128)(2,1)S(1)}, u32[]{:S(2)}, u32[]{:S(2)}) %collective-permute-start.2) | collective-permute-done | bytes 266272 | tf_op jit(solution)/shard_map/ppermute | solution.py:366
  42.2 1.1 collective-permute-done.4.refs_2_
  43.2 0.3 share.1.refs_0_
  43.5 1.0 collective-permute-start.8
  44.5 1.5 %collective-permute-start.13 = (bf16[16,64,128]{2,1,0:T(8,128)(2,1)S(1)}, bf16[16,64,128]{2,1,0:T(8,128)(2,1)S(1)}, u32[]{:S(2)}, u32[]{:S(2)}) collective-permute-start(bf16[16,64,128]{2,1,0:T(8,128)(2,1)S(1)} %share.1.refs_0_), channel_id=1, source_target_pairs={{0,8},{4,12},{8,0},{12,4},{1,9},{5,13},{9,1},{13,5},{2,10},{6,14},... | collective-permute-start | bytes 786440 | tf_op jit(solution)/shard_map/ppermute | solution.py:366
  46.0 2.2 %collective-permute-start.9 = (bf16[16,64,128]{2,1,0:T(8,128)(2,1)S(1)}, bf16[16,64,128]{2,1,0:T(8,128)(2,1)S(1)}, u32[]{:S(2)}, u32[]{:S(2)}) collective-permute-start(bf16[16,64,128]{2,1,0:T(8,128)(2,1)S(1)} %share.1.refs_0_), channel_id=1, source_target_pairs={{0,4},{4,8},{8,12},{12,0},{1,5},{5,9},{9,13},{13,1},{2,6},{6,10},{... | collective-permute-start | bytes 786440 | tf_op jit(solution)/shard_map/ppermute | solution.py:366
  48.2 2.5 %collective-permute-done.8.refs_1_ = bf16[16,64,128]{2,1,0:T(8,128)(2,1)S(1)} collective-permute-done((bf16[16,64,128]{2,1,0:T(8,128)(2,1)S(1)}, bf16[16,64,128]{2,1,0:T(8,128)(2,1)S(1)}, u32[]{:S(2)}, u32[]{:S(2)}) %collective-permute-start.8) | collective-permute-done | bytes 262176 | tf_op jit(solution)/shard_map/ppermute | solution.py:366
  50.8 1.8 %collective-permute-start.10 = (bf16[16,64,128]{2,1,0:T(8,128)(2,1)S(1)}, bf16[16,64,128]{2,1,0:T(8,128)(2,1)S(1)}, u32[]{:S(2)}, u32[]{:S(2)}) collective-permute-start(bf16[16,64,128]{2,1,0:T(8,128)(2,1)S(1)} %share.1.refs_0_), channel_id=1, source_target_pairs={{0,12},{4,0},{8,4},{12,8},{1,13},{5,1},{9,5},{13,9},{2,14},{6,2},{... | collective-permute-start | bytes 786440 | tf_op jit(solution)/shard_map/ppermute | solution.py:366
  52.8 3.0 %collective-permute-start.12 = (bf16[16,64,128]{2,1,0:T(8,128)(2,1)S(1)}, bf16[16,64,128]{2,1,0:T(8,128)(2,1)S(1)}, u32[]{:S(2)}, u32[]{:S(2)}) collective-permute-start(bf16[16,64,128]{2,1,0:T(8,128)(2,1)S(1)} %collective-permute-done.8.refs_1_), channel_id=1, source_target_pairs={{0,12},{4,0},{8,4},{12,8},{1,13},{5,1},{9,5},{13,9},{2,14},{6,2},{... | collective-permute-start | bytes 786440 | tf_op jit(solution)/shard_map/ppermute | solution.py:366
  55.8 1.4 %collective-permute-start.14 = (bf16[16,64,128]{2,1,0:T(8,128)(2,1)S(1)}, bf16[16,64,128]{2,1,0:T(8,128)(2,1)S(1)}, u32[]{:S(2)}, u32[]{:S(2)}) collective-permute-start(bf16[16,64,128]{2,1,0:T(8,128)(2,1)S(1)} %collective-permute-done.13.refs_6_), channel_id=1, source_target_pairs={{0,2},{2,0},{1,3},{3,1},{4,6},{6,4},{5,7},{7,5},{8,10},{10,8},{9,1... | collective-permute-start | bytes 786440 | tf_op jit(solution)/shard_map/ppermute | solution.py:366
  57.3 1.4 %collective-permute-done.9.refs_2_ = bf16[16,64,128]{2,1,0:T(8,128)(2,1)S(1)} collective-permute-done((bf16[16,64,128]{2,1,0:T(8,128)(2,1)S(1)}, bf16[16,64,128]{2,1,0:T(8,128)(2,1)S(1)}, u32[]{:S(2)}, u32[]{:S(2)}) %collective-permute-start.9) | collective-permute-done | bytes 262176 | tf_op jit(solution)/shard_map/ppermute | solution.py:366
  58.6 1.4 %collective-permute-done.10.refs_3_ = bf16[16,64,128]{2,1,0:T(8,128)(2,1)S(1)} collective-permute-done((bf16[16,64,128]{2,1,0:T(8,128)(2,1)S(1)}, bf16[16,64,128]{2,1,0:T(8,128)(2,1)S(1)}, u32[]{:S(2)}, u32[]{:S(2)}) %collective-permute-start.10) | collective-permute-done | bytes 262176 | tf_op jit(solution)/shard_map/ppermute | solution.py:366
  60.0 0.5 collective-permute-start.16
  60.5 3.6 %collective-permute-done.11.refs_4_ = bf16[16,64,128]{2,1,0:T(8,128)(2,1)S(1)} collective-permute-done((bf16[16,64,128]{2,1,0:T(8,128)(2,1)S(1)}, bf16[16,64,128]{2,1,0:T(8,128)(2,1)S(1)}, u32[]{:S(2)}, u32[]{:S(2)}) %collective-permute-start.11) | collective-permute-done | bytes 262176 | tf_op jit(solution)/shard_map/ppermute | solution.py:366
  64.1 0.5 collective-permute-start.18
  64.7 0.4 collective-permute-start.19
  65.3 0.4 collective-permute-done.17.refs_10_
  65.8 0.2 collective-permute-done.18.refs_11_
  66.1 0.4 collective-permute-done.21.refs_14_
  66.4 0.4 collective-permute-done.19.refs_12_
  66.8 0.4 collective-permute-done.20.refs_13_
  67.2 0.4 collective-permute-done.22.refs_15_
  67.6 6.2 %backward.1 = (s16[1040,128]{1,0:T(8,128)(2,1)S(1)}, s16[1040,128]{1,0:T(8,128)(2,1)S(1)}, s16[1040,128]{1,0:T(8,128)(2,1)S(1)}, s16[1040,128]{1,0:T(8,128)(2,1)...) custom-call(s32[2,512]{1,0:T(2,128)S(1)} %bitcast.24, ...), custom_call_target="tpu_custom_call" | custom-call | tf_op jit(solution)/shard_map/backward/pallas_call | solution.py:306
  73.7 3.1 %collective-permute-start.27 = (s16[1040,128]{1,0:T(8,128)(2,1)S(1)}, s16[1040,128]{1,0:T(8,128)(2,1)S(1)}, u32[]{:S(2)}, u32[]{:S(2)}) collective-permute-start(s16[1040,128]{1,0:T(8,128)(2,1)S(1)} %get-tuple-element.53), channel_id=1, source_target_pairs={{0,16},{16,32},{32,48},{48,0},{1,17},{17,33},{33,49},{49,1},{2,18}... | collective-permute-start | bytes 798728 | tf_op jit(solution)/shard_map/ppermute | solution.py:366
  76.8 1.0 collective-permute-start.28
  77.9 4.6 %collective-permute-start.25 = (s16[1040,128]{1,0:T(8,128)(2,1)S(1)}, s16[1040,128]{1,0:T(8,128)(2,1)S(1)}, u32[]{:S(2)}, u32[]{:S(2)}) collective-permute-start(s16[1040,128]{1,0:T(8,128)(2,1)S(1)} %get-tuple-element.51), channel_id=1, source_target_pairs={{0,64},{64,0},{1,65},{65,1},{2,66},{66,2},{3,67},{67,3},{4,68},{68... | collective-permute-start | bytes 798728 | tf_op jit(solution)/shard_map/ppermute | solution.py:366
  82.4 2.0 %collective-permute-start.23 = (s16[1040,128]{1,0:T(8,128)(2,1)S(1)}, s16[1040,128]{1,0:T(8,128)(2,1)S(1)}, u32[]{:S(2)}, u32[]{:S(2)}) collective-permute-start(s16[1040,128]{1,0:T(8,128)(2,1)S(1)} %get-tuple-element.48), channel_id=1, source_target_pairs={{0,16},{16,32},{32,48},{48,0},{1,17},{17,33},{33,49},{49,1},{2,18}... | collective-permute-start | bytes 798728 | tf_op jit(solution)/shard_map/ppermute | solution.py:366
  84.5 1.2 collective-permute-start.24
  85.7 0.3 merge.8
  85.9 6.1 %collective-permute-start.29 = (s16[1040,128]{1,0:T(8,128)(2,1)S(1)}, s16[1040,128]{1,0:T(8,128)(2,1)S(1)}, u32[]{:S(2)}, u32[]{:S(2)}) collective-permute-start(s16[1040,128]{1,0:T(8,128)(2,1)S(1)} %merge.8), channel_id=1, source_target_pairs={{0,64},{64,0},{1,65},{65,1},{2,66},{66,2},{3,67},{67,3},{4,68},{68... | collective-permute-start | bytes 798728 | tf_op jit(solution)/shard_map/ppermute | solution.py:366
  92.3 0.4 collective-permute-start.26
  92.8 4.0 %collective-permute-done.29.refs_3_ = s16[1040,128]{1,0:T(8,128)(2,1)S(1)} collective-permute-done((s16[1040,128]{1,0:T(8,128)(2,1)S(1)}, s16[1040,128]{1,0:T(8,128)(2,1)S(1)}, u32[]{:S(2)}, u32[]{:S(2)}) %collective-permute-start.29) | collective-permute-done | bytes 266272 | tf_op jit(solution)/shard_map/ppermute | solution.py:366
  96.8 3.7 %collective-permute-done.26.refs_2_ = s16[1040,128]{1,0:T(8,128)(2,1)S(1)} collective-permute-done((s16[1040,128]{1,0:T(8,128)(2,1)S(1)}, s16[1040,128]{1,0:T(8,128)(2,1)S(1)}, u32[]{:S(2)}, u32[]{:S(2)}) %collective-permute-start.26) | collective-permute-done | bytes 266272 | tf_op jit(solution)/shard_map/ppermute | solution.py:366
  100.5 0.4 merge.9.refs_0_
  100.9 2.8 %collective-permute-start.30 = (s16[1040,128]{1,0:T(8,128)(2,1)S(1)}, s16[1040,128]{1,0:T(8,128)(2,1)S(1)}, u32[]{:S(2)}, u32[]{:S(2)}) collective-permute-start(s16[1040,128]{1,0:T(8,128)(2,1)S(1)} %merge.9.refs_0_), channel_id=1, source_target_pairs={{0,64},{64,0},{1,65},{65,1},{2,66},{66,2},{3,67},{67,3},{4,68},{68... | collective-permute-start | bytes 798728 | tf_op jit(solution)/shard_map/ppermute | solution.py:366
  103.7 1.4 %collective-permute-start.33 = (s16[1040,128]{1,0:T(8,128)(2,1)S(1)}, s16[1040,128]{1,0:T(8,128)(2,1)S(1)}, u32[]{:S(2)}, u32[]{:S(2)}) collective-permute-start(s16[1040,128]{1,0:T(8,128)(2,1)S(1)} %merge.9.refs_0_), channel_id=1, source_target_pairs={{0,32},{16,48},{32,0},{48,16},{1,33},{17,49},{33,1},{49,17},{2,34}... | collective-permute-start | bytes 798728 | tf_op jit(solution)/shard_map/ppermute | solution.py:366
  105.1 1.0 collective-permute-start.35
  106.0 2.3 %collective-permute-start.36 = (s16[1040,128]{1,0:T(8,128)(2,1)S(1)}, s16[1040,128]{1,0:T(8,128)(2,1)S(1)}, u32[]{:S(2)}, u32[]{:S(2)}) collective-permute-start(s16[1040,128]{1,0:T(8,128)(2,1)S(1)} %merge.9.refs_0_), channel_id=1, source_target_pairs={{0,48},{16,0},{32,16},{48,32},{1,49},{17,1},{33,17},{49,33},{2,50}... | collective-permute-start | bytes 798728 | tf_op jit(solution)/shard_map/ppermute | solution.py:366
  108.3 1.5 %collective-permute-done.30.refs_1_ = s16[1040,128]{1,0:T(8,128)(2,1)S(1)} collective-permute-done((s16[1040,128]{1,0:T(8,128)(2,1)S(1)}, s16[1040,128]{1,0:T(8,128)(2,1)S(1)}, u32[]{:S(2)}, u32[]{:S(2)}) %collective-permute-start.30) | collective-permute-done | bytes 266272 | tf_op jit(solution)/shard_map/ppermute | solution.py:366
  109.8 1.2 collective-permute-start.31
  111.0 3.1 %collective-permute-start.32 = (s16[1040,128]{1,0:T(8,128)(2,1)S(1)}, s16[1040,128]{1,0:T(8,128)(2,1)S(1)}, u32[]{:S(2)}, u32[]{:S(2)}) collective-permute-start(s16[1040,128]{1,0:T(8,128)(2,1)S(1)} %collective-permute-done.30.refs_1_), channel_id=1, source_target_pairs={{0,48},{16,0},{32,16},{48,32},{1,49},{17,1},{33,17},{49,33},{2,50}... | collective-permute-start | bytes 798728 | tf_op jit(solution)/shard_map/ppermute | solution.py:366
  114.1 0.4 collective-permute-done.33.refs_4_
  114.5 1.5 %collective-permute-start.34 = (s16[1040,128]{1,0:T(8,128)(2,1)S(1)}, s16[1040,128]{1,0:T(8,128)(2,1)S(1)}, u32[]{:S(2)}, u32[]{:S(2)}) collective-permute-start(s16[1040,128]{1,0:T(8,128)(2,1)S(1)} %collective-permute-done.33.refs_4_), channel_id=1, source_target_pairs={{0,64},{64,0},{1,65},{65,1},{2,66},{66,2},{3,67},{67,3},{4,68},{68... | collective-permute-start | bytes 798728 | tf_op jit(solution)/shard_map/ppermute | solution.py:366
  116.0 2.3 %collective-permute-done.35.refs_2_ = s16[1040,128]{1,0:T(8,128)(2,1)S(1)} collective-permute-done((s16[1040,128]{1,0:T(8,128)(2,1)S(1)}, s16[1040,128]{1,0:T(8,128)(2,1)S(1)}, u32[]{:S(2)}, u32[]{:S(2)}) %collective-permute-start.35) | collective-permute-done | bytes 266272 | tf_op jit(solution)/shard_map/ppermute | solution.py:366
  118.3 0.7 collective-permute-done.36.refs_3_
  119.1 2.1 %spread.2.refs_3_ = f32[64,16384]{1,0:T(8,128)} custom-call(s32[18]{0:T(128)S(1)} %copy-done.2, s16[1040,128]{1,0:T(8,128)(2,1)S(1)} %merge.9.refs_0_, s16[1040,128]{1,0:T(8,128)(2,1)S(1)} %collective-permute-done.30.refs_1_, s16[1040,128]{1,0:T(8,128)(2,1)S(1)} %collective-permute-done.35.refs_2_, s16[1040,128]{1,0:T(8,128)(2,1)S(1)} %collective-permute-done.36.refs_3_, ...), custom_call_target="tpu_custom_call" | custom-call | tf_op jit(solution)/shard_map/spread/pallas_call | solution.py:348
  121.2 2.7 %collective-permute-done.31.refs_0_ = s16[1040,128]{1,0:T(8,128)(2,1)S(1)} collective-permute-done((s16[1040,128]{1,0:T(8,128)(2,1)S(1)}, s16[1040,128]{1,0:T(8,128)(2,1)S(1)}, u32[]{:S(2)}, u32[]{:S(2)}) %collective-permute-start.31) | collective-permute-done | bytes 266272 | tf_op jit(solution)/shard_map/ppermute | solution.py:366
  123.9 1.8 %spread.3 = f32[64,16384]{1,0:T(8,128)} custom-call(s32[18]{0:T(128)S(1)} %copy-done.2, s16[1040,128]{1,0:T(8,128)(2,1)S(1)} %collective-permute-done.31.refs_0_, s16[1040,128]{1,0:T(8,128)(2,1)S(1)} %collective-permute-done.32.refs_1_, s16[1040,128]{1,0:T(8,128)(2,1)S(1)} %collective-permute-done.34.refs_2_, ...), custom_call_target="tpu_custom_call", output_to_operand_aliasing={{}: (4, {})} | custom-call | tf_op jit(solution)/shard_map/spread/pallas_call | solution.py:348
  (33 shorter events, 1.2 us)
Async XLA Ops:
  1.3 10.4 %copy-start.2 = (s32[18]{0:T(128)S(1)}, s32[18]{0:T(128)}, u32[]{:S(2)}) copy-start(s32[18]{0:T(128)} %stack.71.info) | copy-start | bytes 220
  11.6 4.9 %collective-permute-start = (s16[8320,128]{1,0:T(8,128)(2,1)}, s16[8320,128]{1,0:T(8,128)(2,1)S(1)}, u32[]{:S(2)}, u32[]{:S(2)}) collective-permute-start(s16[8320,128]{1,0:T(8,128)(2,1)} %get-tuple-element.31), channel_id=1, source_target_pairs={{0,1},{1,0},{2,3},{3,2},{4,5},{5,4},{6,7},{7,6},{8,9},{9,8},{10,11... | collective-permute-start | bytes 6389768 | tf_op jit(solution)/shard_map/ppermute | solution.py:366
  11.7 3.4 %copy-start = (f32[128,128,64]{2,1,0:T(8,128)S(1)}, f32[128,128,64]{2,1,0:T(8,128)}, u32[]{:S(2)}) copy-start(f32[128,128,64]{2,1,0:T(8,128)} %get-tuple-element.30.in_ref) | copy-start | bytes 12582916
  15.1 9.9 %copy-start.1 = (f32[128,128,64]{2,1,0:T(8,128)S(1)}, f32[128,128,64]{2,1,0:T(8,128)}, u32[]{:S(2)}) copy-start(f32[128,128,64]{2,1,0:T(8,128)} %get-tuple-element.30.in_ref) | copy-start | bytes 12582916
  17.6 13.8 %collective-permute-start.5 = (s16[1040,128]{1,0:T(8,128)(2,1)S(1)}, s16[1040,128]{1,0:T(8,128)(2,1)S(1)}, u32[]{:S(2)}, u32[]{:S(2)}) collective-permute-start(s16[1040,128]{1,0:T(8,128)(2,1)S(1)} %get-tuple-element.38), channel_id=1, source_target_pairs={{0,4},{4,8},{8,12},{12,0},{1,5},{5,9},{9,13},{13,1},{2,6},{6,10},{... | collective-permute-start | bytes 798728 | tf_op jit(solution)/shard_map/ppermute | solution.py:366
  19.2 12.2 %collective-permute-start.6 = (s16[1040,128]{1,0:T(8,128)(2,1)S(1)}, s16[1040,128]{1,0:T(8,128)(2,1)S(1)}, u32[]{:S(2)}, u32[]{:S(2)}) collective-permute-start(s16[1040,128]{1,0:T(8,128)(2,1)S(1)} %get-tuple-element.39), channel_id=1, source_target_pairs={{0,12},{4,0},{8,4},{12,8},{1,13},{5,1},{9,5},{13,9},{2,14},{6,2},{... | collective-permute-start | bytes 798728 | tf_op jit(solution)/shard_map/ppermute | solution.py:366
  23.7 9.2 %collective-permute-start.3 = (s16[1040,128]{1,0:T(8,128)(2,1)S(1)}, s16[1040,128]{1,0:T(8,128)(2,1)S(1)}, u32[]{:S(2)}, u32[]{:S(2)}) collective-permute-start(s16[1040,128]{1,0:T(8,128)(2,1)S(1)} %get-tuple-element.36), channel_id=1, source_target_pairs={{0,2},{2,0},{1,3},{3,1},{4,6},{6,4},{5,7},{7,5},{8,10},{10,8},{9,1... | collective-permute-start | bytes 798728 | tf_op jit(solution)/shard_map/ppermute | solution.py:366
  28.1 39.5 %copy-start.3 = (s32[1,1,512,2]{2,3,1,0:T(2,128)S(1)}, s32[1,1,512,2]{2,3,1,0:T(2,128)}, u32[]{:S(2)}) copy-start(s32[1,1,512,2]{2,3,1,0:T(2,128)} %param.5) | copy-start | bytes 12292
  28.1 9.9 %collective-permute-start.1 = (s16[1040,128]{1,0:T(8,128)(2,1)S(1)}, s16[1040,128]{1,0:T(8,128)(2,1)S(1)}, u32[]{:S(2)}, u32[]{:S(2)}) collective-permute-start(s16[1040,128]{1,0:T(8,128)(2,1)S(1)} %get-tuple-element.33), channel_id=1, source_target_pairs={{0,4},{4,8},{8,12},{12,0},{1,5},{5,9},{9,13},{13,1},{2,6},{6,10},{... | collective-permute-start | bytes 798728 | tf_op jit(solution)/shard_map/ppermute | solution.py:366
  28.5 13.6 %collective-permute-start.2 = (s16[1040,128]{1,0:T(8,128)(2,1)S(1)}, s16[1040,128]{1,0:T(8,128)(2,1)S(1)}, u32[]{:S(2)}, u32[]{:S(2)}) collective-permute-start(s16[1040,128]{1,0:T(8,128)(2,1)S(1)} %get-tuple-element.34), channel_id=1, source_target_pairs={{0,12},{4,0},{8,4},{12,8},{1,13},{5,1},{9,5},{13,9},{2,14},{6,2},{... | collective-permute-start | bytes 798728 | tf_op jit(solution)/shard_map/ppermute | solution.py:366
  31.7 10.5 %collective-permute-start.7 = (s16[1040,128]{1,0:T(8,128)(2,1)S(1)}, s16[1040,128]{1,0:T(8,128)(2,1)S(1)}, u32[]{:S(2)}, u32[]{:S(2)}) collective-permute-start(s16[1040,128]{1,0:T(8,128)(2,1)S(1)} %merge.6), channel_id=1, source_target_pairs={{0,2},{2,0},{1,3},{3,1},{4,6},{6,4},{5,7},{7,5},{8,10},{10,8},{9,1... | collective-permute-start | bytes 798728 | tf_op jit(solution)/shard_map/ppermute | solution.py:366
  33.1 10.2 %collective-permute-start.4 = (s16[1040,128]{1,0:T(8,128)(2,1)S(1)}, s16[1040,128]{1,0:T(8,128)(2,1)S(1)}, u32[]{:S(2)}, u32[]{:S(2)}) collective-permute-start(s16[1040,128]{1,0:T(8,128)(2,1)S(1)} %merge.5), channel_id=1, source_target_pairs={{0,8},{4,12},{8,0},{12,4},{1,9},{5,13},{9,1},{13,5},{2,10},{6,14},... | collective-permute-start | bytes 798728 | tf_op jit(solution)/shard_map/ppermute | solution.py:366
  43.5 7.2 %collective-permute-start.8 = (bf16[16,64,128]{2,1,0:T(8,128)(2,1)S(1)}, bf16[16,64,128]{2,1,0:T(8,128)(2,1)S(1)}, u32[]{:S(2)}, u32[]{:S(2)}) collective-permute-start(bf16[16,64,128]{2,1,0:T(8,128)(2,1)S(1)} %share.1.refs_0_), channel_id=1, source_target_pairs={{0,2},{2,0},{1,3},{3,1},{4,6},{6,4},{5,7},{7,5},{8,10},{10,8},{9,1... | collective-permute-start | bytes 786440 | tf_op jit(solution)/shard_map/ppermute | solution.py:366
  44.5 11.3 %collective-permute-start.13 = (bf16[16,64,128]{2,1,0:T(8,128)(2,1)S(1)}, bf16[16,64,128]{2,1,0:T(8,128)(2,1)S(1)}, u32[]{:S(2)}, u32[]{:S(2)}) collective-permute-start(bf16[16,64,128]{2,1,0:T(8,128)(2,1)S(1)} %share.1.refs_0_), channel_id=1, source_target_pairs={{0,8},{4,12},{8,0},{12,4},{1,9},{5,13},{9,1},{13,5},{2,10},{6,14},... | collective-permute-start | bytes 786440 | tf_op jit(solution)/shard_map/ppermute | solution.py:366
  46.0 12.6 %collective-permute-start.9 = (bf16[16,64,128]{2,1,0:T(8,128)(2,1)S(1)}, bf16[16,64,128]{2,1,0:T(8,128)(2,1)S(1)}, u32[]{:S(2)}, u32[]{:S(2)}) collective-permute-start(bf16[16,64,128]{2,1,0:T(8,128)(2,1)S(1)} %share.1.refs_0_), channel_id=1, source_target_pairs={{0,4},{4,8},{8,12},{12,0},{1,5},{5,9},{9,13},{13,1},{2,6},{6,10},{... | collective-permute-start | bytes 786440 | tf_op jit(solution)/shard_map/ppermute | solution.py:366
  50.8 9.2 %collective-permute-start.10 = (bf16[16,64,128]{2,1,0:T(8,128)(2,1)S(1)}, bf16[16,64,128]{2,1,0:T(8,128)(2,1)S(1)}, u32[]{:S(2)}, u32[]{:S(2)}) collective-permute-start(bf16[16,64,128]{2,1,0:T(8,128)(2,1)S(1)} %share.1.refs_0_), channel_id=1, source_target_pairs={{0,12},{4,0},{8,4},{12,8},{1,13},{5,1},{9,5},{13,9},{2,14},{6,2},{... | collective-permute-start | bytes 786440 | tf_op jit(solution)/shard_map/ppermute | solution.py:366
  52.6 11.5 %collective-permute-start.11 = (bf16[16,64,128]{2,1,0:T(8,128)(2,1)S(1)}, bf16[16,64,128]{2,1,0:T(8,128)(2,1)S(1)}, u32[]{:S(2)}, u32[]{:S(2)}) collective-permute-start(bf16[16,64,128]{2,1,0:T(8,128)(2,1)S(1)} %collective-permute-done.8.refs_1_), channel_id=1, source_target_pairs={{0,4},{4,8},{8,12},{12,0},{1,5},{5,9},{9,13},{13,1},{2,6},{6,10},{... | collective-permute-start | bytes 786440 | tf_op jit(solution)/shard_map/ppermute | solution.py:366
  52.8 11.3 %collective-permute-start.12 = (bf16[16,64,128]{2,1,0:T(8,128)(2,1)S(1)}, bf16[16,64,128]{2,1,0:T(8,128)(2,1)S(1)}, u32[]{:S(2)}, u32[]{:S(2)}) collective-permute-start(bf16[16,64,128]{2,1,0:T(8,128)(2,1)S(1)} %collective-permute-done.8.refs_1_), channel_id=1, source_target_pairs={{0,12},{4,0},{8,4},{12,8},{1,13},{5,1},{9,5},{13,9},{2,14},{6,2},{... | collective-permute-start | bytes 786440 | tf_op jit(solution)/shard_map/ppermute | solution.py:366
  55.8 8.8 %collective-permute-start.14 = (bf16[16,64,128]{2,1,0:T(8,128)(2,1)S(1)}, bf16[16,64,128]{2,1,0:T(8,128)(2,1)S(1)}, u32[]{:S(2)}, u32[]{:S(2)}) collective-permute-start(bf16[16,64,128]{2,1,0:T(8,128)(2,1)S(1)} %collective-permute-done.13.refs_6_), channel_id=1, source_target_pairs={{0,2},{2,0},{1,3},{3,1},{4,6},{6,4},{5,7},{7,5},{8,10},{10,8},{9,1... | collective-permute-start | bytes 786440 | tf_op jit(solution)/shard_map/ppermute | solution.py:366
  60.0 4.7 %collective-permute-start.15 = (bf16[16,64,128]{2,1,0:T(8,128)(2,1)S(1)}, bf16[16,64,128]{2,1,0:T(8,128)(2,1)S(1)}, u32[]{:S(2)}, u32[]{:S(2)}) collective-permute-start(bf16[16,64,128]{2,1,0:T(8,128)(2,1)S(1)} %share.1.refs_0_), channel_id=1, source_target_pairs={{0,1},{1,0},{2,3},{3,2},{4,5},{5,4},{6,7},{7,6},{8,9},{9,8},{10,11... | collective-permute-start | bytes 786440 | tf_op jit(solution)/shard_map/ppermute | solution.py:366
  60.0 5.2 %collective-permute-start.16 = (bf16[16,64,128]{2,1,0:T(8,128)(2,1)S(1)}, bf16[16,64,128]{2,1,0:T(8,128)(2,1)S(1)}, u32[]{:S(2)}, u32[]{:S(2)}) collective-permute-start(bf16[16,64,128]{2,1,0:T(8,128)(2,1)S(1)} %collective-permute-done.8.refs_1_), channel_id=1, source_target_pairs={{0,1},{1,0},{2,3},{3,2},{4,5},{5,4},{6,7},{7,6},{8,9},{9,8},{10,11... | collective-permute-start | bytes 786440 | tf_op jit(solution)/shard_map/ppermute | solution.py:366
  64.1 1.5 %collective-permute-start.17 = (bf16[16,64,128]{2,1,0:T(8,128)(2,1)S(1)}, bf16[16,64,128]{2,1,0:T(8,128)(2,1)S(1)}, u32[]{:S(2)}, u32[]{:S(2)}) collective-permute-start(bf16[16,64,128]{2,1,0:T(8,128)(2,1)S(1)} %collective-permute-done.9.refs_2_), channel_id=1, source_target_pairs={{0,1},{1,0},{2,3},{3,2},{4,5},{5,4},{6,7},{7,6},{8,9},{9,8},{10,11... | collective-permute-start | bytes 786440 | tf_op jit(solution)/shard_map/ppermute | solution.py:366
  64.1 1.9 %collective-permute-start.18 = (bf16[16,64,128]{2,1,0:T(8,128)(2,1)S(1)}, bf16[16,64,128]{2,1,0:T(8,128)(2,1)S(1)}, u32[]{:S(2)}, u32[]{:S(2)}) collective-permute-start(bf16[16,64,128]{2,1,0:T(8,128)(2,1)S(1)} %collective-permute-done.10.refs_3_), channel_id=1, source_target_pairs={{0,1},{1,0},{2,3},{3,2},{4,5},{5,4},{6,7},{7,6},{8,9},{9,8},{10,11... | collective-permute-start | bytes 786440 | tf_op jit(solution)/shard_map/ppermute | solution.py:366
  64.7 1.8 %collective-permute-start.21 = (bf16[16,64,128]{2,1,0:T(8,128)(2,1)S(1)}, bf16[16,64,128]{2,1,0:T(8,128)(2,1)S(1)}, u32[]{:S(2)}, u32[]{:S(2)}) collective-permute-start(bf16[16,64,128]{2,1,0:T(8,128)(2,1)S(1)} %collective-permute-done.13.refs_6_), channel_id=1, source_target_pairs={{0,1},{1,0},{2,3},{3,2},{4,5},{5,4},{6,7},{7,6},{8,9},{9,8},{10,11... | collective-permute-start | bytes 786440 | tf_op jit(solution)/shard_map/ppermute | solution.py:366
  64.7 2.1 %collective-permute-start.19 = (bf16[16,64,128]{2,1,0:T(8,128)(2,1)S(1)}, bf16[16,64,128]{2,1,0:T(8,128)(2,1)S(1)}, u32[]{:S(2)}, u32[]{:S(2)}) collective-permute-start(bf16[16,64,128]{2,1,0:T(8,128)(2,1)S(1)} %collective-permute-done.11.refs_4_), channel_id=1, source_target_pairs={{0,1},{1,0},{2,3},{3,2},{4,5},{5,4},{6,7},{7,6},{8,9},{9,8},{10,11... | collective-permute-start | bytes 786440 | tf_op jit(solution)/shard_map/ppermute | solution.py:366
  65.2 2.0 %collective-permute-start.20 = (bf16[16,64,128]{2,1,0:T(8,128)(2,1)S(1)}, bf16[16,64,128]{2,1,0:T(8,128)(2,1)S(1)}, u32[]{:S(2)}, u32[]{:S(2)}) collective-permute-start(bf16[16,64,128]{2,1,0:T(8,128)(2,1)S(1)} %collective-permute-done.12.refs_5_), channel_id=1, source_target_pairs={{0,1},{1,0},{2,3},{3,2},{4,5},{5,4},{6,7},{7,6},{8,9},{9,8},{10,11... | collective-permute-start | bytes 786440 | tf_op jit(solution)/shard_map/ppermute | solution.py:366
  65.7 1.9 %collective-permute-start.22 = (bf16[16,64,128]{2,1,0:T(8,128)(2,1)S(1)}, bf16[16,64,128]{2,1,0:T(8,128)(2,1)S(1)}, u32[]{:S(2)}, u32[]{:S(2)}) collective-permute-start(bf16[16,64,128]{2,1,0:T(8,128)(2,1)S(1)} %collective-permute-done.14.refs_7_), channel_id=1, source_target_pairs={{0,1},{1,0},{2,3},{3,2},{4,5},{5,4},{6,7},{7,6},{8,9},{9,8},{10,11... | collective-permute-start | bytes 786440 | tf_op jit(solution)/shard_map/ppermute | solution.py:366
  73.7 11.9 %collective-permute-start.27 = (s16[1040,128]{1,0:T(8,128)(2,1)S(1)}, s16[1040,128]{1,0:T(8,128)(2,1)S(1)}, u32[]{:S(2)}, u32[]{:S(2)}) collective-permute-start(s16[1040,128]{1,0:T(8,128)(2,1)S(1)} %get-tuple-element.53), channel_id=1, source_target_pairs={{0,16},{16,32},{32,48},{48,0},{1,17},{17,33},{33,49},{49,1},{2,18}... | collective-permute-start | bytes 798728 | tf_op jit(solution)/shard_map/ppermute | solution.py:366
  76.8 8.9 %collective-permute-start.28 = (s16[1040,128]{1,0:T(8,128)(2,1)S(1)}, s16[1040,128]{1,0:T(8,128)(2,1)S(1)}, u32[]{:S(2)}, u32[]{:S(2)}) collective-permute-start(s16[1040,128]{1,0:T(8,128)(2,1)S(1)} %get-tuple-element.54), channel_id=1, source_target_pairs={{0,48},{16,0},{32,16},{48,32},{1,49},{17,1},{33,17},{49,33},{2,50}... | collective-permute-start | bytes 798728 | tf_op jit(solution)/shard_map/ppermute | solution.py:366
  77.9 14.2 %collective-permute-start.25 = (s16[1040,128]{1,0:T(8,128)(2,1)S(1)}, s16[1040,128]{1,0:T(8,128)(2,1)S(1)}, u32[]{:S(2)}, u32[]{:S(2)}) collective-permute-start(s16[1040,128]{1,0:T(8,128)(2,1)S(1)} %get-tuple-element.51), channel_id=1, source_target_pairs={{0,64},{64,0},{1,65},{65,1},{2,66},{66,2},{3,67},{67,3},{4,68},{68... | collective-permute-start | bytes 798728 | tf_op jit(solution)/shard_map/ppermute | solution.py:366
  82.4 10.4 %collective-permute-start.23 = (s16[1040,128]{1,0:T(8,128)(2,1)S(1)}, s16[1040,128]{1,0:T(8,128)(2,1)S(1)}, u32[]{:S(2)}, u32[]{:S(2)}) collective-permute-start(s16[1040,128]{1,0:T(8,128)(2,1)S(1)} %get-tuple-element.48), channel_id=1, source_target_pairs={{0,16},{16,32},{32,48},{48,0},{1,17},{17,33},{33,49},{49,1},{2,18}... | collective-permute-start | bytes 798728 | tf_op jit(solution)/shard_map/ppermute | solution.py:366
  84.5 8.4 %collective-permute-start.24 = (s16[1040,128]{1,0:T(8,128)(2,1)S(1)}, s16[1040,128]{1,0:T(8,128)(2,1)S(1)}, u32[]{:S(2)}, u32[]{:S(2)}) collective-permute-start(s16[1040,128]{1,0:T(8,128)(2,1)S(1)} %get-tuple-element.49), channel_id=1, source_target_pairs={{0,48},{16,0},{32,16},{48,32},{1,49},{17,1},{33,17},{49,33},{2,50}... | collective-permute-start | bytes 798728 | tf_op jit(solution)/shard_map/ppermute | solution.py:366
  85.9 10.9 %collective-permute-start.29 = (s16[1040,128]{1,0:T(8,128)(2,1)S(1)}, s16[1040,128]{1,0:T(8,128)(2,1)S(1)}, u32[]{:S(2)}, u32[]{:S(2)}) collective-permute-start(s16[1040,128]{1,0:T(8,128)(2,1)S(1)} %merge.8), channel_id=1, source_target_pairs={{0,64},{64,0},{1,65},{65,1},{2,66},{66,2},{3,67},{67,3},{4,68},{68... | collective-permute-start | bytes 798728 | tf_op jit(solution)/shard_map/ppermute | solution.py:366
  92.3 8.2 %collective-permute-start.26 = (s16[1040,128]{1,0:T(8,128)(2,1)S(1)}, s16[1040,128]{1,0:T(8,128)(2,1)S(1)}, u32[]{:S(2)}, u32[]{:S(2)}) collective-permute-start(s16[1040,128]{1,0:T(8,128)(2,1)S(1)} %merge.7), channel_id=1, source_target_pairs={{0,32},{16,48},{32,0},{48,16},{1,33},{17,49},{33,1},{49,17},{2,34}... | collective-permute-start | bytes 798728 | tf_op jit(solution)/shard_map/ppermute | solution.py:366
  100.9 8.9 %collective-permute-start.30 = (s16[1040,128]{1,0:T(8,128)(2,1)S(1)}, s16[1040,128]{1,0:T(8,128)(2,1)S(1)}, u32[]{:S(2)}, u32[]{:S(2)}) collective-permute-start(s16[1040,128]{1,0:T(8,128)(2,1)S(1)} %merge.9.refs_0_), channel_id=1, source_target_pairs={{0,64},{64,0},{1,65},{65,1},{2,66},{66,2},{3,67},{67,3},{4,68},{68... | collective-permute-start | bytes 798728 | tf_op jit(solution)/shard_map/ppermute | solution.py:366
  103.7 10.9 %collective-permute-start.33 = (s16[1040,128]{1,0:T(8,128)(2,1)S(1)}, s16[1040,128]{1,0:T(8,128)(2,1)S(1)}, u32[]{:S(2)}, u32[]{:S(2)}) collective-permute-start(s16[1040,128]{1,0:T(8,128)(2,1)S(1)} %merge.9.refs_0_), channel_id=1, source_target_pairs={{0,32},{16,48},{32,0},{48,16},{1,33},{17,49},{33,1},{49,17},{2,34}... | collective-permute-start | bytes 798728 | tf_op jit(solution)/shard_map/ppermute | solution.py:366
  105.1 13.2 %collective-permute-start.35 = (s16[1040,128]{1,0:T(8,128)(2,1)S(1)}, s16[1040,128]{1,0:T(8,128)(2,1)S(1)}, u32[]{:S(2)}, u32[]{:S(2)}) collective-permute-start(s16[1040,128]{1,0:T(8,128)(2,1)S(1)} %merge.9.refs_0_), channel_id=1, source_target_pairs={{0,16},{16,32},{32,48},{48,0},{1,17},{17,33},{33,49},{49,1},{2,18}... | collective-permute-start | bytes 798728 | tf_op jit(solution)/shard_map/ppermute | solution.py:366
  106.0 13.0 %collective-permute-start.36 = (s16[1040,128]{1,0:T(8,128)(2,1)S(1)}, s16[1040,128]{1,0:T(8,128)(2,1)S(1)}, u32[]{:S(2)}, u32[]{:S(2)}) collective-permute-start(s16[1040,128]{1,0:T(8,128)(2,1)S(1)} %merge.9.refs_0_), channel_id=1, source_target_pairs={{0,48},{16,0},{32,16},{48,32},{1,49},{17,1},{33,17},{49,33},{2,50}... | collective-permute-start | bytes 798728 | tf_op jit(solution)/shard_map/ppermute | solution.py:366
  109.8 14.1 %collective-permute-start.31 = (s16[1040,128]{1,0:T(8,128)(2,1)S(1)}, s16[1040,128]{1,0:T(8,128)(2,1)S(1)}, u32[]{:S(2)}, u32[]{:S(2)}) collective-permute-start(s16[1040,128]{1,0:T(8,128)(2,1)S(1)} %collective-permute-done.30.refs_1_), channel_id=1, source_target_pairs={{0,16},{16,32},{32,48},{48,0},{1,17},{17,33},{33,49},{49,1},{2,18}... | collective-permute-start | bytes 798728 | tf_op jit(solution)/shard_map/ppermute | solution.py:366
  111.0 12.9 %collective-permute-start.32 = (s16[1040,128]{1,0:T(8,128)(2,1)S(1)}, s16[1040,128]{1,0:T(8,128)(2,1)S(1)}, u32[]{:S(2)}, u32[]{:S(2)}) collective-permute-start(s16[1040,128]{1,0:T(8,128)(2,1)S(1)} %collective-permute-done.30.refs_1_), channel_id=1, source_target_pairs={{0,48},{16,0},{32,16},{48,32},{1,49},{17,1},{33,17},{49,33},{2,50}... | collective-permute-start | bytes 798728 | tf_op jit(solution)/shard_map/ppermute | solution.py:366
  114.5 9.4 %collective-permute-start.34 = (s16[1040,128]{1,0:T(8,128)(2,1)S(1)}, s16[1040,128]{1,0:T(8,128)(2,1)S(1)}, u32[]{:S(2)}, u32[]{:S(2)}) collective-permute-start(s16[1040,128]{1,0:T(8,128)(2,1)S(1)} %collective-permute-done.33.refs_4_), channel_id=1, source_target_pairs={{0,64},{64,0},{1,65},{65,1},{2,66},{66,2},{3,67},{67,3},{4,68},{68... | collective-permute-start | bytes 798728 | tf_op jit(solution)/shard_map/ppermute | solution.py:366

commit v6 on v5

--- a/solution.py
+++ b/solution.py
@@ -12,7 +12,7 @@
 CHUNK = 64
 UNROLL = 64
 LAG = 8
-BLOCKS = 32
+BLOCKS = 64
 LEVEL = 32700.0
 STEPS = 8.0
 MIB = 1024 * 1024
@@ -415,8 +415,8 @@
     rest = pair(info, turn(info, keep, others), got, others, len(SENT) - FIRST)
     sent, kept = sent + rest[: len(SENT) - FIRST], rest[len(SENT) - FIRST :]
     mine = gather(scatter(sent, kept, *CHIPS, share), *CHIPS, True)
-    early = lax.optimization_barrier([mine[n] for n in EARLY])
-    given = [*early[:-1], mine[4], mine[5], early[-1], mine[7]]
+    own, across, up, far, far_across = lax.optimization_barrier([mine[n] for n in (0, 1, 3, 6, 7)])
+    given = [own, across, mine[2], up, mine[4], mine[5], far, far_across]
     theirs = [shift(value, "core", 1) for value in given]
     out = backward(blocks, coords, info, mine + theirs, blk_col)
     parts = gather(scatter(out[: len(SENT)], out[len(SENT) :], "z", "yh", merge), "z", "yh", False)

time: 126 us -> 126 us (level); the launches traced: 126 us -> 125 us
  transfers between devices with their start and end apart: 37 -> 37, of which waited for: 21 -> 20; matrix products, arithmetic and copies ran while one was open for 0% -> 0% of each run, Pallas kernels for 6% -> 6%
where the time goes in v6:
time: 126 us; the launch traced here: 125 us
  starting transfers between devices  57.6 us (46%)
  waiting for transfers between devices  34.5 us (27%)
  Pallas kernels  27.5 us (22%)
  local copies, waits for them, and re-layouts  4.04 us (3%)
    ppermute x37, starting transfers between devices, shift(): lax.ppermute(value, axis, [(i, (i + by) % count) for i in range(count)])  57.6 us
    ppermute x37, waiting for transfers between devices, shift(): lax.ppermute(value, axis, [(i, (i + by) % count) for i in range(count)])  34.5 us
    pallas_call x1, Pallas kernels, forward(): pl.pallas_call(forward_kernel, out_shape=(jax.ShapeDtypeStruct((half, TIL...  10.3 us
    pallas_call x1, Pallas kernels, backward(): pl.pallas_call(backward_kernel, out_shape=[coded] * len(SENT) + [plain] *...  6.16 us
    pallas_call x2, Pallas kernels, spread(): pl.pallas_call(functools.partial(spread_kernel, which), out_shape=jax.Sha...  3.88 us
    unnamed x8, local copies, waits for them, and re-layouts  3.39 us
    pallas_call x2, Pallas kernels, turn(): pl.pallas_call(functools.partial(turn_kernel, which), out_shape=jax.Shape...  3.33 us
  transfers between devices with their start and end apart: 37, of which 20 were waited for; matrix products, arithmetic and copies ran while one was open for 0% of the time, Pallas kernels for 6%

profile of v6, /device:TPU:0, one launch (start us, length us, event | category | flops | bytes accessed | tf_op | source)
XLA Modules:
  0.0 124.6 jit_solution(16986447933477099962)
XLA Ops:
  0.7 0.6 stack.71.info
  1.3 10.3 %forward.1 = (f32[128,128,64]{2,1,0:T(8,128)}, s16[8320,128]{1,0:T(8,128)(2,1)}) custom-call(s32[2,512]{1,0:T(2,128)} %bitcast.23, s32[18]{0:T(128)} %stack.71.info, bf16[64,16384]{1,0:T(8,128)(2,1)} %omega_ref.1, bf16[512,128,128]{2,1,0:T(8,128)(2,1)} %bitcast.25), custom_call_target="tpu_custom_call" | custom-call | tf_op jit(solution)/shard_map/forward/pallas_call | solution.py:128
  11.8 3.4 %copy-done = f32[128,128,64]{2,1,0:T(8,128)S(1)} copy-done((f32[128,128,64]{2,1,0:T(8,128)S(1)}, f32[128,128,64]{2,1,0:T(8,128)}, u32[]{:S(2)}) %copy-start) | copy-done | bytes 4194328
  15.1 1.4 %turn.3.keep_ref = f32[3,16,64,128]{3,2,1,0:T(8,128)S(1)} custom-call(s32[18]{0:T(128)S(1)} %copy-done.2, f32[128,128,64]{2,1,0:T(8,128)S(1)} %copy-done), custom_call_target="tpu_custom_call" | custom-call | tf_op jit(solution)/shard_map/turn/pallas_call | solution.py:161
  16.5 1.1 pair.3
  17.6 4.7 %collective-permute-start.5 = (s16[1040,128]{1,0:T(8,128)(2,1)S(1)}, s16[1040,128]{1,0:T(8,128)(2,1)S(1)}, u32[]{:S(2)}, u32[]{:S(2)}) collective-permute-start(s16[1040,128]{1,0:T(8,128)(2,1)S(1)} %get-tuple-element.38), channel_id=1, source_target_pairs={{0,4},{4,8},{8,12},{12,0},{1,5},{5,9},{9,13},{13,1},{2,6},{6,10},{... | collective-permute-start | bytes 798728 | tf_op jit(solution)/shard_map/ppermute | solution.py:366
  22.3 2.9 %collective-permute-start.3 = (s16[1040,128]{1,0:T(8,128)(2,1)S(1)}, s16[1040,128]{1,0:T(8,128)(2,1)S(1)}, u32[]{:S(2)}, u32[]{:S(2)}) collective-permute-start(s16[1040,128]{1,0:T(8,128)(2,1)S(1)} %get-tuple-element.36), channel_id=1, source_target_pairs={{0,2},{2,0},{1,3},{3,1},{4,6},{6,4},{5,7},{7,5},{8,10},{10,8},{9,1... | collective-permute-start | bytes 798728 | tf_op jit(solution)/shard_map/ppermute | solution.py:366
  25.2 1.9 %turn.2.keep_ref = f32[5,16,64,128]{3,2,1,0:T(8,128)S(1)} custom-call(s32[18]{0:T(128)S(1)} %copy-done.2, f32[128,128,64]{2,1,0:T(8,128)S(1)} %copy-done.1), custom_call_target="tpu_custom_call" | custom-call | tf_op jit(solution)/shard_map/turn/pallas_call | solution.py:161
  27.2 1.1 pair.2
  28.3 0.7 collective-permute-start.1
  29.0 2.6 %collective-permute-start.2 = (s16[1040,128]{1,0:T(8,128)(2,1)S(1)}, s16[1040,128]{1,0:T(8,128)(2,1)S(1)}, u32[]{:S(2)}, u32[]{:S(2)}) collective-permute-start(s16[1040,128]{1,0:T(8,128)(2,1)S(1)} %get-tuple-element.34), channel_id=1, source_target_pairs={{0,12},{4,0},{8,4},{12,8},{1,13},{5,1},{9,5},{13,9},{2,14},{6,2},{... | collective-permute-start | bytes 798728 | tf_op jit(solution)/shard_map/ppermute | solution.py:366
  31.6 0.3 merge.6
  31.9 1.5 %collective-permute-start.7 = (s16[1040,128]{1,0:T(8,128)(2,1)S(1)}, s16[1040,128]{1,0:T(8,128)(2,1)S(1)}, u32[]{:S(2)}, u32[]{:S(2)}) collective-permute-start(s16[1040,128]{1,0:T(8,128)(2,1)S(1)} %merge.6), channel_id=1, source_target_pairs={{0,2},{2,0},{1,3},{3,1},{4,6},{6,4},{5,7},{7,5},{8,10},{10,8},{9,1... | collective-permute-start | bytes 798728 | tf_op jit(solution)/shard_map/ppermute | solution.py:366
  33.4 0.2 merge.5
  33.6 2.8 %collective-permute-start.4 = (s16[1040,128]{1,0:T(8,128)(2,1)S(1)}, s16[1040,128]{1,0:T(8,128)(2,1)S(1)}, u32[]{:S(2)}, u32[]{:S(2)}) collective-permute-start(s16[1040,128]{1,0:T(8,128)(2,1)S(1)} %merge.5), channel_id=1, source_target_pairs={{0,8},{4,12},{8,0},{12,4},{1,9},{5,13},{9,1},{13,5},{2,10},{6,14},... | collective-permute-start | bytes 798728 | tf_op jit(solution)/shard_map/ppermute | solution.py:366
  36.5 7.1 %collective-permute-done.1.refs_0_ = s16[1040,128]{1,0:T(8,128)(2,1)S(1)} collective-permute-done((s16[1040,128]{1,0:T(8,128)(2,1)S(1)}, s16[1040,128]{1,0:T(8,128)(2,1)S(1)}, u32[]{:S(2)}, u32[]{:S(2)}) %collective-permute-start.1) | collective-permute-done | bytes 266272 | tf_op jit(solution)/shard_map/ppermute | solution.py:366
  43.6 0.3 share.1.refs_0_
  43.9 1.3 %collective-permute-start.8 = (bf16[16,64,128]{2,1,0:T(8,128)(2,1)S(1)}, bf16[16,64,128]{2,1,0:T(8,128)(2,1)S(1)}, u32[]{:S(2)}, u32[]{:S(2)}) collective-permute-start(bf16[16,64,128]{2,1,0:T(8,128)(2,1)S(1)} %share.1.refs_0_), channel_id=1, source_target_pairs={{0,2},{2,0},{1,3},{3,1},{4,6},{6,4},{5,7},{7,5},{8,10},{10,8},{9,1... | collective-permute-start | bytes 786440 | tf_op jit(solution)/shard_map/ppermute | solution.py:366
  45.2 0.8 collective-permute-start.13
  46.0 2.1 %collective-permute-start.9 = (bf16[16,64,128]{2,1,0:T(8,128)(2,1)S(1)}, bf16[16,64,128]{2,1,0:T(8,128)(2,1)S(1)}, u32[]{:S(2)}, u32[]{:S(2)}) collective-permute-start(bf16[16,64,128]{2,1,0:T(8,128)(2,1)S(1)} %share.1.refs_0_), channel_id=1, source_target_pairs={{0,4},{4,8},{8,12},{12,0},{1,5},{5,9},{9,13},{13,1},{2,6},{6,10},{... | collective-permute-start | bytes 786440 | tf_op jit(solution)/shard_map/ppermute | solution.py:366
  48.0 3.3 %collective-permute-done.8.refs_1_ = bf16[16,64,128]{2,1,0:T(8,128)(2,1)S(1)} collective-permute-done((bf16[16,64,128]{2,1,0:T(8,128)(2,1)S(1)}, bf16[16,64,128]{2,1,0:T(8,128)(2,1)S(1)}, u32[]{:S(2)}, u32[]{:S(2)}) %collective-permute-start.8) | collective-permute-done | bytes 262176 | tf_op jit(solution)/shard_map/ppermute | solution.py:366
  51.4 1.9 %collective-permute-start.10 = (bf16[16,64,128]{2,1,0:T(8,128)(2,1)S(1)}, bf16[16,64,128]{2,1,0:T(8,128)(2,1)S(1)}, u32[]{:S(2)}, u32[]{:S(2)}) collective-permute-start(bf16[16,64,128]{2,1,0:T(8,128)(2,1)S(1)} %share.1.refs_0_), channel_id=1, source_target_pairs={{0,12},{4,0},{8,4},{12,8},{1,13},{5,1},{9,5},{13,9},{2,14},{6,2},{... | collective-permute-start | bytes 786440 | tf_op jit(solution)/shard_map/ppermute | solution.py:366
  53.3 2.7 %collective-permute-done.13.refs_6_ = bf16[16,64,128]{2,1,0:T(8,128)(2,1)S(1)} collective-permute-done((bf16[16,64,128]{2,1,0:T(8,128)(2,1)S(1)}, bf16[16,64,128]{2,1,0:T(8,128)(2,1)S(1)}, u32[]{:S(2)}, u32[]{:S(2)}) %collective-permute-start.13) | collective-permute-done | bytes 262176 | tf_op jit(solution)/shard_map/ppermute | solution.py:366
  55.9 0.8 collective-permute-start.14
  56.7 0.3 collective-permute-start.11
  57.1 2.9 %collective-permute-start.12 = (bf16[16,64,128]{2,1,0:T(8,128)(2,1)S(1)}, bf16[16,64,128]{2,1,0:T(8,128)(2,1)S(1)}, u32[]{:S(2)}, u32[]{:S(2)}) collective-permute-start(bf16[16,64,128]{2,1,0:T(8,128)(2,1)S(1)} %collective-permute-done.8.refs_1_), channel_id=1, source_target_pairs={{0,12},{4,0},{8,4},{12,8},{1,13},{5,1},{9,5},{13,9},{2,14},{6,2},{... | collective-permute-start | bytes 786440 | tf_op jit(solution)/shard_map/ppermute | solution.py:366
  60.0 0.6 collective-permute-done.10.refs_3_
  60.6 1.7 %collective-permute-done.14.refs_7_ = bf16[16,64,128]{2,1,0:T(8,128)(2,1)S(1)} collective-permute-done((bf16[16,64,128]{2,1,0:T(8,128)(2,1)S(1)}, bf16[16,64,128]{2,1,0:T(8,128)(2,1)S(1)}, u32[]{:S(2)}, u32[]{:S(2)}) %collective-permute-start.14) | collective-permute-done | bytes 262176 | tf_op jit(solution)/shard_map/ppermute | solution.py:366
  62.3 0.5 collective-permute-start.16
  62.8 2.7 %collective-permute-done.11.refs_4_ = bf16[16,64,128]{2,1,0:T(8,128)(2,1)S(1)} collective-permute-done((bf16[16,64,128]{2,1,0:T(8,128)(2,1)S(1)}, bf16[16,64,128]{2,1,0:T(8,128)(2,1)S(1)}, u32[]{:S(2)}, u32[]{:S(2)}) %collective-permute-start.11) | collective-permute-done | bytes 262176 | tf_op jit(solution)/shard_map/ppermute | solution.py:366
  65.5 0.5 collective-permute-start.21
  66.1 0.4 collective-permute-start.19
  66.7 0.4 collective-permute-done.18.refs_11_
  67.1 0.4 collective-permute-done.21.refs_14_
  67.4 0.4 collective-permute-done.22.refs_15_
  67.8 0.4 collective-permute-done.19.refs_12_
  68.2 0.4 collective-permute-done.20.refs_13_
  68.6 6.2 %backward.1 = (s16[1040,128]{1,0:T(8,128)(2,1)S(1)}, s16[1040,128]{1,0:T(8,128)(2,1)S(1)}, s16[1040,128]{1,0:T(8,128)(2,1)S(1)}, s16[1040,128]{1,0:T(8,128)(2,1)...) custom-call(s32[2,512]{1,0:T(2,128)S(1)} %bitcast.24, ...), custom_call_target="tpu_custom_call" | custom-call | tf_op jit(solution)/shard_map/backward/pallas_call | solution.py:306
  74.7 0.6 collective-permute-start.27
  75.3 2.7 %collective-permute-start.28 = (s16[1040,128]{1,0:T(8,128)(2,1)S(1)}, s16[1040,128]{1,0:T(8,128)(2,1)S(1)}, u32[]{:S(2)}, u32[]{:S(2)}) collective-permute-start(s16[1040,128]{1,0:T(8,128)(2,1)S(1)} %get-tuple-element.54), channel_id=1, source_target_pairs={{0,48},{16,0},{32,16},{48,32},{1,49},{17,1},{33,17},{49,33},{2,50}... | collective-permute-start | bytes 798728 | tf_op jit(solution)/shard_map/ppermute | solution.py:366
  78.1 5.4 %collective-permute-start.25 = (s16[1040,128]{1,0:T(8,128)(2,1)S(1)}, s16[1040,128]{1,0:T(8,128)(2,1)S(1)}, u32[]{:S(2)}, u32[]{:S(2)}) collective-permute-start(s16[1040,128]{1,0:T(8,128)(2,1)S(1)} %get-tuple-element.51), channel_id=1, source_target_pairs={{0,64},{64,0},{1,65},{65,1},{2,66},{66,2},{3,67},{67,3},{4,68},{68... | collective-permute-start | bytes 798728 | tf_op jit(solution)/shard_map/ppermute | solution.py:366
  83.5 0.8 collective-permute-start.23
  84.3 2.4 %collective-permute-start.24 = (s16[1040,128]{1,0:T(8,128)(2,1)S(1)}, s16[1040,128]{1,0:T(8,128)(2,1)S(1)}, u32[]{:S(2)}, u32[]{:S(2)}) collective-permute-start(s16[1040,128]{1,0:T(8,128)(2,1)S(1)} %get-tuple-element.49), channel_id=1, source_target_pairs={{0,48},{16,0},{32,16},{48,32},{1,49},{17,1},{33,17},{49,33},{2,50}... | collective-permute-start | bytes 798728 | tf_op jit(solution)/shard_map/ppermute | solution.py:366
  86.8 0.3 merge.8
  87.1 3.9 %collective-permute-start.29 = (s16[1040,128]{1,0:T(8,128)(2,1)S(1)}, s16[1040,128]{1,0:T(8,128)(2,1)S(1)}, u32[]{:S(2)}, u32[]{:S(2)}) collective-permute-start(s16[1040,128]{1,0:T(8,128)(2,1)S(1)} %merge.8), channel_id=1, source_target_pairs={{0,64},{64,0},{1,65},{65,1},{2,66},{66,2},{3,67},{67,3},{4,68},{68... | collective-permute-start | bytes 798728 | tf_op jit(solution)/shard_map/ppermute | solution.py:366
  91.0 0.2 merge.7
  91.2 3.5 %collective-permute-start.26 = (s16[1040,128]{1,0:T(8,128)(2,1)S(1)}, s16[1040,128]{1,0:T(8,128)(2,1)S(1)}, u32[]{:S(2)}, u32[]{:S(2)}) collective-permute-start(s16[1040,128]{1,0:T(8,128)(2,1)S(1)} %merge.7), channel_id=1, source_target_pairs={{0,32},{16,48},{32,0},{48,16},{1,33},{17,49},{33,1},{49,17},{2,34}... | collective-permute-start | bytes 798728 | tf_op jit(solution)/shard_map/ppermute | solution.py:366
  94.8 2.7 %collective-permute-done.29.refs_3_ = s16[1040,128]{1,0:T(8,128)(2,1)S(1)} collective-permute-done((s16[1040,128]{1,0:T(8,128)(2,1)S(1)}, s16[1040,128]{1,0:T(8,128)(2,1)S(1)}, u32[]{:S(2)}, u32[]{:S(2)}) %collective-permute-start.29) | collective-permute-done | bytes 266272 | tf_op jit(solution)/shard_map/ppermute | solution.py:366
  97.4 2.4 %collective-permute-done.26.refs_2_ = s16[1040,128]{1,0:T(8,128)(2,1)S(1)} collective-permute-done((s16[1040,128]{1,0:T(8,128)(2,1)S(1)}, s16[1040,128]{1,0:T(8,128)(2,1)S(1)}, u32[]{:S(2)}, u32[]{:S(2)}) %collective-permute-start.26) | collective-permute-done | bytes 266272 | tf_op jit(solution)/shard_map/ppermute | solution.py:366
  99.9 0.4 merge.9.refs_0_
  100.3 2.9 %collective-permute-start.30 = (s16[1040,128]{1,0:T(8,128)(2,1)S(1)}, s16[1040,128]{1,0:T(8,128)(2,1)S(1)}, u32[]{:S(2)}, u32[]{:S(2)}) collective-permute-start(s16[1040,128]{1,0:T(8,128)(2,1)S(1)} %merge.9.refs_0_), channel_id=1, source_target_pairs={{0,64},{64,0},{1,65},{65,1},{2,66},{66,2},{3,67},{67,3},{4,68},{68... | collective-permute-start | bytes 798728 | tf_op jit(solution)/shard_map/ppermute | solution.py:366
  103.2 0.9 collective-permute-start.33
  104.1 1.8 %collective-permute-start.35 = (s16[1040,128]{1,0:T(8,128)(2,1)S(1)}, s16[1040,128]{1,0:T(8,128)(2,1)S(1)}, u32[]{:S(2)}, u32[]{:S(2)}) collective-permute-start(s16[1040,128]{1,0:T(8,128)(2,1)S(1)} %merge.9.refs_0_), channel_id=1, source_target_pairs={{0,16},{16,32},{32,48},{48,0},{1,17},{17,33},{33,49},{49,1},{2,18}... | collective-permute-start | bytes 798728 | tf_op jit(solution)/shard_map/ppermute | solution.py:366
  105.9 1.4 %collective-permute-start.36 = (s16[1040,128]{1,0:T(8,128)(2,1)S(1)}, s16[1040,128]{1,0:T(8,128)(2,1)S(1)}, u32[]{:S(2)}, u32[]{:S(2)}) collective-permute-start(s16[1040,128]{1,0:T(8,128)(2,1)S(1)} %merge.9.refs_0_), channel_id=1, source_target_pairs={{0,48},{16,0},{32,16},{48,32},{1,49},{17,1},{33,17},{49,33},{2,50}... | collective-permute-start | bytes 798728 | tf_op jit(solution)/shard_map/ppermute | solution.py:366
  107.3 1.0 collective-permute-done.30.refs_1_
  108.3 1.6 %collective-permute-start.31 = (s16[1040,128]{1,0:T(8,128)(2,1)S(1)}, s16[1040,128]{1,0:T(8,128)(2,1)S(1)}, u32[]{:S(2)}, u32[]{:S(2)}) collective-permute-start(s16[1040,128]{1,0:T(8,128)(2,1)S(1)} %collective-permute-done.30.refs_1_), channel_id=1, source_target_pairs={{0,16},{16,32},{32,48},{48,0},{1,17},{17,33},{33,49},{49,1},{2,18}... | collective-permute-start | bytes 798728 | tf_op jit(solution)/shard_map/ppermute | solution.py:366
  109.9 1.7 %collective-permute-start.32 = (s16[1040,128]{1,0:T(8,128)(2,1)S(1)}, s16[1040,128]{1,0:T(8,128)(2,1)S(1)}, u32[]{:S(2)}, u32[]{:S(2)}) collective-permute-start(s16[1040,128]{1,0:T(8,128)(2,1)S(1)} %collective-permute-done.30.refs_1_), channel_id=1, source_target_pairs={{0,48},{16,0},{32,16},{48,32},{1,49},{17,1},{33,17},{49,33},{2,50}... | collective-permute-start | bytes 798728 | tf_op jit(solution)/shard_map/ppermute | solution.py:366
  111.5 2.5 %collective-permute-done.33.refs_4_ = s16[1040,128]{1,0:T(8,128)(2,1)S(1)} collective-permute-done((s16[1040,128]{1,0:T(8,128)(2,1)S(1)}, s16[1040,128]{1,0:T(8,128)(2,1)S(1)}, u32[]{:S(2)}, u32[]{:S(2)}) %collective-permute-start.33) | collective-permute-done | bytes 266272 | tf_op jit(solution)/shard_map/ppermute | solution.py:366
  114.0 0.7 collective-permute-start.34
  114.7 2.4 %collective-permute-done.35.refs_2_ = s16[1040,128]{1,0:T(8,128)(2,1)S(1)} collective-permute-done((s16[1040,128]{1,0:T(8,128)(2,1)S(1)}, s16[1040,128]{1,0:T(8,128)(2,1)S(1)}, u32[]{:S(2)}, u32[]{:S(2)}) %collective-permute-start.35) | collective-permute-done | bytes 266272 | tf_op jit(solution)/shard_map/ppermute | solution.py:366
  117.1 1.8 %collective-permute-done.36.refs_3_ = s16[1040,128]{1,0:T(8,128)(2,1)S(1)} collective-permute-done((s16[1040,128]{1,0:T(8,128)(2,1)S(1)}, s16[1040,128]{1,0:T(8,128)(2,1)S(1)}, u32[]{:S(2)}, u32[]{:S(2)}) %collective-permute-start.36) | collective-permute-done | bytes 266272 | tf_op jit(solution)/shard_map/ppermute | solution.py:366
  118.9 2.1 %spread.2.refs_3_ = f32[64,16384]{1,0:T(8,128)} custom-call(s32[18]{0:T(128)S(1)} %copy-done.2, s16[1040,128]{1,0:T(8,128)(2,1)S(1)} %merge.9.refs_0_, s16[1040,128]{1,0:T(8,128)(2,1)S(1)} %collective-permute-done.30.refs_1_, s16[1040,128]{1,0:T(8,128)(2,1)S(1)} %collective-permute-done.35.refs_2_, s16[1040,128]{1,0:T(8,128)(2,1)S(1)} %collective-permute-done.36.refs_3_, ...), custom_call_target="tpu_custom_call" | custom-call | tf_op jit(solution)/shard_map/spread/pallas_call | solution.py:348
  121.1 1.6 %collective-permute-done.31.refs_0_ = s16[1040,128]{1,0:T(8,128)(2,1)S(1)} collective-permute-done((s16[1040,128]{1,0:T(8,128)(2,1)S(1)}, s16[1040,128]{1,0:T(8,128)(2,1)S(1)}, u32[]{:S(2)}, u32[]{:S(2)}) %collective-permute-start.31) | collective-permute-done | bytes 266272 | tf_op jit(solution)/shard_map/ppermute | solution.py:366
  122.6 1.8 %spread.3 = f32[64,16384]{1,0:T(8,128)} custom-call(s32[18]{0:T(128)S(1)} %copy-done.2, s16[1040,128]{1,0:T(8,128)(2,1)S(1)} %collective-permute-done.31.refs_0_, s16[1040,128]{1,0:T(8,128)(2,1)S(1)} %collective-permute-done.32.refs_1_, s16[1040,128]{1,0:T(8,128)(2,1)S(1)} %collective-permute-done.34.refs_2_, ...), custom_call_target="tpu_custom_call", output_to_operand_aliasing={{}: (4, {})} | custom-call | tf_op jit(solution)/shard_map/spread/pallas_call | solution.py:348
  (33 shorter events, 0.5 us)
Async XLA Ops:
  1.3 10.4 %copy-start.2 = (s32[18]{0:T(128)S(1)}, s32[18]{0:T(128)}, u32[]{:S(2)}) copy-start(s32[18]{0:T(128)} %stack.71.info) | copy-start | bytes 220
  11.6 4.9 %collective-permute-start = (s16[8320,128]{1,0:T(8,128)(2,1)}, s16[8320,128]{1,0:T(8,128)(2,1)S(1)}, u32[]{:S(2)}, u32[]{:S(2)}) collective-permute-start(s16[8320,128]{1,0:T(8,128)(2,1)} %get-tuple-element.31), channel_id=1, source_target_pairs={{0,1},{1,0},{2,3},{3,2},{4,5},{5,4},{6,7},{7,6},{8,9},{9,8},{10,11... | collective-permute-start | bytes 6389768 | tf_op jit(solution)/shard_map/ppermute | solution.py:366
  11.7 3.4 %copy-start = (f32[128,128,64]{2,1,0:T(8,128)S(1)}, f32[128,128,64]{2,1,0:T(8,128)}, u32[]{:S(2)}) copy-start(f32[128,128,64]{2,1,0:T(8,128)} %get-tuple-element.30.in_ref) | copy-start | bytes 12582916
  15.1 10.1 %copy-start.1 = (f32[128,128,64]{2,1,0:T(8,128)S(1)}, f32[128,128,64]{2,1,0:T(8,128)}, u32[]{:S(2)}) copy-start(f32[128,128,64]{2,1,0:T(8,128)} %get-tuple-element.30.in_ref) | copy-start | bytes 12582916
  17.6 14.0 %collective-permute-start.5 = (s16[1040,128]{1,0:T(8,128)(2,1)S(1)}, s16[1040,128]{1,0:T(8,128)(2,1)S(1)}, u32[]{:S(2)}, u32[]{:S(2)}) collective-permute-start(s16[1040,128]{1,0:T(8,128)(2,1)S(1)} %get-tuple-element.38), channel_id=1, source_target_pairs={{0,4},{4,8},{8,12},{12,0},{1,5},{5,9},{9,13},{13,1},{2,6},{6,10},{... | collective-permute-start | bytes 798728 | tf_op jit(solution)/shard_map/ppermute | solution.py:366
  22.3 9.4 %collective-permute-start.6 = (s16[1040,128]{1,0:T(8,128)(2,1)S(1)}, s16[1040,128]{1,0:T(8,128)(2,1)S(1)}, u32[]{:S(2)}, u32[]{:S(2)}) collective-permute-start(s16[1040,128]{1,0:T(8,128)(2,1)S(1)} %get-tuple-element.39), channel_id=1, source_target_pairs={{0,12},{4,0},{8,4},{12,8},{1,13},{5,1},{9,5},{13,9},{2,14},{6,2},{... | collective-permute-start | bytes 798728 | tf_op jit(solution)/shard_map/ppermute | solution.py:366
  22.3 11.1 %collective-permute-start.3 = (s16[1040,128]{1,0:T(8,128)(2,1)S(1)}, s16[1040,128]{1,0:T(8,128)(2,1)S(1)}, u32[]{:S(2)}, u32[]{:S(2)}) collective-permute-start(s16[1040,128]{1,0:T(8,128)(2,1)S(1)} %get-tuple-element.36), channel_id=1, source_target_pairs={{0,2},{2,0},{1,3},{3,1},{4,6},{6,4},{5,7},{7,5},{8,10},{10,8},{9,1... | collective-permute-start | bytes 798728 | tf_op jit(solution)/shard_map/ppermute | solution.py:366
  28.3 40.3 %copy-start.3 = (s32[1,1,512,2]{2,3,1,0:T(2,128)S(1)}, s32[1,1,512,2]{2,3,1,0:T(2,128)}, u32[]{:S(2)}) copy-start(s32[1,1,512,2]{2,3,1,0:T(2,128)} %param.5) | copy-start | bytes 12292
  28.3 15.2 %collective-permute-start.1 = (s16[1040,128]{1,0:T(8,128)(2,1)S(1)}, s16[1040,128]{1,0:T(8,128)(2,1)S(1)}, u32[]{:S(2)}, u32[]{:S(2)}) collective-permute-start(s16[1040,128]{1,0:T(8,128)(2,1)S(1)} %get-tuple-element.33), channel_id=1, source_target_pairs={{0,4},{4,8},{8,12},{12,0},{1,5},{5,9},{9,13},{13,1},{2,6},{6,10},{... | collective-permute-start | bytes 798728 | tf_op jit(solution)/shard_map/ppermute | solution.py:366
  29.0 14.5 %collective-permute-start.2 = (s16[1040,128]{1,0:T(8,128)(2,1)S(1)}, s16[1040,128]{1,0:T(8,128)(2,1)S(1)}, u32[]{:S(2)}, u32[]{:S(2)}) collective-permute-start(s16[1040,128]{1,0:T(8,128)(2,1)S(1)} %get-tuple-element.34), channel_id=1, source_target_pairs={{0,12},{4,0},{8,4},{12,8},{1,13},{5,1},{9,5},{13,9},{2,14},{6,2},{... | collective-permute-start | bytes 798728 | tf_op jit(solution)/shard_map/ppermute | solution.py:366
  31.9 11.6 %collective-permute-start.7 = (s16[1040,128]{1,0:T(8,128)(2,1)S(1)}, s16[1040,128]{1,0:T(8,128)(2,1)S(1)}, u32[]{:S(2)}, u32[]{:S(2)}) collective-permute-start(s16[1040,128]{1,0:T(8,128)(2,1)S(1)} %merge.6), channel_id=1, source_target_pairs={{0,2},{2,0},{1,3},{3,1},{4,6},{6,4},{5,7},{7,5},{8,10},{10,8},{9,1... | collective-permute-start | bytes 798728 | tf_op jit(solution)/shard_map/ppermute | solution.py:366
  33.6 9.9 %collective-permute-start.4 = (s16[1040,128]{1,0:T(8,128)(2,1)S(1)}, s16[1040,128]{1,0:T(8,128)(2,1)S(1)}, u32[]{:S(2)}, u32[]{:S(2)}) collective-permute-start(s16[1040,128]{1,0:T(8,128)(2,1)S(1)} %merge.5), channel_id=1, source_target_pairs={{0,8},{4,12},{8,0},{12,4},{1,9},{5,13},{9,1},{13,5},{2,10},{6,14},... | collective-permute-start | bytes 798728 | tf_op jit(solution)/shard_map/ppermute | solution.py:366
  43.9 7.5 %collective-permute-start.8 = (bf16[16,64,128]{2,1,0:T(8,128)(2,1)S(1)}, bf16[16,64,128]{2,1,0:T(8,128)(2,1)S(1)}, u32[]{:S(2)}, u32[]{:S(2)}) collective-permute-start(bf16[16,64,128]{2,1,0:T(8,128)(2,1)S(1)} %share.1.refs_0_), channel_id=1, source_target_pairs={{0,2},{2,0},{1,3},{3,1},{4,6},{6,4},{5,7},{7,5},{8,10},{10,8},{9,1... | collective-permute-start | bytes 786440 | tf_op jit(solution)/shard_map/ppermute | solution.py:366
  45.2 10.7 %collective-permute-start.13 = (bf16[16,64,128]{2,1,0:T(8,128)(2,1)S(1)}, bf16[16,64,128]{2,1,0:T(8,128)(2,1)S(1)}, u32[]{:S(2)}, u32[]{:S(2)}) collective-permute-start(bf16[16,64,128]{2,1,0:T(8,128)(2,1)S(1)} %share.1.refs_0_), channel_id=1, source_target_pairs={{0,8},{4,12},{8,0},{12,4},{1,9},{5,13},{9,1},{13,5},{2,10},{6,14},... | collective-permute-start | bytes 786440 | tf_op jit(solution)/shard_map/ppermute | solution.py:366
  46.0 14.1 %collective-permute-start.9 = (bf16[16,64,128]{2,1,0:T(8,128)(2,1)S(1)}, bf16[16,64,128]{2,1,0:T(8,128)(2,1)S(1)}, u32[]{:S(2)}, u32[]{:S(2)}) collective-permute-start(bf16[16,64,128]{2,1,0:T(8,128)(2,1)S(1)} %share.1.refs_0_), channel_id=1, source_target_pairs={{0,4},{4,8},{8,12},{12,0},{1,5},{5,9},{9,13},{13,1},{2,6},{6,10},{... | collective-permute-start | bytes 786440 | tf_op jit(solution)/shard_map/ppermute | solution.py:366
  51.4 9.2 %collective-permute-start.10 = (bf16[16,64,128]{2,1,0:T(8,128)(2,1)S(1)}, bf16[16,64,128]{2,1,0:T(8,128)(2,1)S(1)}, u32[]{:S(2)}, u32[]{:S(2)}) collective-permute-start(bf16[16,64,128]{2,1,0:T(8,128)(2,1)S(1)} %share.1.refs_0_), channel_id=1, source_target_pairs={{0,12},{4,0},{8,4},{12,8},{1,13},{5,1},{9,5},{13,9},{2,14},{6,2},{... | collective-permute-start | bytes 786440 | tf_op jit(solution)/shard_map/ppermute | solution.py:366
  55.9 6.4 %collective-permute-start.14 = (bf16[16,64,128]{2,1,0:T(8,128)(2,1)S(1)}, bf16[16,64,128]{2,1,0:T(8,128)(2,1)S(1)}, u32[]{:S(2)}, u32[]{:S(2)}) collective-permute-start(bf16[16,64,128]{2,1,0:T(8,128)(2,1)S(1)} %collective-permute-done.13.refs_6_), channel_id=1, source_target_pairs={{0,2},{2,0},{1,3},{3,1},{4,6},{6,4},{5,7},{7,5},{8,10},{10,8},{9,1... | collective-permute-start | bytes 786440 | tf_op jit(solution)/shard_map/ppermute | solution.py:366
  56.7 8.8 %collective-permute-start.11 = (bf16[16,64,128]{2,1,0:T(8,128)(2,1)S(1)}, bf16[16,64,128]{2,1,0:T(8,128)(2,1)S(1)}, u32[]{:S(2)}, u32[]{:S(2)}) collective-permute-start(bf16[16,64,128]{2,1,0:T(8,128)(2,1)S(1)} %collective-permute-done.8.refs_1_), channel_id=1, source_target_pairs={{0,4},{4,8},{8,12},{12,0},{1,5},{5,9},{9,13},{13,1},{2,6},{6,10},{... | collective-permute-start | bytes 786440 | tf_op jit(solution)/shard_map/ppermute | solution.py:366
  57.1 8.5 %collective-permute-start.12 = (bf16[16,64,128]{2,1,0:T(8,128)(2,1)S(1)}, bf16[16,64,128]{2,1,0:T(8,128)(2,1)S(1)}, u32[]{:S(2)}, u32[]{:S(2)}) collective-permute-start(bf16[16,64,128]{2,1,0:T(8,128)(2,1)S(1)} %collective-permute-done.8.refs_1_), channel_id=1, source_target_pairs={{0,12},{4,0},{8,4},{12,8},{1,13},{5,1},{9,5},{13,9},{2,14},{6,2},{... | collective-permute-start | bytes 786440 | tf_op jit(solution)/shard_map/ppermute | solution.py:366
  60.0 6.0 %collective-permute-start.17 = (bf16[16,64,128]{2,1,0:T(8,128)(2,1)S(1)}, bf16[16,64,128]{2,1,0:T(8,128)(2,1)S(1)}, u32[]{:S(2)}, u32[]{:S(2)}) collective-permute-start(bf16[16,64,128]{2,1,0:T(8,128)(2,1)S(1)} %collective-permute-done.9.refs_2_), channel_id=1, source_target_pairs={{0,1},{1,0},{2,3},{3,2},{4,5},{5,4},{6,7},{7,6},{8,9},{9,8},{10,11... | collective-permute-start | bytes 786440 | tf_op jit(solution)/shard_map/ppermute | solution.py:366
  62.3 3.8 %collective-permute-start.15 = (bf16[16,64,128]{2,1,0:T(8,128)(2,1)S(1)}, bf16[16,64,128]{2,1,0:T(8,128)(2,1)S(1)}, u32[]{:S(2)}, u32[]{:S(2)}) collective-permute-start(bf16[16,64,128]{2,1,0:T(8,128)(2,1)S(1)} %share.1.refs_0_), channel_id=1, source_target_pairs={{0,1},{1,0},{2,3},{3,2},{4,5},{5,4},{6,7},{7,6},{8,9},{9,8},{10,11... | collective-permute-start | bytes 786440 | tf_op jit(solution)/shard_map/ppermute | solution.py:366
  62.3 4.3 %collective-permute-start.16 = (bf16[16,64,128]{2,1,0:T(8,128)(2,1)S(1)}, bf16[16,64,128]{2,1,0:T(8,128)(2,1)S(1)}, u32[]{:S(2)}, u32[]{:S(2)}) collective-permute-start(bf16[16,64,128]{2,1,0:T(8,128)(2,1)S(1)} %collective-permute-done.8.refs_1_), channel_id=1, source_target_pairs={{0,1},{1,0},{2,3},{3,2},{4,5},{5,4},{6,7},{7,6},{8,9},{9,8},{10,11... | collective-permute-start | bytes 786440 | tf_op jit(solution)/shard_map/ppermute | solution.py:366
  65.5 1.5 %collective-permute-start.18 = (bf16[16,64,128]{2,1,0:T(8,128)(2,1)S(1)}, bf16[16,64,128]{2,1,0:T(8,128)(2,1)S(1)}, u32[]{:S(2)}, u32[]{:S(2)}) collective-permute-start(bf16[16,64,128]{2,1,0:T(8,128)(2,1)S(1)} %collective-permute-done.10.refs_3_), channel_id=1, source_target_pairs={{0,1},{1,0},{2,3},{3,2},{4,5},{5,4},{6,7},{7,6},{8,9},{9,8},{10,11... | collective-permute-start | bytes 786440 | tf_op jit(solution)/shard_map/ppermute | solution.py:366
  65.5 1.9 %collective-permute-start.21 = (bf16[16,64,128]{2,1,0:T(8,128)(2,1)S(1)}, bf16[16,64,128]{2,1,0:T(8,128)(2,1)S(1)}, u32[]{:S(2)}, u32[]{:S(2)}) collective-permute-start(bf16[16,64,128]{2,1,0:T(8,128)(2,1)S(1)} %collective-permute-done.13.refs_6_), channel_id=1, source_target_pairs={{0,1},{1,0},{2,3},{3,2},{4,5},{5,4},{6,7},{7,6},{8,9},{9,8},{10,11... | collective-permute-start | bytes 786440 | tf_op jit(solution)/shard_map/ppermute | solution.py:366
  66.1 1.8 %collective-permute-start.22 = (bf16[16,64,128]{2,1,0:T(8,128)(2,1)S(1)}, bf16[16,64,128]{2,1,0:T(8,128)(2,1)S(1)}, u32[]{:S(2)}, u32[]{:S(2)}) collective-permute-start(bf16[16,64,128]{2,1,0:T(8,128)(2,1)S(1)} %collective-permute-done.14.refs_7_), channel_id=1, source_target_pairs={{0,1},{1,0},{2,3},{3,2},{4,5},{5,4},{6,7},{7,6},{8,9},{9,8},{10,11... | collective-permute-start | bytes 786440 | tf_op jit(solution)/shard_map/ppermute | solution.py:366
  66.1 2.1 %collective-permute-start.19 = (bf16[16,64,128]{2,1,0:T(8,128)(2,1)S(1)}, bf16[16,64,128]{2,1,0:T(8,128)(2,1)S(1)}, u32[]{:S(2)}, u32[]{:S(2)}) collective-permute-start(bf16[16,64,128]{2,1,0:T(8,128)(2,1)S(1)} %collective-permute-done.11.refs_4_), channel_id=1, source_target_pairs={{0,1},{1,0},{2,3},{3,2},{4,5},{5,4},{6,7},{7,6},{8,9},{9,8},{10,11... | collective-permute-start | bytes 786440 | tf_op jit(solution)/shard_map/ppermute | solution.py:366
  66.6 2.0 %collective-permute-start.20 = (bf16[16,64,128]{2,1,0:T(8,128)(2,1)S(1)}, bf16[16,64,128]{2,1,0:T(8,128)(2,1)S(1)}, u32[]{:S(2)}, u32[]{:S(2)}) collective-permute-start(bf16[16,64,128]{2,1,0:T(8,128)(2,1)S(1)} %collective-permute-done.12.refs_5_), channel_id=1, source_target_pairs={{0,1},{1,0},{2,3},{3,2},{4,5},{5,4},{6,7},{7,6},{8,9},{9,8},{10,11... | collective-permute-start | bytes 786440 | tf_op jit(solution)/shard_map/ppermute | solution.py:366
  74.7 12.0 %collective-permute-start.27 = (s16[1040,128]{1,0:T(8,128)(2,1)S(1)}, s16[1040,128]{1,0:T(8,128)(2,1)S(1)}, u32[]{:S(2)}, u32[]{:S(2)}) collective-permute-start(s16[1040,128]{1,0:T(8,128)(2,1)S(1)} %get-tuple-element.53), channel_id=1, source_target_pairs={{0,16},{16,32},{32,48},{48,0},{1,17},{17,33},{33,49},{49,1},{2,18}... | collective-permute-start | bytes 798728 | tf_op jit(solution)/shard_map/ppermute | solution.py:366
  75.3 11.5 %collective-permute-start.28 = (s16[1040,128]{1,0:T(8,128)(2,1)S(1)}, s16[1040,128]{1,0:T(8,128)(2,1)S(1)}, u32[]{:S(2)}, u32[]{:S(2)}) collective-permute-start(s16[1040,128]{1,0:T(8,128)(2,1)S(1)} %get-tuple-element.54), channel_id=1, source_target_pairs={{0,48},{16,0},{32,16},{48,32},{1,49},{17,1},{33,17},{49,33},{2,50}... | collective-permute-start | bytes 798728 | tf_op jit(solution)/shard_map/ppermute | solution.py:366
  78.1 13.0 %collective-permute-start.25 = (s16[1040,128]{1,0:T(8,128)(2,1)S(1)}, s16[1040,128]{1,0:T(8,128)(2,1)S(1)}, u32[]{:S(2)}, u32[]{:S(2)}) collective-permute-start(s16[1040,128]{1,0:T(8,128)(2,1)S(1)} %get-tuple-element.51), channel_id=1, source_target_pairs={{0,64},{64,0},{1,65},{65,1},{2,66},{66,2},{3,67},{67,3},{4,68},{68... | collective-permute-start | bytes 798728 | tf_op jit(solution)/shard_map/ppermute | solution.py:366
  83.5 11.3 %collective-permute-start.23 = (s16[1040,128]{1,0:T(8,128)(2,1)S(1)}, s16[1040,128]{1,0:T(8,128)(2,1)S(1)}, u32[]{:S(2)}, u32[]{:S(2)}) collective-permute-start(s16[1040,128]{1,0:T(8,128)(2,1)S(1)} %get-tuple-element.48), channel_id=1, source_target_pairs={{0,16},{16,32},{32,48},{48,0},{1,17},{17,33},{33,49},{49,1},{2,18}... | collective-permute-start | bytes 798728 | tf_op jit(solution)/shard_map/ppermute | solution.py:366
  84.3 10.5 %collective-permute-start.24 = (s16[1040,128]{1,0:T(8,128)(2,1)S(1)}, s16[1040,128]{1,0:T(8,128)(2,1)S(1)}, u32[]{:S(2)}, u32[]{:S(2)}) collective-permute-start(s16[1040,128]{1,0:T(8,128)(2,1)S(1)} %get-tuple-element.49), channel_id=1, source_target_pairs={{0,48},{16,0},{32,16},{48,32},{1,49},{17,1},{33,17},{49,33},{2,50}... | collective-permute-start | bytes 798728 | tf_op jit(solution)/shard_map/ppermute | solution.py:366
  87.1 10.4 %collective-permute-start.29 = (s16[1040,128]{1,0:T(8,128)(2,1)S(1)}, s16[1040,128]{1,0:T(8,128)(2,1)S(1)}, u32[]{:S(2)}, u32[]{:S(2)}) collective-permute-start(s16[1040,128]{1,0:T(8,128)(2,1)S(1)} %merge.8), channel_id=1, source_target_pairs={{0,64},{64,0},{1,65},{65,1},{2,66},{66,2},{3,67},{67,3},{4,68},{68... | collective-permute-start | bytes 798728 | tf_op jit(solution)/shard_map/ppermute | solution.py:366
  91.2 8.7 %collective-permute-start.26 = (s16[1040,128]{1,0:T(8,128)(2,1)S(1)}, s16[1040,128]{1,0:T(8,128)(2,1)S(1)}, u32[]{:S(2)}, u32[]{:S(2)}) collective-permute-start(s16[1040,128]{1,0:T(8,128)(2,1)S(1)} %merge.7), channel_id=1, source_target_pairs={{0,32},{16,48},{32,0},{48,16},{1,33},{17,49},{33,1},{49,17},{2,34}... | collective-permute-start | bytes 798728 | tf_op jit(solution)/shard_map/ppermute | solution.py:366
  100.3 8.0 %collective-permute-start.30 = (s16[1040,128]{1,0:T(8,128)(2,1)S(1)}, s16[1040,128]{1,0:T(8,128)(2,1)S(1)}, u32[]{:S(2)}, u32[]{:S(2)}) collective-permute-start(s16[1040,128]{1,0:T(8,128)(2,1)S(1)} %merge.9.refs_0_), channel_id=1, source_target_pairs={{0,64},{64,0},{1,65},{65,1},{2,66},{66,2},{3,67},{67,3},{4,68},{68... | collective-permute-start | bytes 798728 | tf_op jit(solution)/shard_map/ppermute | solution.py:366
  103.2 10.8 %collective-permute-start.33 = (s16[1040,128]{1,0:T(8,128)(2,1)S(1)}, s16[1040,128]{1,0:T(8,128)(2,1)S(1)}, u32[]{:S(2)}, u32[]{:S(2)}) collective-permute-start(s16[1040,128]{1,0:T(8,128)(2,1)S(1)} %merge.9.refs_0_), channel_id=1, source_target_pairs={{0,32},{16,48},{32,0},{48,16},{1,33},{17,49},{33,1},{49,17},{2,34}... | collective-permute-start | bytes 798728 | tf_op jit(solution)/shard_map/ppermute | solution.py:366
  104.1 13.1 %collective-permute-start.35 = (s16[1040,128]{1,0:T(8,128)(2,1)S(1)}, s16[1040,128]{1,0:T(8,128)(2,1)S(1)}, u32[]{:S(2)}, u32[]{:S(2)}) collective-permute-start(s16[1040,128]{1,0:T(8,128)(2,1)S(1)} %merge.9.refs_0_), channel_id=1, source_target_pairs={{0,16},{16,32},{32,48},{48,0},{1,17},{17,33},{33,49},{49,1},{2,18}... | collective-permute-start | bytes 798728 | tf_op jit(solution)/shard_map/ppermute | solution.py:366
  105.9 13.1 %collective-permute-start.36 = (s16[1040,128]{1,0:T(8,128)(2,1)S(1)}, s16[1040,128]{1,0:T(8,128)(2,1)S(1)}, u32[]{:S(2)}, u32[]{:S(2)}) collective-permute-start(s16[1040,128]{1,0:T(8,128)(2,1)S(1)} %merge.9.refs_0_), channel_id=1, source_target_pairs={{0,48},{16,0},{32,16},{48,32},{1,49},{17,1},{33,17},{49,33},{2,50}... | collective-permute-start | bytes 798728 | tf_op jit(solution)/shard_map/ppermute | solution.py:366
  108.3 14.4 %collective-permute-start.31 = (s16[1040,128]{1,0:T(8,128)(2,1)S(1)}, s16[1040,128]{1,0:T(8,128)(2,1)S(1)}, u32[]{:S(2)}, u32[]{:S(2)}) collective-permute-start(s16[1040,128]{1,0:T(8,128)(2,1)S(1)} %collective-permute-done.30.refs_1_), channel_id=1, source_target_pairs={{0,16},{16,32},{32,48},{48,0},{1,17},{17,33},{33,49},{49,1},{2,18}... | collective-permute-start | bytes 798728 | tf_op jit(solution)/shard_map/ppermute | solution.py:366
  109.9 12.8 %collective-permute-start.32 = (s16[1040,128]{1,0:T(8,128)(2,1)S(1)}, s16[1040,128]{1,0:T(8,128)(2,1)S(1)}, u32[]{:S(2)}, u32[]{:S(2)}) collective-permute-start(s16[1040,128]{1,0:T(8,128)(2,1)S(1)} %collective-permute-done.30.refs_1_), channel_id=1, source_target_pairs={{0,48},{16,0},{32,16},{48,32},{1,49},{17,1},{33,17},{49,33},{2,50}... | collective-permute-start | bytes 798728 | tf_op jit(solution)/shard_map/ppermute | solution.py:366
  114.0 8.6 %collective-permute-start.34 = (s16[1040,128]{1,0:T(8,128)(2,1)S(1)}, s16[1040,128]{1,0:T(8,128)(2,1)S(1)}, u32[]{:S(2)}, u32[]{:S(2)}) collective-permute-start(s16[1040,128]{1,0:T(8,128)(2,1)S(1)} %collective-permute-done.33.refs_4_), channel_id=1, source_target_pairs={{0,64},{64,0},{1,65},{65,1},{2,66},{66,2},{3,67},{67,3},{4,68},{68... | collective-permute-start | bytes 798728 | tf_op jit(solution)/shard_map/ppermute | solution.py:366
